TPU v7x, 256 devices: a whole 4x4x8 slice. The times are simulated.
256 devices in a mesh: ta: 4 (over x), ha: 8 (over y, core), wa: 8 (over z).
Axes of the slice: x: 4, y: 4, z: 8, core: 2. Of those that a mesh axis runs over, the one named last changes fastest.
Arguments:
- latent: bfloat16 [4, 64, 64, 512], P('ta', 'ha', 'wa'), may hold values from -20 to 20, as said below
- norm1_gain: float32 [512], replicated, may hold values from 0.1 to 1.9
- norm1_shift: float32 [512], replicated, may hold values from -3 to 3
- conv1_kernel: bfloat16 [27, 512, 512], P(None, None, 'ta'), may hold values from -0.0546875 to 0.0546875
- conv1_shift: float32 [512], P('ta'), may hold values from -3 to 3
- norm2_gain: float32 [512], replicated, may hold values from 0.1 to 1.9
- norm2_shift: float32 [512], replicated, may hold values from -3 to 3
- conv2_kernel: bfloat16 [27, 512, 512], P(None, None, 'ta'), may hold values from -0.0546875 to 0.0546875
- conv2_shift: float32 [512], P('ta'), may hold values from -3 to 3
- norm3_gain: float32 [512], replicated, may hold values from 0.1 to 1.9
- norm3_shift: float32 [512], replicated, may hold values from -3 to 3
- query_weight: bfloat16 [512, 512], replicated, may hold values from -0.32 to 0.32, as said below
- query_shift: float32 [512], replicated, may hold values from -3 to 3
- key_weight: bfloat16 [512, 512], replicated, may hold values from -0.32 to 0.32, as said below
- value_weight: bfloat16 [512, 512], replicated, may hold values from -0.25 to 0.25
- value_shift: float32 [512], replicated, may hold values from -3 to 3
- output_weight: bfloat16 [512, 512], replicated, may hold values from -0.25 to 0.25
- output_shift: float32 [512], replicated, may hold values from -3 to 3
Outputs:
- block_out: bfloat16 [4, 64, 64, 512], P('ta', 'ha', 'wa')
Inputs may be any that keep to these rules, and one draw needn't show every extreme that they name: `latent`: features of order one. `query_weight`: entries of order 512 ** -0.5. `key_weight`: entries of order 512 ** -0.5.
All inputs are finite; a program needn't handle non-finite values.
Results may differ from a plain program's by a relative error of at most 0.017.
Values may be sent and summed in bfloat16 or wider, within the bound.
No kernel may reach another device: no remote copies, remote signals or barrier semaphores. Data moves between devices by JAX's collectives and lax.ppermute only.
A program may use at most 64 MiB of HBM per device.

v0:
```python
import jax
import jax.numpy as jnp
from jax import lax
from jax.sharding import PartitionSpec as P

GROUPS = 32


EPS = 1e-06


def with_halo(block, sides, width):
    for axis, dim in sides:
        count = lax.axis_size(axis)
        forward = [(i, i + 1) for i in range(count - 1)]
        backward = [(target, source) for source, target in forward]
        low = lax.ppermute(
            lax.slice_in_dim(block, block.shape[dim] - width, None, axis=dim), axis, forward
        )
        high = lax.ppermute(lax.slice_in_dim(block, 0, width, axis=dim), axis, backward)
        block = jnp.concatenate([low, block, high], axis=dim)
    return block


def group_norm(values, gain, shift):
    channels = values.shape[-1]
    members = channels // GROUPS
    devices = lax.axis_size("ta") * lax.axis_size("ha") * lax.axis_size("wa")
    count = values.shape[0] * values.shape[1] * values.shape[2] * members * devices
    grouped = values.reshape(-1, GROUPS, members)
    center = lax.psum(jnp.sum(grouped, axis=(0, 2)), ("ta", "ha", "wa")) / count
    deviation = grouped - center[None, :, None]
    spread = lax.psum(jnp.sum(deviation * deviation, axis=(0, 2)), ("ta", "ha", "wa")) / count
    normed = ((grouped - center[None, :, None]) * lax.rsqrt(spread + EPS)[None, :, None]).reshape(
        values.shape
    )
    return normed * gain + shift


def causal_conv(inputs, kernel, shift):
    frames_here, height, width, channels = inputs.shape
    rimmed = with_halo(inputs, (("ha", 1), ("wa", 2)), 1)
    gathered = lax.all_gather(rimmed, "ta", axis=0, tiled=True)
    gathered = jnp.concatenate([gathered[:1], gathered[:1], gathered], axis=0)
    frame_count = gathered.shape[0] - 2
    total = jnp.zeros((frame_count * height * width, kernel.shape[2]), jnp.float32)
    for tap in range(27):
        depth, row, column = (tap // 9, tap // 3 % 3, tap % 3)
        window = lax.slice(
            gathered,
            (depth, row, column, 0),
            (depth + frame_count, row + height, column + width, channels),
        )
        total = total + jnp.dot(
            window.reshape(-1, channels), kernel[tap], preferred_element_type=jnp.float32
        )
    result = (
        (total + shift).astype(jnp.bfloat16).reshape(frame_count, height, width, kernel.shape[2])
    )
    return lax.all_to_all(result, "ta", split_axis=0, concat_axis=3, tiled=True)


def body(
    latent,
    norm1_gain,
    norm1_shift,
    conv1_kernel,
    conv1_shift,
    norm2_gain,
    norm2_shift,
    conv2_kernel,
    conv2_shift,
    norm3_gain,
    norm3_shift,
    query_weight,
    query_shift,
    key_weight,
    value_weight,
    value_shift,
    output_weight,
    output_shift,
):
    channels = latent.shape[-1]
    frames_here = latent.shape[0]
    first_act = jax.nn.silu(group_norm(latent.astype(jnp.float32), norm1_gain, norm1_shift)).astype(
        jnp.bfloat16
    )
    hidden = causal_conv(first_act, conv1_kernel, conv1_shift)
    second_act = jax.nn.silu(
        group_norm(hidden.astype(jnp.float32), norm2_gain, norm2_shift)
    ).astype(jnp.bfloat16)
    branch = causal_conv(second_act, conv2_kernel, conv2_shift)
    residual = (latent.astype(jnp.float32) + branch.astype(jnp.float32)).astype(jnp.bfloat16)
    normed = group_norm(residual.astype(jnp.float32), norm3_gain, norm3_shift).astype(jnp.bfloat16)
    flat = normed.reshape(-1, channels)
    frame_shape = (frames_here, -1, channels)
    queries = (
        (jnp.dot(flat, query_weight, preferred_element_type=jnp.float32) + query_shift)
        .astype(jnp.bfloat16)
        .reshape(frame_shape)
    )
    scale = channels ** (-0.5)
    cells = queries.shape[1]
    keys = (
        jnp.dot(flat, key_weight, preferred_element_type=jnp.float32)
        .astype(jnp.bfloat16)
        .reshape(frame_shape)
    )
    values = (
        (jnp.dot(flat, value_weight, preferred_element_type=jnp.float32) + value_shift)
        .astype(jnp.bfloat16)
        .reshape(frame_shape)
    )
    absorb_keys = lax.all_gather(keys, ("ha", "wa"), axis=1, tiled=True)
    absorb_values = lax.all_gather(values, ("ha", "wa"), axis=1, tiled=True)
    highest = jnp.full((frames_here, cells), -jnp.inf, jnp.float32)
    total = jnp.zeros((frames_here, cells), jnp.float32)
    mixed = jnp.zeros((frames_here, cells, channels), jnp.float32)
    scores = (
        jnp.einsum("tqc,tkc->tqk", queries, absorb_keys, preferred_element_type=jnp.float32) * scale
    )
    new_high = jnp.max(scores, axis=-1)
    fade = jnp.exp(highest - new_high)
    weights = jnp.exp(scores - new_high[..., None])
    total = total * fade + jnp.sum(weights, axis=-1)
    mixed = mixed * fade[..., None] + jnp.einsum(
        "tqk,tkc->tqc",
        weights.astype(jnp.bfloat16),
        absorb_values,
        preferred_element_type=jnp.float32,
    )
    attended = (mixed / total[..., None]).astype(jnp.bfloat16).reshape(-1, channels)
    block_out = (
        residual.astype(jnp.float32).reshape(-1, channels)
        + jnp.dot(attended, output_weight, preferred_element_type=jnp.float32)
        + output_shift
    )
    return block_out.astype(jnp.bfloat16).reshape(latent.shape)


def solution(mesh):
    in_specs = (
        P("ta", "ha", "wa", None),
        P(),
        P(),
        P(None, None, "ta"),
        P("ta"),
        P(),
        P(),
        P(None, None, "ta"),
        P("ta"),
        P(),
        P(),
        P(),
        P(),
        P(),
        P(),
        P(),
        P(),
        P(),
    )
    out_specs = P("ta", "ha", "wa", None)
    return jax.shard_map(body, mesh=mesh, in_specs=in_specs, out_specs=out_specs, check_vma=False)
```

profile of v0, /device:TPU:6, one launch (start us, length us, event | category | flops | bytes accessed | tf_op | source)
XLA Modules:
  0.0 717.0 jit_solution(13417554767649410080)
XLA Ops:
  7.7 78.7 %psum.42 = f32[32]{0:T(128)S(1)} all-reduce(f32[32]{0:T(128)S(1)} %reduce_sum.82), channel_id=1, replica_groups=mesh['ta'=4,'ha'=8,'wa'=8] {'ta','ha','wa'}, use_global_device_ids=true, to_apply=%region_2.0 | all-reduce | flops 32 | bytes 256 | tf_op jit(solution)/shard_map/psum | solution.py:31
  87.6 73.4 %psum.43 = f32[32]{0:T(128)S(1)} all-reduce(f32[32]{0:T(128)S(1)} %reduce_sum.85), channel_id=1, replica_groups=mesh['ta'=4,'ha'=8,'wa'=8] {'ta','ha','wa'}, use_global_device_ids=true, to_apply=%region_5.6 | all-reduce | flops 32 | bytes 256 | tf_op jit(solution)/shard_map/psum | solution.py:33
  162.1 1.7 collective-permute-start
  163.9 1.3 collective-permute-start.1
  165.2 1.8 collective-permute-done.1
  167.0 4.0 collective-permute-start.2
  172.4 4.2 collective-permute-done.3
  176.7 13.9 %all_gather.12 = bf16[4,10,10,512]{3,2,1,0:T(8,128)(2,1)S(1)} all-gather(bf16[1,10,10,512]{3,2,1,0:T(8,128)(2,1)S(1)} %pad_maximum_fusion.4), channel_id=1, replica_groups=mesh['ta'=4,'ha'=8,'wa'=8] {'ta'}, dimensions={0}, use_global_device_ids=true | all-gather | bytes 512000 | tf_op jit(solution)/shard_map/all_gather | solution.py:43
  198.9 7.9 %all_to_all.8 = bf16[4,8,8,128]{3,2,1,0:T(8,128)(2,1)S(1)} all-to-all(bf16[4,8,8,128]{3,2,1,0:T(8,128)(2,1)S(1)} %bitcast.379), channel_id=1, replica_groups=mesh['ta'=4,'ha'=8,'wa'=8] {'ta'}, dimensions={0} | all-to-all | bytes 131072 | tf_op jit(solution)/shard_map/all_to_all | solution.py:60
  207.0 74.5 %psum.44 = f32[32]{0:T(128)S(1)} all-reduce(f32[32]{0:T(128)S(1)} %reduce_sum.91), channel_id=1, replica_groups=mesh['ta'=4,'ha'=8,'wa'=8] {'ta','ha','wa'}, use_global_device_ids=true, to_apply=%region_8.9 | all-reduce | flops 32 | bytes 256 | tf_op jit(solution)/shard_map/psum | solution.py:31
  282.0 73.5 %psum.45 = f32[32]{0:T(128)S(1)} all-reduce(f32[32]{0:T(128)S(1)} %reduce_sum.116), channel_id=1, replica_groups=mesh['ta'=4,'ha'=8,'wa'=8] {'ta','ha','wa'}, use_global_device_ids=true, to_apply=%region_11.12 | all-reduce | flops 32 | bytes 256 | tf_op jit(solution)/shard_map/psum | solution.py:33
  355.9 1.7 collective-permute-start.4
  358.9 1.8 collective-permute-done.5
  360.7 3.9 collective-permute-start.6
  364.7 1.3 collective-permute-start.7
  366.2 4.2 collective-permute-done.7
  370.5 14.1 %all_gather.13 = bf16[4,10,10,512]{3,2,1,0:T(8,128)(2,1)S(1)} all-gather(bf16[1,10,10,512]{3,2,1,0:T(8,128)(2,1)S(1)} %pad_maximum_fusion.5), channel_id=1, replica_groups=mesh['ta'=4,'ha'=8,'wa'=8] {'ta'}, dimensions={0}, use_global_device_ids=true | all-gather | bytes 512000 | tf_op jit(solution)/shard_map/all_gather | solution.py:43
  393.0 7.9 %all_to_all.9 = bf16[4,8,8,128]{3,2,1,0:T(8,128)(2,1)S(1)} all-to-all(bf16[4,8,8,128]{3,2,1,0:T(8,128)(2,1)S(1)} %bitcast.380), channel_id=1, replica_groups=mesh['ta'=4,'ha'=8,'wa'=8] {'ta'}, dimensions={0} | all-to-all | bytes 131072 | tf_op jit(solution)/shard_map/all_to_all | solution.py:60
  401.1 74.7 %psum.46 = f32[32]{0:T(128)S(1)} all-reduce(f32[32]{0:T(128)S(1)} %reduce_sum.119), channel_id=1, replica_groups=mesh['ta'=4,'ha'=8,'wa'=8] {'ta','ha','wa'}, use_global_device_ids=true, to_apply=%region_14.15 | all-reduce | flops 32 | bytes 256 | tf_op jit(solution)/shard_map/psum | solution.py:31
  476.2 73.4 %psum.47 = f32[32]{0:T(128)S(1)} all-reduce(f32[32]{0:T(128)S(1)} %reduce_sum.122), channel_id=1, replica_groups=mesh['ta'=4,'ha'=8,'wa'=8] {'ta','ha','wa'}, use_global_device_ids=true, to_apply=%region_17.18 | all-reduce | flops 32 | bytes 256 | tf_op jit(solution)/shard_map/psum | solution.py:33
  551.7 75.6 %all-gather.5.cloned.1.call-done = bf16[4096,512]{1,0:T(8,128)(2,1)} async-done(((bf16[64,512]{1,0:T(8,128)(2,1)}), bf16[4096,512]{1,0:T(8,128)(2,1)}) %all-gather.5.cloned.1.call-update) | async-done | bytes 4194320 | tf_op jit(solution)/shard_map/all_gather | solution.py:114
  627.3 3.8 fusion.181
  631.4 74.8 %all-gather.7.cloned.1.call-done = bf16[4096,512]{1,0:T(8,128)(2,1)} async-done(((bf16[64,512]{1,0:T(8,128)(2,1)}), bf16[4096,512]{1,0:T(8,128)(2,1)}) %all-gather.7.cloned.1.call-update) | async-done | bytes 4194320 | tf_op jit(solution)/shard_map/all_gather | solution.py:115
  706.3 3.9 fusion.10
  (157 shorter events, 26.9 us)
Async XLA Ops:
  6.5 620.7 %copy-start = (bf16[512,512]{1,0:T(8,128)(2,1)S(1)}, bf16[512,512]{1,0:T(8,128)(2,1)}, u32[]{:S(2)}) copy-start(bf16[512,512]{1,0:T(8,128)(2,1)} %param.29) | copy-start | bytes 1572868
  6.5 620.7 %all-gather.5.cloned.1.call-start = ((), (), s32[]{:S(2)}) async-start(), calls=%async_computation.2 | async-start | bytes 4259840 | tf_op jit(solution)/shard_map/all_gather | solution.py:114
  162.1 3.0 collective-permute-start
  163.9 3.1 collective-permute-start.1
  167.0 5.4 collective-permute-start.2
  170.9 5.7 collective-permute-start.3
  196.3 2.4 copy-start.14
  196.7 159.1 %copy-start.9 = (f32[512]{0:T(512)S(1)}, f32[512]{0:T(512)}, u32[]{:S(2)}) copy-start(f32[512]{0:T(512)} %param.24) | copy-start | bytes 6148
  196.7 159.1 %copy-start.10 = (f32[512]{0:T(512)S(1)}, f32[512]{0:T(512)}, u32[]{:S(2)}) copy-start(f32[512]{0:T(512)} %param.23) | copy-start | bytes 6148
  355.9 3.0 collective-permute-start.4
  357.6 3.1 collective-permute-start.5
  360.7 5.4 collective-permute-start.6
  364.7 5.7 collective-permute-start.7
  390.2 2.5 copy-start.15
  390.4 10.4 %copy-start.3 = (bf16[1,8,8,512]{3,2,1,0:T(8,128)(2,1)S(1)}, bf16[1,8,8,512]{3,2,1,0:T(8,128)(2,1)}, u32[]{:S(2)}) copy-start(bf16[1,8,8,512]{3,2,1,0:T(8,128)(2,1)} %param.18) | copy-start | bytes 196612
  390.7 159.2 %copy-start.5 = (bf16[512,512]{1,0:T(8,128)(2,1)S(1)}, bf16[512,512]{1,0:T(8,128)(2,1)}, u32[]{:S(2)}) copy-start(bf16[512,512]{1,0:T(8,128)(2,1)} %param.31) | copy-start | bytes 1572868
  390.7 159.1 %copy-start.7 = (f32[512]{0:T(512)S(1)}, f32[512]{0:T(512)}, u32[]{:S(2)}) copy-start(f32[512]{0:T(512)} %param.28) | copy-start | bytes 6148
  390.7 159.1 %copy-start.8 = (f32[512]{0:T(512)S(1)}, f32[512]{0:T(512)}, u32[]{:S(2)}) copy-start(f32[512]{0:T(512)} %param.27) | copy-start | bytes 6148
  390.9 159.8 %copy-start.6 = (bf16[512,512]{1,0:T(8,128)(2,1)S(1)}, bf16[512,512]{1,0:T(8,128)(2,1)}, u32[]{:S(2)}) copy-start(bf16[512,512]{1,0:T(8,128)(2,1)} %param.32) | copy-start | bytes 1572868
  390.9 159.8 %copy-start.11 = (f32[512]{0:T(512)S(1)}, f32[512]{0:T(512)}, u32[]{:S(2)}) copy-start(f32[512]{0:T(512)} %param.33) | copy-start | bytes 6148
  391.2 236.1 %copy-start.12 = (f32[512]{0:T(512)S(1)}, f32[512]{0:T(512)}, u32[]{:S(2)}) copy-start(f32[512]{0:T(512)} %param.30) | copy-start | bytes 6148
  550.7 155.5 %all-gather.7.cloned.1.call-start = ((), (), s32[]{:S(2)}) async-start(), calls=%async_computation.3 | async-start | bytes 4259840 | tf_op jit(solution)/shard_map/all_gather | solution.py:115
  551.6 154.6 %copy-start.4 = (bf16[512,512]{1,0:T(8,128)(2,1)S(1)}, bf16[512,512]{1,0:T(8,128)(2,1)}, u32[]{:S(2)}) copy-start(bf16[512,512]{1,0:T(8,128)(2,1)} %param.34) | copy-start | bytes 1572868
  551.6 154.6 %copy-start.13 = (f32[512]{0:T(512)S(1)}, f32[512]{0:T(512)}, u32[]{:S(2)}) copy-start(f32[512]{0:T(512)} %param.35) | copy-start | bytes 6148
  (2 other events, 4.0 us)
Sparse Core Ops, SparseCore 0:
  550.8 76.3 all-gather.4
  630.0 76.1 all-gather.6
where the time goes:
time: 720 us; the launch traced here: 717 us
  blocking collectives  492 us (68%)
  waiting for transfers between devices  163 us (23%)
  matrix products  20.9 us (3%)
  starting transfers between devices  16.6 us (2%)
  between operations  14.1 us (2%)
    psum x3, blocking collectives, group_norm(): center = lax.psum(jnp.sum(grouped, axis=(0, 2)), ('ta', 'ha', 'wa')) / count  228 us
    psum x3, blocking collectives, group_norm(): lax.psum(jnp.sum(deviation * deviation, axis=(0, 2)), ('ta', 'ha', 'wa'))  220 us
    all_gather x1, waiting for transfers between devices, body(): absorb_keys = lax.all_gather(keys, ('ha', 'wa'), axis=1, tiled=True)  75.6 us
    all_gather x1, waiting for transfers between devices, body(): absorb_values = lax.all_gather(values, ('ha', 'wa'), axis=1, tiled=True)  74.8 us
    all_gather x2, blocking collectives, causal_conv(): gathered = lax.all_gather(rimmed, 'ta', axis=0, tiled=True)  27.9 us
    all_to_all x2, blocking collectives, causal_conv(): return lax.all_to_all(result, 'ta', split_axis=0, concat_axis=3, tiled=True)  15.8 us
  transfers between devices with their start and end apart: 10, of which 8 were waited for; matrix products, arithmetic and copies ran while one was open for 1% of the time, Pallas kernels for 0%

commit v1 on v0

v1 whole, which is shorter than its diff:
```python
import functools

import jax
import jax.numpy as jnp
from jax import lax
from jax.experimental import pallas as pl
from jax.experimental.pallas import tpu as pltpu
from jax.sharding import Mesh, PartitionSpec as P

GROUPS = 32
EPS = 1e-06
HA = ("y", "core")
BF = jnp.bfloat16
F32 = jnp.float32
LANES = 128
LIMIT = 32 * 1024 * 1024
VMEM = pl.BlockSpec(memory_space=pltpu.VMEM)


def lane_in_group(shape):
    return lax.broadcasted_iota(jnp.int32, shape, 1) & 15


def segment_sum(x):
    lane = lane_in_group(x.shape)
    for bit in (1, 2, 4, 8):
        after = pltpu.roll(x, LANES - bit, 1)
        before = pltpu.roll(x, bit, 1)
        x = x + jnp.where((lane & bit) == 0, after, before)
    return x


def rows8(x):
    return jnp.broadcast_to(x, (8, LANES))


def cell_rows(rows, pitch):
    index = lax.broadcasted_iota(jnp.int32, (rows, LANES), 0)
    row = (index * {10: 52429, 12: 43691}[pitch]) >> 19
    return row, index - row * pitch


def encode(out_ref, stats):
    lane = lane_in_group((8, LANES))
    row = jnp.zeros((8, LANES), F32)
    for block, mean, spread in stats:
        row = jnp.where(lane == block, mean, row)
        row = jnp.where(lane == block + 4, spread, row)
    out_ref[...] = jnp.broadcast_to(row[0:1][None], out_ref.shape)


def thirds(x):
    high = x.astype(BF).astype(F32)
    middle = (x - high).astype(BF).astype(F32)
    return high, middle, x - high - middle


def pack_stats(mean, spread):
    row = lax.broadcasted_iota(jnp.int32, mean.shape, 0)
    packed = jnp.zeros(mean.shape, F32)
    for k, piece in enumerate(thirds(mean) + thirds(spread)):
        packed = jnp.where(row == k, piece, packed)
    return packed.astype(BF)


def unpack_stats(packed):
    x = packed.astype(F32)
    return x[0:1] + x[1:2] + x[2:3], x[3:4] + x[4:5] + x[5:6]


def merge_stats(stats):
    scale = 1.0 / len(stats)
    middle = sum(mean for mean, _ in stats) * scale
    spread = sum(spread + (mean - middle) * (mean - middle) for mean, spread in stats) * scale
    return middle, spread


def all_rows(x):
    return jnp.broadcast_to(x, (8, x.shape[1]))


def channel_stats(x, keep, count):
    mean = jnp.sum(x, axis=0, keepdims=True) * (1.0 / count)
    deviation = x - mean
    if keep is not None:
        deviation = jnp.where(keep, deviation, 0.0)
    spread = jnp.sum(deviation * deviation, axis=0, keepdims=True) * (1.0 / count)
    return group_stats(mean, spread)


def group_stats(mean, spread):
    mean, spread = rows8(mean), rows8(spread)
    middle = segment_sum(mean) * (1.0 / 16)
    off = mean - middle
    return middle, segment_sum(spread + off * off) * (1.0 / 16)


def tile_stats(rows_ref):
    rows = rows_ref[...].reshape(rows_ref.shape[0], LANES)
    count = rows.shape[0]
    mean = jnp.sum(rows, axis=0, keepdims=True) * (1.0 / count)
    off = rows - mean
    between = jnp.sum(off * off, axis=0, keepdims=True) * (1.0 / count)
    return rows8(mean), rows8(between)


def block_stats(mean, between, block):
    lane = lane_in_group((8, LANES))
    middle = segment_sum(jnp.where(lane == block, mean, 0.0))
    spread = segment_sum(jnp.where(lane == block + 4, mean, jnp.where(lane == block, between, 0.0)))
    return middle[0:1], lax.rsqrt(spread[0:1] + EPS)


def decode(rows_ref, small_ref, at):
    mean, between = tile_stats(rows_ref)
    result = []
    for block in range(4):
        middle, inverse = block_stats(mean, between, block)
        gain, shift = gain_and_shift(small_ref, at, block)
        result.append((middle, inverse * gain, shift))
    return result


def gain_and_shift(small_ref, at, block):
    return small_ref[at + block : at + block + 1, :], small_ref[at + 4 + block : at + 5 + block, :]


def wide(small_ref, at):
    return jnp.concatenate([small_ref[at + b : at + b + 1, :] for b in range(4)], axis=1)


def silu(v):
    half = 0.5 * v
    return half + half * jnp.tanh(half)


def turned(ta, s):
    return lax.rem(ta - s + 4, 4)


def first_kernel(latent_ref, out_ref):
    out_ref[...] = latent_ref[...]


def frame_moments_kernel(s0, s1, s2, s3, out_ref, first_ref, last_ref):
    slots = (s0, s1, s2, s3)
    stats = []
    for block in range(4):
        x = jnp.concatenate(
            [ref[:, block * LANES : (block + 1) * LANES].astype(F32) for ref in slots], axis=0
        )
        stats.append((block,) + channel_stats(x, None, x.shape[0]))
    encode(out_ref, stats)
    for s, ref in enumerate(slots):
        first_ref[s] = ref[0:16, :]
        last_ref[s] = ref[48:64, :]


def columns_kernel(s0, s1, s2, s3, top_ref, bottom_ref, first_ref, last_ref, tall, sides):
    for s, ref in enumerate((s0, s1, s2, s3)):
        for b in range(4):
            lanes = slice(b * LANES, (b + 1) * LANES)
            tall[b, 0:16, :] = top_ref[s, :, lanes].astype(F32)
            tall[b, 16:80, :] = ref[:, lanes].astype(F32)
            tall[b, 80:96, :] = bottom_ref[s, :, lanes].astype(F32)
            for k, out_ref in ((0, first_ref), (6, last_ref)):
                for j in range(2):
                    sides[b, 12 * j : 12 * j + 12, :] = tall[b, pl.ds(j + k, 12, stride=8), :]
                out_ref[s, :, lanes] = sides[b].astype(BF)


def activate_kernel(grid, hidden_ref, rows_ref, small_ref, out_ref):
    ta = lax.axis_index("ta")
    middle, inverse = block_stats(*tile_stats(rows_ref), 0)
    scale = inverse * small_ref[pl.ds(8 + ta, 1), :]
    shift = small_ref[pl.ds(12 + ta, 1), :]
    keep = inside(8 * lax.axis_index(HA) - 1, 8 * lax.axis_index("z") - 1, 104, 10, grid)
    for f in range(4):
        v = (hidden_ref[f].astype(F32) - middle) * scale + shift
        out_ref[f] = jnp.where(keep, silu(v), 0.0).astype(BF)


def residual_kernel(s0, s1, s2, s3, out_ref, parts):
    for s, ref in enumerate((s0, s1, s2, s3)):
        parts[turned(lax.axis_index("ta"), s)] = ref[...]
    out_ref[...] = jnp.concatenate([parts[b] for b in range(4)], axis=1)


def merge_kernel(*refs):
    slots, out_ref = refs[:-1], refs[-1]
    room = out_ref.shape[0] - 8
    middle, spread = merge_stats([unpack_stats(ref[64:72, :]) for ref in slots])
    for s in range(room // 64):
        out_ref[64 * s : 64 * s + 64, :] = slots[s][0:64, :]
    out_ref[room : room + 8, :] = pack_stats(all_rows(middle), all_rows(spread))


def convolve(lhs, weights, product, frame_rows, pitch, out_rows):
    for pair in ((0, 1), (2, 3), (4, 5), (6, 7), (8,)):
        rhs = jnp.concatenate(
            [jnp.concatenate([weights[9 * d + s] for s in pair], axis=1) for d in range(3)], axis=0
        )
        lane = pair[0] * LANES
        product[0 : 4 * frame_rows, lane : lane + rhs.shape[1]] = jnp.dot(
            lhs[...], rhs, preferred_element_type=F32
        )
    totals = []
    for f in range(4):
        total = None
        for s in range(9):
            at = f * frame_rows + pitch * (s // 3) + s % 3
            piece = product[at : at + out_rows, s * LANES : (s + 1) * LANES]
            total = piece if total is None else total + piece
        totals.append(total)
    return totals


def inside(base_row, base_column, rows, pitch, grid):
    row, column = cell_rows(rows, pitch)
    row, column = row + base_row, column + base_column
    return (row >= 0) & (row < grid[0]) & (column >= 0) & (column < grid[1])


def rimmed_kernel(
    grid,
    s0,
    s1,
    s2,
    s3,
    top_ref,
    bottom_ref,
    left_ref,
    right_ref,
    rows_ref,
    small_ref,
    lhs_ref,
    own_ref,
    frames,
    tile,
    sides,
):
    ta = lax.axis_index("ta")
    coefficients = decode(rows_ref, small_ref, 0)
    keep = inside(8 * lax.axis_index(HA) - 2, 8 * lax.axis_index("z") - 2, 144, 12, grid)
    for s, ref in enumerate((s0, s1, s2, s3)):
        frames[turned(ta, s)] = ref[...]
    for frame in range(4):
        s = turned(ta, frame)
        own = jnp.zeros((64, LANES), F32)
        for b in range(4):
            lanes = slice(b * LANES, (b + 1) * LANES)
            middle = frames[frame, :, lanes].astype(F32)
            own = jnp.where(ta == b, middle, own)
            top, bottom = top_ref[s, :, lanes].astype(F32), bottom_ref[s, :, lanes].astype(F32)
            for r in range(12):
                if r < 2:
                    piece = top[8 * r : 8 * r + 8]
                elif r < 10:
                    piece = middle[8 * (r - 2) : 8 * (r - 2) + 8]
                else:
                    piece = bottom[8 * (r - 10) : 8 * (r - 10) + 8]
                tile[b, 12 * r + 2 : 12 * r + 10, :] = piece
            for k, side_ref in ((0, left_ref), (10, right_ref)):
                sides[b] = side_ref[s, :, lanes].astype(F32)
                for j in range(2):
                    tile[b, pl.ds(j + k, 12, stride=12), :] = sides[b, 12 * j : 12 * j + 12, :]
            mean, scale, shift = coefficients[b]
            v = (tile[b] - mean) * scale + shift
            act = jnp.where(keep, silu(v), 0.0).astype(BF)
            for f in range(4):
                for d in range(3):
                    if max(f + d - 2, 0) == frame:
                        lane = (4 * d + b) * LANES
                        lhs_ref[f * 144 : (f + 1) * 144, lane : lane + LANES] = act
        own_ref[frame] = own.astype(BF)


def first_conv_kernel(lhs, small_ref, kernel_ref, out_ref, moments_ref, product, wide_rows, tight_rows):
    totals = convolve(lhs, kernel_ref, product, 144, 12, 120)
    row, column = cell_rows(104, 10)
    keep = (row >= 1) & (row <= 8) & (column >= 1) & (column <= 8)
    bias = small_ref[36:37, :]
    kept = []
    for f in range(4):
        wide_rows[f] = totals[f] + bias
        for r in range(10):
            tight_rows[f, 10 * r : 10 * r + 10, :] = wide_rows[f, 12 * r : 12 * r + 10, :]
        tight_rows[f, 100:104, :] = jnp.zeros((4, LANES), F32)
        hidden = tight_rows[f].astype(BF)
        out_ref[f] = hidden
        kept.append(jnp.where(keep, hidden.astype(F32), 0.0))
    mean = sum(jnp.sum(x, axis=0, keepdims=True) for x in kept) * (1.0 / 256)
    squares = [jnp.square(jnp.where(keep, x - mean, 0.0)) for x in kept]
    spread = sum(jnp.sum(x, axis=0, keepdims=True) for x in squares) * (1.0 / 256)
    encode(moments_ref, [(0,) + group_stats(mean, spread)])


def second_conv_kernel(
    s0,
    s1,
    s2,
    s3,
    small_ref,
    own_ref,
    kernel_ref,
    out0,
    out1,
    out2,
    out3,
    lhs,
    product,
    wide_rows,
    parts,
):
    ta = lax.axis_index("ta")
    for s, ref in enumerate((s0, s1, s2, s3)):
        block = turned(ta, s)
        for f in range(4):
            for d in range(3):
                lane = pl.multiple_of((4 * d + block) * LANES, LANES)
                lhs[f * 112 : f * 112 + 104, pl.ds(lane, LANES)] = ref[max(f + d - 2, 0)]
    totals = convolve(lhs, kernel_ref, product, 112, 10, 80)
    bias = small_ref[37:38, :]
    tiles = []
    for f in range(4):
        wide_rows[f] = totals[f] + bias
        branch = jnp.concatenate([wide_rows[f, 10 * r : 10 * r + 8, :] for r in range(8)], axis=0)
        branch = branch.astype(BF).astype(F32)
        residual = (own_ref[f].astype(F32) + branch).astype(BF)
        parts[f] = residual
        tiles.append(residual.astype(F32))
    mean, spread = channel_stats(jnp.concatenate(tiles, axis=0), None, 256)
    packed = pack_stats(mean, spread)
    for s, ref in enumerate((out0, out1, out2, out3)):
        ref[0:64, :] = parts[lax.rem(ta + s, 4)]
        ref[64:72, :] = packed


def normalise(x, coefficients):
    parts = []
    for b, (mean, scale, shift) in enumerate(coefficients):
        part = x[:, b * LANES : (b + 1) * LANES].astype(F32)
        parts.append(((part - mean) * scale + shift).astype(BF))
    return jnp.concatenate(parts, axis=1)


def attention_kernel(*refs):
    asked, told = refs[:4], refs[4:6]
    small_ref, query_ref, key_ref = refs[6:9]
    outs, normed = refs[9:13], refs[13]
    middle, spread = merge_stats([unpack_stats(ref[512:520, :]) for ref in told])
    inverse = lax.rsqrt(spread + EPS)
    coefficients = []
    for b in range(4):
        lanes = slice(b * LANES, (b + 1) * LANES)
        gain, shift = gain_and_shift(small_ref, 16, b)
        coefficients.append((middle[:, lanes], inverse[:, lanes] * gain, shift))
    normed_q = normalise(jnp.concatenate([ref[0:64, :] for ref in asked], axis=0), coefficients)
    for k, ref in enumerate(told):
        normed[512 * k : 512 * k + 512, :] = normalise(ref[0:512, :], coefficients)
    queries = jnp.dot(normed_q, query_ref[...], preferred_element_type=F32) + wide(small_ref, 24)
    folded = lax.dot_general(
        queries.astype(BF), key_ref[...], (((1,), (1,)), ((), ())), preferred_element_type=F32
    ).astype(BF)
    scores = lax.dot_general(
        folded, normed[...], (((1,), (1,)), ((), ())), preferred_element_type=F32
    ) * 512 ** (-0.5)
    highest = jnp.max(scores, axis=1, keepdims=True)
    weights = jnp.exp(scores - highest)
    total = jnp.sum(weights, axis=1, keepdims=True)
    mixed = jnp.dot(weights.astype(BF), normed[...], preferred_element_type=F32) / total
    level = highest + jnp.log(total)
    top, middle, low = thirds(level)
    lane = lax.broadcasted_iota(jnp.int32, (256, LANES), 1)
    tail = jnp.where(lane == 0, top, jnp.where(lane == 1, middle, jnp.where(lane == 2, low, 0.0)))
    for s, ref in enumerate(outs):
        ref[:, 0:512] = mixed[64 * s : 64 * s + 64].astype(BF)
        ref[:, 512:640] = tail[64 * s : 64 * s + 64].astype(BF)


def finish_kernel(b0, b1, b2, b3, residual_ref, small_ref, value_ref, output_ref, out_ref):
    backs = [ref[...].astype(F32) for ref in (b0, b1, b2, b3)]
    levels = [jnp.sum(back[:, 512:640], axis=1, keepdims=True) for back in backs]
    highest = functools.reduce(jnp.maximum, levels)
    shares = [jnp.exp(level - highest) for level in levels]
    inverse = 1.0 / sum(shares)
    mean_normed = sum(back[:, 0:512] * (share * inverse) for back, share in zip(backs, shares))
    attended = jnp.dot(mean_normed.astype(BF), value_ref[...], preferred_element_type=F32)
    attended = (attended + wide(small_ref, 28)).astype(BF)
    mixed = jnp.dot(attended, output_ref[...], preferred_element_type=F32)
    out_ref[...] = (residual_ref[0:64, :].astype(F32) + mixed + wide(small_ref, 32)).astype(BF)


def call(kernel, out_shape, specs, scratch, flops, *args):
    shapes = out_shape if isinstance(out_shape, tuple) else (out_shape,)
    moved = sum(a.size * a.dtype.itemsize for a in args) + sum(
        s.size * jnp.dtype(s.dtype).itemsize for s in shapes
    )
    return pl.pallas_call(
        kernel,
        out_shape=out_shape,
        in_specs=specs,
        out_specs=tuple(VMEM for _ in shapes) if isinstance(out_shape, tuple) else VMEM,
        scratch_shapes=scratch,
        compiler_params=pltpu.CompilerParams(vmem_limit_bytes=LIMIT),
        cost_estimate=pl.CostEstimate(flops=flops, bytes_accessed=moved, transcendentals=0),
    )(*args)


def ring(count, step):
    return [(i, (i + step) % count) for i in range(count)]


def long_first(count):
    return sorted(range(1, count), key=lambda s: -min(s, count - s))


def spread_out(blocks, axis, sign=1):
    count = lax.axis_size(axis)
    arrived = {0: blocks[0]}
    for s in long_first(count):
        arrived[s] = lax.ppermute(blocks[s], axis, ring(count, sign * s))
    return [arrived[s] for s in range(count)]


def around(block, axis):
    return spread_out([block] * lax.axis_size(axis), axis)


def relayed(block, axis):
    count = lax.axis_size(axis)
    after = {step: lax.ppermute(block, axis, ring(count, step)) for step in (2, 1, -1, -2)}
    further = [lax.ppermute(after[step], axis, ring(count, move)) for step, move in ((1, 2), (-1, -2), (2, 2))]
    return [block, *after.values(), *further]


def both_sides(low, high, axis):
    count = lax.axis_size(axis)
    return lax.ppermute(high, axis, ring(count, 1)), lax.ppermute(low, axis, ring(count, -1))


def over_tiles(rows):
    return lax.all_to_all(rows, HA + ("z",), split_axis=0, concat_axis=0, tiled=True)


def body(
    latent,
    norm1_gain,
    norm1_shift,
    conv1_kernel,
    conv1_shift,
    norm2_gain,
    norm2_shift,
    conv2_kernel,
    conv2_shift,
    norm3_gain,
    norm3_shift,
    query_weight,
    query_shift,
    key_weight,
    value_weight,
    value_shift,
    output_weight,
    output_shift,
):
    _, height, width, channels = latent.shape
    cells = height * width
    tiles = lax.axis_size(HA) * lax.axis_size("z")
    grid = (lax.axis_size(HA) * height, lax.axis_size("z") * width)
    vectors = [norm1_gain, norm1_shift, norm2_gain, norm2_shift, norm3_gain, norm3_shift]
    vectors += [query_shift, value_shift, output_shift, conv1_shift, conv2_shift]
    small = jnp.concatenate(vectors).reshape(-1, LANES)

    def bf(*shape):
        return jax.ShapeDtypeStruct(shape, BF)

    rows = jax.ShapeDtypeStruct((tiles, 1, LANES), F32)

    slots = around(latent[0].reshape(cells, channels), "ta")
    slots[0] = call(first_kernel, bf(cells, channels), [VMEM], [], 4 * 10**9, slots[0])
    rows1, low, high = call(
        frame_moments_kernel, (rows, bf(4, 16, channels), bf(4, 16, channels)), [VMEM] * 4, [], 10**6, *slots
    )
    top, bottom = both_sides(low, high, HA)
    rows1 = over_tiles(rows1)
    low, high = call(
        columns_kernel,
        (bf(4, 24, channels), bf(4, 24, channels)),
        [VMEM] * 6,
        [pltpu.VMEM((4, 96, LANES), F32), pltpu.VMEM((4, 24, LANES), F32)],
        10**6,
        *slots,
        top,
        bottom,
    )
    left, right = both_sides(low, high, "z")
    lhs, own = call(
        functools.partial(rimmed_kernel, grid),
        (bf(576, 1536), bf(4, cells, LANES)),
        [VMEM] * 10,
        [pltpu.VMEM((4, cells, channels), BF), pltpu.VMEM((4, 144, LANES), F32), pltpu.VMEM((4, 24, LANES), F32)],
        4 * 10**9,
        *slots,
        top,
        bottom,
        left,
        right,
        rows1,
        small,
    )
    hidden, rows2 = call(
        first_conv_kernel,
        (bf(4, 104, LANES), rows),
        [VMEM] * 3,
        [
            pltpu.VMEM((584, 1152), F32),
            pltpu.VMEM((4, 120, LANES), F32),
            pltpu.VMEM((4, 104, LANES), F32),
        ],
        2 * 10**9,
        lhs,
        small,
        conv1_kernel,
    )

    act = call(
        functools.partial(activate_kernel, grid),
        bf(4, 104, LANES),
        [VMEM] * 3,
        [],
        4 * 10**9,
        hidden,
        over_tiles(rows2),
        small,
    )
    parts = call(
        second_conv_kernel,
        (bf(cells + 8, LANES),) * 4,
        [VMEM] * 7,
        [
            pltpu.VMEM((448, 1536), BF),
            pltpu.VMEM((448, 1152), F32),
            pltpu.VMEM((4, 80, LANES), F32),
            pltpu.VMEM((4, cells, LANES), BF),
        ],
        2 * 10**9,
        *around(act, "ta"),
        small,
        own,
        conv2_kernel,
    )

    residual = call(
        residual_kernel,
        bf(cells + 8, channels),
        [VMEM] * 4,
        [pltpu.VMEM((4, cells + 8, LANES), BF)],
        10**6,
        *spread_out(parts, "ta"),
    )
    asked = around(residual, "y")
    told = call(merge_kernel, bf(cells + 8, channels), [VMEM] * 4, [], 10**6, *asked)
    told = call(merge_kernel, bf(8 * cells + 8, channels), [VMEM] * 8, [], 10**6, *relayed(told, "z"))
    packed = call(
        attention_kernel,
        (bf(cells, channels + LANES),) * 4,
        [VMEM] * 9,
        [pltpu.VMEM((1024, channels), BF)],
        10**9,
        *asked,
        told,
        lax.ppermute(told, "core", ring(2, 1)),
        small,
        query_weight,
        key_weight,
    )

    block_out = call(
        finish_kernel,
        bf(cells, channels),
        [VMEM] * 8,
        [],
        10**8,
        *spread_out(packed, "y", -1),
        residual,
        small,
        value_weight,
        output_weight,
    )
    return block_out.reshape(latent.shape)


def solution(mesh):
    frames, rows, columns = mesh.devices.shape
    split = Mesh(mesh.devices.reshape(frames, rows // 2, 2, columns), ("ta", "y", "core", "z"))
    tile = P("ta", HA, "z", None)
    kernel, shift = P(None, None, "ta"), P("ta")
    in_specs = (tile, P(), P(), kernel, shift, P(), P(), kernel, shift) + (P(),) * 9
    return jax.shard_map(body, mesh=split, in_specs=in_specs, out_specs=tile, check_vma=False)
```

time: 720 us -> 115 us (0.16)
  blocking collectives: 492 us -> 16.8 us
  waiting for transfers between devices: 163 us -> 40.4 us
  starting transfers between devices: 16.6 us -> 42.4 us
  matrix products: 20.9 us -> 0 us
  between operations: 14.1 us -> 0.28 us
  Pallas kernels: 0 us -> 11.4 us
    psum x6 -> x0, blocking collectives: 448 us -> none  [the longest x3 228 us: group_norm(): center = lax.psum(jnp.sum(grouped, axis=(0, 2)), ('ta', 'ha', 'wa')) / count]
    all_gather x2 -> x0, waiting for transfers between devices: 150 us -> none  [the longest x1 75.6 us: body(): absorb_keys = lax.all_gather(keys, ('ha', 'wa'), axis=1, tiled=True)]
    all_gather x2 -> x0, blocking collectives: 27.9 us -> none  [causal_conv(): gathered = lax.all_gather(rimmed, 'ta', axis=0, tiled=True)]
    ppermute x8 -> x27, waiting for transfers between devices: 12.3 us -> 34.4 us  [the longest x15 23.8 us: spread_out(): arrived[s] = lax.ppermute(blocks[s], axis, ring(count, sign * s))]
    dot_general x58 -> x0, matrix products: 20.9 us -> none  [the longest x54 11.5 us: causal_conv(): jnp.dot(window.reshape(-1, channels), kernel[tap], preferred_element_type...]
    ppermute x8 -> x27, starting transfers between devices: 16.5 us -> 32.4 us  [the longest x15 16.8 us: spread_out(): arrived[s] = lax.ppermute(blocks[s], axis, ring(count, sign * s))]
    pallas_call x0 -> x12, Pallas kernels: none -> 11.4 us  [call(): pl.pallas_call(kernel, out_shape=out_shape, in_specs=specs, out_specs=tup...]
    all_to_all x0 -> x1, starting transfers between devices: none -> 10 us  [over_tiles(): lax.all_to_all(rows, HA + ('z',), split_axis=0, concat_axis=0, tiled=True)]
  transfers between devices with their start and end apart: 10 -> 28, of which waited for: 8 -> 22; matrix products, arithmetic and copies ran while one was open for 1% -> 0% of each run, Pallas kernels for 0% -> 0%
where the time goes in v1:
time: 115 us; the launch traced here: 114 us
  starting transfers between devices  42.4 us (37%)
  waiting for transfers between devices  40.4 us (35%)
  blocking collectives  16.8 us (15%)
  Pallas kernels  11.4 us (10%)
  local copies, waits for them, and re-layouts  2.63 us (2%)
    ppermute x15, waiting for transfers between devices, spread_out(): arrived[s] = lax.ppermute(blocks[s], axis, ring(count, sign * s))  23.8 us
    ppermute x15, starting transfers between devices, spread_out(): arrived[s] = lax.ppermute(blocks[s], axis, ring(count, sign * s))  16.8 us
    all_to_all x1, blocking collectives, over_tiles(): lax.all_to_all(rows, HA + ('z',), split_axis=0, concat_axis=0, tiled=True)  16.8 us
    pallas_call x12, Pallas kernels, call(): pl.pallas_call(kernel, out_shape=out_shape, in_specs=specs, out_specs=tup...  11.4 us
    all_to_all x1, starting transfers between devices, over_tiles(): lax.all_to_all(rows, HA + ('z',), split_axis=0, concat_axis=0, tiled=True)  10 us
    ppermute x3, waiting for transfers between devices, relayed(): lax.ppermute(after[step], axis, ring(count, move))  6.46 us
    ppermute x4, starting transfers between devices, relayed(): lax.ppermute(block, axis, ring(count, step))  6.24 us
    all_to_all x1, waiting for transfers between devices, over_tiles(): lax.all_to_all(rows, HA + ('z',), split_axis=0, concat_axis=0, tiled=True)  6.01 us
  transfers between devices with their start and end apart: 28, of which 22 were waited for; matrix products, arithmetic and copies ran while one was open for 0% of the time, Pallas kernels for 0%

profile of v1, /device:TPU:6, one launch (start us, length us, event | category | flops | bytes accessed | tf_op | source)
XLA Modules:
  0.0 114.0 jit_solution(1120890189309906444)
XLA Ops:
  0.8 2.8 %collective-permute-start.1 = (bf16[64,512]{1,0:T(8,128)(2,1)}, bf16[64,512]{1,0:T(8,128)(2,1)S(1)}, u32[]{:S(2)}, u32[]{:S(2)}) collective-permute-start(bf16[64,512]{1,0:T(8,128)(2,1)} %bitcast.10), channel_id=1, source_target_pairs={{0,128},{64,192},{128,0},{192,64},{1,129},{65,193},{129,1},{193,65... | collective-permute-start | bytes 196616 | tf_op jit(solution)/shard_map/ppermute | solution.py:422
  9.4 3.0 %collective-permute-start.4 = (bf16[4,16,512]{2,1,0:T(8,128)(2,1)S(1)}, bf16[4,16,512]{2,1,0:T(8,128)(2,1)S(1)}, u32[]{:S(2)}, u32[]{:S(2)}) collective-permute-start(bf16[4,16,512]{2,1,0:T(8,128)(2,1)S(1)} %get-tuple-element.23), channel_id=1, source_target_pairs={{0,56},{8,0},{16,8},{24,16},{32,24},{40,32},{48,40},{56,48},{1,57}... | collective-permute-start | bytes 196616 | tf_op jit(solution)/shard_map/ppermute | solution.py:439
  12.4 10.0 %all-to-all-start = ((f32[64,1,128]{2,1,0:T(1,128)}), f32[64,1,128]{2,1,0:T(1,128)S(1)}, u32[]{:S(2)}, u32[]{:S(2)}) async-start(f32[64,1,128]{2,1,0:T(1,128)} %get-tuple-element.26), calls=%async_computation | async-start | bytes 65536 | tf_op jit(solution)/shard_map/all_to_all | solution.py:443
  22.6 1.6 %collective-permute-start.5 = (bf16[4,24,512]{2,1,0:T(8,128)(2,1)S(1)}, bf16[4,24,512]{2,1,0:T(8,128)(2,1)S(1)}, u32[]{:S(2)}, u32[]{:S(2)}) collective-permute-start(bf16[4,24,512]{2,1,0:T(8,128)(2,1)S(1)} %get-tuple-element.24), channel_id=1, source_target_pairs={{0,1},{1,2},{2,3},{3,4},{4,5},{5,6},{6,7},{7,0},{8,9},{9,10},{10,1... | collective-permute-start | bytes 294920 | tf_op jit(solution)/shard_map/ppermute | solution.py:439
  24.2 1.7 %collective-permute-start.6 = (bf16[4,24,512]{2,1,0:T(8,128)(2,1)S(1)}, bf16[4,24,512]{2,1,0:T(8,128)(2,1)S(1)}, u32[]{:S(2)}, u32[]{:S(2)}) collective-permute-start(bf16[4,24,512]{2,1,0:T(8,128)(2,1)S(1)} %get-tuple-element.25), channel_id=1, source_target_pairs={{0,7},{1,0},{2,1},{3,2},{4,3},{5,4},{6,5},{7,6},{8,15},{9,8},{10,9... | collective-permute-start | bytes 294920 | tf_op jit(solution)/shard_map/ppermute | solution.py:439
  25.9 6.0 %all-to-all-done.rows_ref = f32[64,1,128]{2,1,0:T(1,128)S(1)} async-done(((f32[64,1,128]{2,1,0:T(1,128)}), f32[64,1,128]{2,1,0:T(1,128)S(1)}, u32[]{:S(2)}, u32[]{:S(2)}) %all-to-all-start) | async-done | bytes 32800 | tf_op jit(solution)/shard_map/all_to_all | solution.py:443
  33.9 3.2 %shard_map.176 = (bf16[4,104,128]{2,1,0:T(8,128)(2,1)S(1)}, f32[64,1,128]{2,1,0:T(1,128)S(1)}) custom-call(bf16[576,1536]{1,0:T(8,128)(2,1)S(1)} %get-tuple-element.27.lhs, f32[38,128]{1,0:T(8,128)S(1)} %bitcast.4, bf16[27,512,128]{2,1,0:T(8,128)(2,1)S(1)} %copy-done.2), custom_call_target="tpu_custom_call" | custom-call | flops 2000000000 | bytes 5467136 | tf_op jit(solution)/shard_map/pallas_call | solution.py:399
  37.1 16.8 %all_to_all.10.rows_ref = f32[64,1,128]{2,1,0:T(1,128)S(1)} all-to-all(f32[64,1,128]{2,1,0:T(1,128)S(1)} %get-tuple-element.29), channel_id=1, replica_groups=mesh['ta'=4,'y'=4,'core'=2,'z'=8] {'y','core','z'}, dimensions={0} | all-to-all | bytes 65536 | tf_op jit(solution)/shard_map/all_to_all | solution.py:443
  55.7 2.8 %collective-permute-start.8 = (bf16[4,104,128]{2,1,0:T(8,128)(2,1)S(1)}, bf16[4,104,128]{2,1,0:T(8,128)(2,1)S(1)}, u32[]{:S(2)}, u32[]{:S(2)}) collective-permute-start(bf16[4,104,128]{2,1,0:T(8,128)(2,1)S(1)} %shard_map.177.s0), channel_id=1, source_target_pairs={{0,128},{64,192},{128,0},{192,64},{1,129},{65,193},{129,1},{193,65... | collective-permute-start | bytes 319496 | tf_op jit(solution)/shard_map/ppermute | solution.py:422
  58.6 2.3 %collective-permute-done.9.s3 = bf16[4,104,128]{2,1,0:T(8,128)(2,1)S(1)} collective-permute-done((bf16[4,104,128]{2,1,0:T(8,128)(2,1)S(1)}, bf16[4,104,128]{2,1,0:T(8,128)(2,1)S(1)}, u32[]{:S(2)}, u32[]{:S(2)}) %collective-permute-start.9) | collective-permute-done | bytes 106528 | tf_op jit(solution)/shard_map/ppermute | solution.py:422
  60.9 2.4 %collective-permute-done.8.s2 = bf16[4,104,128]{2,1,0:T(8,128)(2,1)S(1)} collective-permute-done((bf16[4,104,128]{2,1,0:T(8,128)(2,1)S(1)}, bf16[4,104,128]{2,1,0:T(8,128)(2,1)S(1)}, u32[]{:S(2)}, u32[]{:S(2)}) %collective-permute-start.8) | collective-permute-done | bytes 106528 | tf_op jit(solution)/shard_map/ppermute | solution.py:422
  63.4 2.8 %shard_map.178 = (bf16[72,128]{1,0:T(8,128)(2,1)S(1)}, bf16[72,128]{1,0:T(8,128)(2,1)S(1)}, bf16[72,128]{1,0:T(8,128)(2,1)S(1)}, bf16[72,128]{1,0:T(8,128)(2,1)S(1)}) custom-call(bf16[4,104,128]{2,1,0:T(8,128)(2,1)S(1)} %shard_map.177.s0, bf16[4,104,128]{2,1,0:T(8,128)(2,1)S(1)} %collective-permute-done.7.s1, ...), custom_call_target="tpu_custom_call" | custom-call | flops 2000000000 | bytes 4123648 | tf_op jit(solution)/shard_map/pallas_call | solution.py:399
  66.3 2.3 %collective-permute-start.10 = (bf16[72,128]{1,0:T(8,128)(2,1)S(1)}, bf16[72,128]{1,0:T(8,128)(2,1)S(1)}, u32[]{:S(2)}, u32[]{:S(2)}) collective-permute-start(bf16[72,128]{1,0:T(8,128)(2,1)S(1)} %get-tuple-element.32), channel_id=1, source_target_pairs={{0,64},{64,128},{128,192},{192,0},{1,65},{65,129},{129,193},{193,1... | collective-permute-start | bytes 55304 | tf_op jit(solution)/shard_map/ppermute | solution.py:422
  70.1 3.7 %collective-permute-done.11.s2 = bf16[72,128]{1,0:T(8,128)(2,1)S(1)} collective-permute-done((bf16[72,128]{1,0:T(8,128)(2,1)S(1)}, bf16[72,128]{1,0:T(8,128)(2,1)S(1)}, u32[]{:S(2)}, u32[]{:S(2)}) %collective-permute-start.11) | collective-permute-done | bytes 18464 | tf_op jit(solution)/shard_map/ppermute | solution.py:422
  75.3 1.7 %collective-permute-start.14 = (bf16[72,512]{1,0:T(8,128)(2,1)S(1)}, bf16[72,512]{1,0:T(8,128)(2,1)S(1)}, u32[]{:S(2)}, u32[]{:S(2)}) collective-permute-start(bf16[72,512]{1,0:T(8,128)(2,1)S(1)} %shard_map.179.refs_0_.residual_ref), channel_id=1, source_target_pairs={{0,32},{16,48},{32,0},{48,16},{1,33},{17,49},{33,1},{49,17},{2,34}... | collective-permute-start | bytes 221192 | tf_op jit(solution)/shard_map/ppermute | solution.py:422
  77.0 1.5 %collective-permute-done.15.refs_3_ = bf16[72,512]{1,0:T(8,128)(2,1)S(1)} collective-permute-done((bf16[72,512]{1,0:T(8,128)(2,1)S(1)}, bf16[72,512]{1,0:T(8,128)(2,1)S(1)}, u32[]{:S(2)}, u32[]{:S(2)}) %collective-permute-start.15) | collective-permute-done | bytes 73760 | tf_op jit(solution)/shard_map/ppermute | solution.py:422
  78.5 2.6 %collective-permute-done.14.refs_2_ = bf16[72,512]{1,0:T(8,128)(2,1)S(1)} collective-permute-done((bf16[72,512]{1,0:T(8,128)(2,1)S(1)}, bf16[72,512]{1,0:T(8,128)(2,1)S(1)}, u32[]{:S(2)}, u32[]{:S(2)}) %collective-permute-start.14) | collective-permute-done | bytes 73760 | tf_op jit(solution)/shard_map/ppermute | solution.py:422
  85.3 3.5 %collective-permute-start.19 = (bf16[72,512]{1,0:T(8,128)(2,1)S(1)}, bf16[72,512]{1,0:T(8,128)(2,1)S(1)}, u32[]{:S(2)}, u32[]{:S(2)}) collective-permute-start(bf16[72,512]{1,0:T(8,128)(2,1)S(1)} %shard_map.180.refs_0_), channel_id=1, source_target_pairs={{0,6},{1,7},{2,0},{3,1},{4,2},{5,3},{6,4},{7,5},{8,14},{9,15},{10,... | collective-permute-start | bytes 221192 | tf_op jit(solution)/shard_map/ppermute | solution.py:432
  89.0 2.7 %collective-permute-start.20 = (bf16[72,512]{1,0:T(8,128)(2,1)S(1)}, bf16[72,512]{1,0:T(8,128)(2,1)S(1)}, u32[]{:S(2)}, u32[]{:S(2)}) collective-permute-start(bf16[72,512]{1,0:T(8,128)(2,1)S(1)} %collective-permute-done.17.refs_2_), channel_id=1, source_target_pairs={{0,2},{1,3},{2,4},{3,5},{4,6},{5,7},{6,0},{7,1},{8,10},{9,11},{10,... | collective-permute-start | bytes 221192 | tf_op jit(solution)/shard_map/ppermute | solution.py:433
  91.7 2.0 %collective-permute-done.16.refs_1_ = bf16[72,512]{1,0:T(8,128)(2,1)S(1)} collective-permute-done((bf16[72,512]{1,0:T(8,128)(2,1)S(1)}, bf16[72,512]{1,0:T(8,128)(2,1)S(1)}, u32[]{:S(2)}, u32[]{:S(2)}) %collective-permute-start.16) | collective-permute-done | bytes 73760 | tf_op jit(solution)/shard_map/ppermute | solution.py:432
  95.9 4.3 %collective-permute-done.22.refs_7_ = bf16[72,512]{1,0:T(8,128)(2,1)S(1)} collective-permute-done((bf16[72,512]{1,0:T(8,128)(2,1)S(1)}, bf16[72,512]{1,0:T(8,128)(2,1)S(1)}, u32[]{:S(2)}, u32[]{:S(2)}) %collective-permute-start.22) | collective-permute-done | bytes 73760 | tf_op jit(solution)/shard_map/ppermute | solution.py:433
  100.6 1.9 %collective-permute-done.23.refs_5_ = bf16[520,512]{1,0:T(8,128)(2,1)S(1)} collective-permute-done((bf16[520,512]{1,0:T(8,128)(2,1)S(1)}, bf16[520,512]{1,0:T(8,128)(2,1)S(1)}, u32[]{:S(2)}, u32[]{:S(2)}) %collective-permute-start.23) | collective-permute-done | bytes 532512 | tf_op jit(solution)/shard_map/ppermute | solution.py:572
  106.3 3.0 %collective-permute-done.24.b1 = bf16[64,640]{1,0:T(8,128)(2,1)S(1)} collective-permute-done((bf16[64,640]{1,0:T(8,128)(2,1)S(1)}, bf16[64,640]{1,0:T(8,128)(2,1)S(1)}, u32[]{:S(2)}, u32[]{:S(2)}) %collective-permute-start.24) | collective-permute-done | bytes 81952 | tf_op jit(solution)/shard_map/ppermute | solution.py:422
  109.3 2.8 %collective-permute-done.25.b2 = bf16[64,640]{1,0:T(8,128)(2,1)S(1)} collective-permute-done((bf16[64,640]{1,0:T(8,128)(2,1)S(1)}, bf16[64,640]{1,0:T(8,128)(2,1)S(1)}, u32[]{:S(2)}, u32[]{:S(2)}) %collective-permute-start.25) | collective-permute-done | bytes 81952 | tf_op jit(solution)/shard_map/ppermute | solution.py:422
  (93 shorter events, 26.2 us)
Async XLA Ops:
  0.0 6.1 %collective-permute-start.2 = (bf16[64,512]{1,0:T(8,128)(2,1)}, bf16[64,512]{1,0:T(8,128)(2,1)S(1)}, u32[]{:S(2)}, u32[]{:S(2)}) collective-permute-start(bf16[64,512]{1,0:T(8,128)(2,1)} %bitcast.9), channel_id=1, source_target_pairs={{0,192},{64,0},{128,64},{192,128},{1,193},{65,1},{129,65},{193,129... | collective-permute-start | bytes 196616 | tf_op jit(solution)/shard_map/ppermute | solution.py:422
  0.8 6.0 %collective-permute-start.1 = (bf16[64,512]{1,0:T(8,128)(2,1)}, bf16[64,512]{1,0:T(8,128)(2,1)S(1)}, u32[]{:S(2)}, u32[]{:S(2)}) collective-permute-start(bf16[64,512]{1,0:T(8,128)(2,1)} %bitcast.10), channel_id=1, source_target_pairs={{0,128},{64,192},{128,0},{192,64},{1,129},{65,193},{129,1},{193,65... | collective-permute-start | bytes 196616 | tf_op jit(solution)/shard_map/ppermute | solution.py:422
  9.4 13.0 %collective-permute-start.3 = (bf16[4,16,512]{2,1,0:T(8,128)(2,1)S(1)}, bf16[4,16,512]{2,1,0:T(8,128)(2,1)S(1)}, u32[]{:S(2)}, u32[]{:S(2)}) collective-permute-start(bf16[4,16,512]{2,1,0:T(8,128)(2,1)S(1)} %get-tuple-element.22), channel_id=1, source_target_pairs={{0,8},{8,16},{16,24},{24,32},{32,40},{40,48},{48,56},{56,0},{1,9},... | collective-permute-start | bytes 196616 | tf_op jit(solution)/shard_map/ppermute | solution.py:439
  9.4 13.0 %collective-permute-start.4 = (bf16[4,16,512]{2,1,0:T(8,128)(2,1)S(1)}, bf16[4,16,512]{2,1,0:T(8,128)(2,1)S(1)}, u32[]{:S(2)}, u32[]{:S(2)}) collective-permute-start(bf16[4,16,512]{2,1,0:T(8,128)(2,1)S(1)} %get-tuple-element.23), channel_id=1, source_target_pairs={{0,56},{8,0},{16,8},{24,16},{32,24},{40,32},{48,40},{56,48},{1,57}... | collective-permute-start | bytes 196616 | tf_op jit(solution)/shard_map/ppermute | solution.py:439
  12.4 19.5 %all-to-all-start = ((f32[64,1,128]{2,1,0:T(1,128)}), f32[64,1,128]{2,1,0:T(1,128)S(1)}, u32[]{:S(2)}, u32[]{:S(2)}) async-start(f32[64,1,128]{2,1,0:T(1,128)} %get-tuple-element.26), calls=%async_computation | async-start | bytes 65536 | tf_op jit(solution)/shard_map/all_to_all | solution.py:443
  22.6 9.3 %collective-permute-start.5 = (bf16[4,24,512]{2,1,0:T(8,128)(2,1)S(1)}, bf16[4,24,512]{2,1,0:T(8,128)(2,1)S(1)}, u32[]{:S(2)}, u32[]{:S(2)}) collective-permute-start(bf16[4,24,512]{2,1,0:T(8,128)(2,1)S(1)} %get-tuple-element.24), channel_id=1, source_target_pairs={{0,1},{1,2},{2,3},{3,4},{4,5},{5,6},{6,7},{7,0},{8,9},{9,10},{10,1... | collective-permute-start | bytes 294920 | tf_op jit(solution)/shard_map/ppermute | solution.py:439
  24.2 7.7 %collective-permute-start.6 = (bf16[4,24,512]{2,1,0:T(8,128)(2,1)S(1)}, bf16[4,24,512]{2,1,0:T(8,128)(2,1)S(1)}, u32[]{:S(2)}, u32[]{:S(2)}) collective-permute-start(bf16[4,24,512]{2,1,0:T(8,128)(2,1)S(1)} %get-tuple-element.25), channel_id=1, source_target_pairs={{0,7},{1,0},{2,1},{3,2},{4,3},{5,4},{6,5},{7,6},{8,15},{9,8},{10,9... | collective-permute-start | bytes 294920 | tf_op jit(solution)/shard_map/ppermute | solution.py:439
  54.3 6.6 %collective-permute-start.9 = (bf16[4,104,128]{2,1,0:T(8,128)(2,1)S(1)}, bf16[4,104,128]{2,1,0:T(8,128)(2,1)S(1)}, u32[]{:S(2)}, u32[]{:S(2)}) collective-permute-start(bf16[4,104,128]{2,1,0:T(8,128)(2,1)S(1)} %shard_map.177.s0), channel_id=1, source_target_pairs={{0,192},{64,0},{128,64},{192,128},{1,193},{65,1},{129,65},{193,129... | collective-permute-start | bytes 319496 | tf_op jit(solution)/shard_map/ppermute | solution.py:422
  55.7 7.6 %collective-permute-start.8 = (bf16[4,104,128]{2,1,0:T(8,128)(2,1)S(1)}, bf16[4,104,128]{2,1,0:T(8,128)(2,1)S(1)}, u32[]{:S(2)}, u32[]{:S(2)}) collective-permute-start(bf16[4,104,128]{2,1,0:T(8,128)(2,1)S(1)} %shard_map.177.s0), channel_id=1, source_target_pairs={{0,128},{64,192},{128,0},{192,64},{1,129},{65,193},{129,1},{193,65... | collective-permute-start | bytes 319496 | tf_op jit(solution)/shard_map/ppermute | solution.py:422
  58.5 4.9 %collective-permute-start.7 = (bf16[4,104,128]{2,1,0:T(8,128)(2,1)S(1)}, bf16[4,104,128]{2,1,0:T(8,128)(2,1)S(1)}, u32[]{:S(2)}, u32[]{:S(2)}) collective-permute-start(bf16[4,104,128]{2,1,0:T(8,128)(2,1)S(1)} %shard_map.177.s0), channel_id=1, source_target_pairs={{0,64},{64,128},{128,192},{192,0},{1,65},{65,129},{129,193},{193,1... | collective-permute-start | bytes 319496 | tf_op jit(solution)/shard_map/ppermute | solution.py:422
  68.6 5.3 %collective-permute-start.11 = (bf16[72,128]{1,0:T(8,128)(2,1)S(1)}, bf16[72,128]{1,0:T(8,128)(2,1)S(1)}, u32[]{:S(2)}, u32[]{:S(2)}) collective-permute-start(bf16[72,128]{1,0:T(8,128)(2,1)S(1)} %get-tuple-element.33), channel_id=1, source_target_pairs={{0,128},{64,192},{128,0},{192,64},{1,129},{65,193},{129,1},{193,65... | collective-permute-start | bytes 55304 | tf_op jit(solution)/shard_map/ppermute | solution.py:422
  69.1 5.0 %collective-permute-start.12 = (bf16[72,128]{1,0:T(8,128)(2,1)S(1)}, bf16[72,128]{1,0:T(8,128)(2,1)S(1)}, u32[]{:S(2)}, u32[]{:S(2)}) collective-permute-start(bf16[72,128]{1,0:T(8,128)(2,1)S(1)} %get-tuple-element.34), channel_id=1, source_target_pairs={{0,192},{64,0},{128,64},{192,128},{1,193},{65,1},{129,65},{193,129... | collective-permute-start | bytes 55304 | tf_op jit(solution)/shard_map/ppermute | solution.py:422
  75.3 5.9 %collective-permute-start.14 = (bf16[72,512]{1,0:T(8,128)(2,1)S(1)}, bf16[72,512]{1,0:T(8,128)(2,1)S(1)}, u32[]{:S(2)}, u32[]{:S(2)}) collective-permute-start(bf16[72,512]{1,0:T(8,128)(2,1)S(1)} %shard_map.179.refs_0_.residual_ref), channel_id=1, source_target_pairs={{0,32},{16,48},{32,0},{48,16},{1,33},{17,49},{33,1},{49,17},{2,34}... | collective-permute-start | bytes 221192 | tf_op jit(solution)/shard_map/ppermute | solution.py:422
  76.9 5.6 %collective-permute-start.13 = (bf16[72,512]{1,0:T(8,128)(2,1)S(1)}, bf16[72,512]{1,0:T(8,128)(2,1)S(1)}, u32[]{:S(2)}, u32[]{:S(2)}) collective-permute-start(bf16[72,512]{1,0:T(8,128)(2,1)S(1)} %shard_map.179.refs_0_.residual_ref), channel_id=1, source_target_pairs={{0,16},{16,32},{32,48},{48,0},{1,17},{17,33},{33,49},{49,1},{2,18}... | collective-permute-start | bytes 221192 | tf_op jit(solution)/shard_map/ppermute | solution.py:422
  82.5 6.2 %collective-permute-start.18 = (bf16[72,512]{1,0:T(8,128)(2,1)S(1)}, bf16[72,512]{1,0:T(8,128)(2,1)S(1)}, u32[]{:S(2)}, u32[]{:S(2)}) collective-permute-start(bf16[72,512]{1,0:T(8,128)(2,1)S(1)} %shard_map.180.refs_0_), channel_id=1, source_target_pairs={{0,7},{1,0},{2,1},{3,2},{4,3},{5,4},{6,5},{7,6},{8,15},{9,8},{10,9... | collective-permute-start | bytes 221192 | tf_op jit(solution)/shard_map/ppermute | solution.py:432
  83.4 5.6 %collective-permute-start.17 = (bf16[72,512]{1,0:T(8,128)(2,1)S(1)}, bf16[72,512]{1,0:T(8,128)(2,1)S(1)}, u32[]{:S(2)}, u32[]{:S(2)}) collective-permute-start(bf16[72,512]{1,0:T(8,128)(2,1)S(1)} %shard_map.180.refs_0_), channel_id=1, source_target_pairs={{0,1},{1,2},{2,3},{3,4},{4,5},{5,6},{6,7},{7,0},{8,9},{9,10},{10,1... | collective-permute-start | bytes 221192 | tf_op jit(solution)/shard_map/ppermute | solution.py:432
  84.7 9.1 %collective-permute-start.16 = (bf16[72,512]{1,0:T(8,128)(2,1)S(1)}, bf16[72,512]{1,0:T(8,128)(2,1)S(1)}, u32[]{:S(2)}, u32[]{:S(2)}) collective-permute-start(bf16[72,512]{1,0:T(8,128)(2,1)S(1)} %shard_map.180.refs_0_), channel_id=1, source_target_pairs={{0,2},{1,3},{2,4},{3,5},{4,6},{5,7},{6,0},{7,1},{8,10},{9,11},{10,... | collective-permute-start | bytes 221192 | tf_op jit(solution)/shard_map/ppermute | solution.py:432
  85.3 8.4 %collective-permute-start.19 = (bf16[72,512]{1,0:T(8,128)(2,1)S(1)}, bf16[72,512]{1,0:T(8,128)(2,1)S(1)}, u32[]{:S(2)}, u32[]{:S(2)}) collective-permute-start(bf16[72,512]{1,0:T(8,128)(2,1)S(1)} %shard_map.180.refs_0_), channel_id=1, source_target_pairs={{0,6},{1,7},{2,0},{3,1},{4,2},{5,3},{6,4},{7,5},{8,14},{9,15},{10,... | collective-permute-start | bytes 221192 | tf_op jit(solution)/shard_map/ppermute | solution.py:432
  88.8 6.1 %collective-permute-start.21 = (bf16[72,512]{1,0:T(8,128)(2,1)S(1)}, bf16[72,512]{1,0:T(8,128)(2,1)S(1)}, u32[]{:S(2)}, u32[]{:S(2)}) collective-permute-start(bf16[72,512]{1,0:T(8,128)(2,1)S(1)} %collective-permute-done.18.refs_3_), channel_id=1, source_target_pairs={{0,6},{1,7},{2,0},{3,1},{4,2},{5,3},{6,4},{7,5},{8,14},{9,15},{10,... | collective-permute-start | bytes 221192 | tf_op jit(solution)/shard_map/ppermute | solution.py:433
  89.0 6.9 %collective-permute-start.20 = (bf16[72,512]{1,0:T(8,128)(2,1)S(1)}, bf16[72,512]{1,0:T(8,128)(2,1)S(1)}, u32[]{:S(2)}, u32[]{:S(2)}) collective-permute-start(bf16[72,512]{1,0:T(8,128)(2,1)S(1)} %collective-permute-done.17.refs_2_), channel_id=1, source_target_pairs={{0,2},{1,3},{2,4},{3,5},{4,6},{5,7},{6,0},{7,1},{8,10},{9,11},{10,... | collective-permute-start | bytes 221192 | tf_op jit(solution)/shard_map/ppermute | solution.py:433
  93.8 6.5 %collective-permute-start.22 = (bf16[72,512]{1,0:T(8,128)(2,1)S(1)}, bf16[72,512]{1,0:T(8,128)(2,1)S(1)}, u32[]{:S(2)}, u32[]{:S(2)}) collective-permute-start(bf16[72,512]{1,0:T(8,128)(2,1)S(1)} %collective-permute-done.16.refs_1_), channel_id=1, source_target_pairs={{0,2},{1,3},{2,4},{3,5},{4,6},{5,7},{6,0},{7,1},{8,10},{9,11},{10,... | collective-permute-start | bytes 221192 | tf_op jit(solution)/shard_map/ppermute | solution.py:433
  104.0 5.4 %collective-permute-start.24 = (bf16[64,640]{1,0:T(8,128)(2,1)S(1)}, bf16[64,640]{1,0:T(8,128)(2,1)S(1)}, u32[]{:S(2)}, u32[]{:S(2)}) collective-permute-start(bf16[64,640]{1,0:T(8,128)(2,1)S(1)} %get-tuple-element.36), channel_id=1, source_target_pairs={{0,48},{16,0},{32,16},{48,32},{1,49},{17,1},{33,17},{49,33},{2,50}... | collective-permute-start | bytes 245768 | tf_op jit(solution)/shard_map/ppermute | solution.py:422
  105.4 6.8 %collective-permute-start.25 = (bf16[64,640]{1,0:T(8,128)(2,1)S(1)}, bf16[64,640]{1,0:T(8,128)(2,1)S(1)}, u32[]{:S(2)}, u32[]{:S(2)}) collective-permute-start(bf16[64,640]{1,0:T(8,128)(2,1)S(1)} %get-tuple-element.37), channel_id=1, source_target_pairs={{0,32},{16,48},{32,0},{48,16},{1,33},{17,49},{33,1},{49,17},{2,34}... | collective-permute-start | bytes 245768 | tf_op jit(solution)/shard_map/ppermute | solution.py:422
  106.1 6.8 %collective-permute-start.26 = (bf16[64,640]{1,0:T(8,128)(2,1)S(1)}, bf16[64,640]{1,0:T(8,128)(2,1)S(1)}, u32[]{:S(2)}, u32[]{:S(2)}) collective-permute-start(bf16[64,640]{1,0:T(8,128)(2,1)S(1)} %get-tuple-element.38), channel_id=1, source_target_pairs={{0,16},{16,32},{32,48},{48,0},{1,17},{17,33},{33,49},{49,1},{2,18}... | collective-permute-start | bytes 245768 | tf_op jit(solution)/shard_map/ppermute | solution.py:422
  (22 other events, 233.7 us)

commit v2 on v1

--- a/solution.py
+++ b/solution.py
@@ -14,6 +14,7 @@
 F32 = jnp.float32
 LANES = 128
 LIMIT = 32 * 1024 * 1024
+PAIRS = ((0, 1), (2, 3), (4, 5), (6, 7), (8,))
 VMEM = pl.BlockSpec(memory_space=pltpu.VMEM)
 
 
@@ -196,7 +197,7 @@
 
 
 def convolve(lhs, weights, product, frame_rows, pitch, out_rows):
-    for pair in ((0, 1), (2, 3), (4, 5), (6, 7), (8,)):
+    for pair in PAIRS:
         rhs = jnp.concatenate(
             [jnp.concatenate([weights[9 * d + s] for s in pair], axis=1) for d in range(3)], axis=0
         )
@@ -204,6 +205,10 @@
         product[0 : 4 * frame_rows, lane : lane + rhs.shape[1]] = jnp.dot(
             lhs[...], rhs, preferred_element_type=F32
         )
+    return shifted_sums(product, frame_rows, pitch, out_rows)
+
+
+def shifted_sums(product, frame_rows, pitch, out_rows):
     totals = []
     for f in range(4):
         total = None
@@ -295,11 +300,41 @@
     encode(moments_ref, [(0,) + group_stats(mean, spread)])
 
 
+def add_blocks(refs, shifts, kernel_ref, lhs, product, before=None):
+    ta = lax.axis_index("ta")
+    for k, ref in enumerate(refs):
+        for f in range(4):
+            for d in range(3):
+                lane = (len(refs) * d + k) * LANES
+                lhs[f * 112 : f * 112 + 104, lane : lane + LANES] = ref[max(f + d - 2, 0)]
+    for pair in PAIRS:
+        rhs = jnp.concatenate(
+            [
+                jnp.concatenate(
+                    [
+                        kernel_ref[9 * d + s, pl.ds(pl.multiple_of(turned(ta, shift) * LANES, LANES), LANES), :]
+                        for s in pair
+                    ],
+                    axis=1,
+                )
+                for d in range(3)
+                for shift in shifts
+            ],
+            axis=0,
+        )
+        lanes = slice(pair[0] * LANES, pair[0] * LANES + rhs.shape[1])
+        part = jnp.dot(lhs[...], rhs, preferred_element_type=F32)
+        product[:, lanes] = part if before is None else before[:, lanes] + part
+
+
+def second_conv_first_kernel(s0, s3, kernel_ref, out_ref, lhs):
+    add_blocks((s0, s3), (0, 3), kernel_ref, lhs, out_ref)
+
+
 def second_conv_kernel(
-    s0,
     s1,
     s2,
-    s3,
+    before_ref,
     small_ref,
     own_ref,
     kernel_ref,
@@ -313,13 +348,8 @@
     parts,
 ):
     ta = lax.axis_index("ta")
-    for s, ref in enumerate((s0, s1, s2, s3)):
-        block = turned(ta, s)
-        for f in range(4):
-            for d in range(3):
-                lane = pl.multiple_of((4 * d + block) * LANES, LANES)
-                lhs[f * 112 : f * 112 + 104, pl.ds(lane, LANES)] = ref[max(f + d - 2, 0)]
-    totals = convolve(lhs, kernel_ref, product, 112, 10, 80)
+    add_blocks((s1, s2), (1, 2), kernel_ref, lhs, product, before_ref)
+    totals = shifted_sums(product, 112, 10, 80)
     bias = small_ref[37:38, :]
     tiles = []
     for f in range(4):
@@ -533,18 +563,31 @@
         over_tiles(rows2),
         small,
     )
+    blocks = around(act, "ta")
+    before = call(
+        second_conv_first_kernel,
+        jax.ShapeDtypeStruct((448, 1152), F32),
+        [VMEM] * 3,
+        [pltpu.VMEM((448, 768), BF)],
+        10**9,
+        blocks[0],
+        blocks[3],
+        conv2_kernel,
+    )
     parts = call(
         second_conv_kernel,
         (bf(cells + 8, LANES),) * 4,
-        [VMEM] * 7,
+        [VMEM] * 6,
         [
-            pltpu.VMEM((448, 1536), BF),
+            pltpu.VMEM((448, 768), BF),
             pltpu.VMEM((448, 1152), F32),
             pltpu.VMEM((4, 80, LANES), F32),
             pltpu.VMEM((4, cells, LANES), BF),
         ],
         2 * 10**9,
-        *around(act, "ta"),
+        blocks[1],
+        blocks[2],
+        before,
         small,
         own,
         conv2_kernel,

time: 115 us -> 116 us (level)
  starting transfers between devices: 42.4 us -> 45.5 us
  waiting for transfers between devices: 40.4 us -> 37.6 us
    ppermute x4, waiting for transfers between devices: 2.23 us -> 0.01 us  [relayed(): lax.ppermute(block, axis, ring(count, step))]
    ppermute x3, starting transfers between devices: 2.74 us -> 4.14 us  [relayed(): lax.ppermute(after[step], axis, ring(count, move))]
    ppermute x4, starting transfers between devices: 6.24 us -> 7.45 us  [relayed(): lax.ppermute(block, axis, ring(count, step))]
    pallas_call x12 -> x13, Pallas kernels: 11.4 us -> 11.5 us  [call(): pl.pallas_call(kernel, out_shape=out_shape, in_specs=specs, out_specs=tup...]
  transfers between devices with their start and end apart: 28 -> 28, of which waited for: 22 -> 18; matrix products, arithmetic and copies ran while one was open for 0% -> 0% of each run, Pallas kernels for 0% -> 1%
where the time goes in v2:
time: 116 us; the launch traced here: 114 us
  starting transfers between devices  45.5 us (39%)
  waiting for transfers between devices  37.6 us (32%)
  blocking collectives  16.8 us (14%)
  Pallas kernels  11.5 us (10%)
  local copies, waits for them, and re-layouts  2.64 us (2%)
    ppermute x15, waiting for transfers between devices, spread_out(): arrived[s] = lax.ppermute(blocks[s], axis, ring(count, sign * s))  23.2 us
    all_to_all x1, blocking collectives, over_tiles(): lax.all_to_all(rows, HA + ('z',), split_axis=0, concat_axis=0, tiled=True)  16.8 us
    ppermute x15, starting transfers between devices, spread_out(): arrived[s] = lax.ppermute(blocks[s], axis, ring(count, sign * s))  16.8 us
    pallas_call x13, Pallas kernels, call(): pl.pallas_call(kernel, out_shape=out_shape, in_specs=specs, out_specs=tup...  11.5 us
    all_to_all x1, starting transfers between devices, over_tiles(): lax.all_to_all(rows, HA + ('z',), split_axis=0, concat_axis=0, tiled=True)  10.6 us
    ppermute x4, starting transfers between devices, relayed(): lax.ppermute(block, axis, ring(count, step))  7.45 us
    ppermute x3, waiting for transfers between devices, relayed(): lax.ppermute(after[step], axis, ring(count, move))  6.45 us
    all_to_all x1, waiting for transfers between devices, over_tiles(): lax.all_to_all(rows, HA + ('z',), split_axis=0, concat_axis=0, tiled=True)  6.01 us
  transfers between devices with their start and end apart: 28, of which 18 were waited for; matrix products, arithmetic and copies ran while one was open for 0% of the time, Pallas kernels for 1%

profile of v2, /device:TPU:6, one launch (start us, length us, event | category | flops | bytes accessed | tf_op | source)
XLA Modules:
  0.0 114.4 jit_solution(5867277108727959790)
XLA Ops:
  0.0 2.2 %collective-permute-start = (bf16[64,512]{1,0:T(8,128)(2,1)}, bf16[64,512]{1,0:T(8,128)(2,1)S(1)}, u32[]{:S(2)}, u32[]{:S(2)}) collective-permute-start(bf16[64,512]{1,0:T(8,128)(2,1)} %bitcast.9), channel_id=1, source_target_pairs={{0,64},{64,128},{128,192},{192,0},{1,65},{65,129},{129,193},{193,1... | collective-permute-start | bytes 196616 | tf_op jit(solution)/shard_map/ppermute | solution.py:452
  5.1 3.2 %collective-permute-done.1.s2 = bf16[64,512]{1,0:T(8,128)(2,1)S(1)} collective-permute-done((bf16[64,512]{1,0:T(8,128)(2,1)}, bf16[64,512]{1,0:T(8,128)(2,1)S(1)}, u32[]{:S(2)}, u32[]{:S(2)}) %collective-permute-start.1) | collective-permute-done | bytes 65568 | tf_op jit(solution)/shard_map/ppermute | solution.py:452
  10.2 3.0 %collective-permute-start.4 = (bf16[4,16,512]{2,1,0:T(8,128)(2,1)S(1)}, bf16[4,16,512]{2,1,0:T(8,128)(2,1)S(1)}, u32[]{:S(2)}, u32[]{:S(2)}) collective-permute-start(bf16[4,16,512]{2,1,0:T(8,128)(2,1)S(1)} %get-tuple-element.23), channel_id=1, source_target_pairs={{0,56},{8,0},{16,8},{24,16},{32,24},{40,32},{48,40},{56,48},{1,57}... | collective-permute-start | bytes 196616 | tf_op jit(solution)/shard_map/ppermute | solution.py:469
  13.1 10.6 %all-to-all-start = ((f32[64,1,128]{2,1,0:T(1,128)}), f32[64,1,128]{2,1,0:T(1,128)S(1)}, u32[]{:S(2)}, u32[]{:S(2)}) async-start(f32[64,1,128]{2,1,0:T(1,128)} %get-tuple-element.26), calls=%async_computation | async-start | bytes 65536 | tf_op jit(solution)/shard_map/all_to_all | solution.py:473
  23.9 1.6 %collective-permute-start.5 = (bf16[4,24,512]{2,1,0:T(8,128)(2,1)S(1)}, bf16[4,24,512]{2,1,0:T(8,128)(2,1)S(1)}, u32[]{:S(2)}, u32[]{:S(2)}) collective-permute-start(bf16[4,24,512]{2,1,0:T(8,128)(2,1)S(1)} %get-tuple-element.24), channel_id=1, source_target_pairs={{0,1},{1,2},{2,3},{3,4},{4,5},{5,6},{6,7},{7,0},{8,9},{9,10},{10,1... | collective-permute-start | bytes 294920 | tf_op jit(solution)/shard_map/ppermute | solution.py:469
  25.6 1.7 %collective-permute-start.6 = (bf16[4,24,512]{2,1,0:T(8,128)(2,1)S(1)}, bf16[4,24,512]{2,1,0:T(8,128)(2,1)S(1)}, u32[]{:S(2)}, u32[]{:S(2)}) collective-permute-start(bf16[4,24,512]{2,1,0:T(8,128)(2,1)S(1)} %get-tuple-element.25), channel_id=1, source_target_pairs={{0,7},{1,0},{2,1},{3,2},{4,3},{5,4},{6,5},{7,6},{8,15},{9,8},{10,9... | collective-permute-start | bytes 294920 | tf_op jit(solution)/shard_map/ppermute | solution.py:469
  27.2 6.0 %all-to-all-done.rows_ref = f32[64,1,128]{2,1,0:T(1,128)S(1)} async-done(((f32[64,1,128]{2,1,0:T(1,128)}), f32[64,1,128]{2,1,0:T(1,128)S(1)}, u32[]{:S(2)}, u32[]{:S(2)}) %all-to-all-start) | async-done | bytes 32800 | tf_op jit(solution)/shard_map/all_to_all | solution.py:473
  35.3 3.2 %shard_map.176 = (bf16[4,104,128]{2,1,0:T(8,128)(2,1)S(1)}, f32[64,1,128]{2,1,0:T(1,128)S(1)}) custom-call(bf16[576,1536]{1,0:T(8,128)(2,1)S(1)} %get-tuple-element.27.lhs, f32[38,128]{1,0:T(8,128)S(1)} %bitcast.4, bf16[27,512,128]{2,1,0:T(8,128)(2,1)S(1)} %copy-done.3), custom_call_target="tpu_custom_call" | custom-call | flops 2000000000 | bytes 5467136 | tf_op jit(solution)/shard_map/pallas_call | solution.py:429
  38.4 16.8 %all_to_all.10.rows_ref = f32[64,1,128]{2,1,0:T(1,128)S(1)} all-to-all(f32[64,1,128]{2,1,0:T(1,128)S(1)} %get-tuple-element.29), channel_id=1, replica_groups=mesh['ta'=4,'y'=4,'core'=2,'z'=8] {'y','core','z'}, dimensions={0} | all-to-all | bytes 65536 | tf_op jit(solution)/shard_map/all_to_all | solution.py:473
  55.7 3.2 %collective-permute-start.7 = (bf16[4,104,128]{2,1,0:T(8,128)(2,1)S(1)}, bf16[4,104,128]{2,1,0:T(8,128)(2,1)S(1)}, u32[]{:S(2)}, u32[]{:S(2)}) collective-permute-start(bf16[4,104,128]{2,1,0:T(8,128)(2,1)S(1)} %shard_map.177.s0), channel_id=1, source_target_pairs={{0,64},{64,128},{128,192},{192,0},{1,65},{65,129},{129,193},{193,1... | collective-permute-start | bytes 319496 | tf_op jit(solution)/shard_map/ppermute | solution.py:452
  59.0 2.7 %collective-permute-done.9.s3 = bf16[4,104,128]{2,1,0:T(8,128)(2,1)S(1)} collective-permute-done((bf16[4,104,128]{2,1,0:T(8,128)(2,1)S(1)}, bf16[4,104,128]{2,1,0:T(8,128)(2,1)S(1)}, u32[]{:S(2)}, u32[]{:S(2)}) %collective-permute-start.9) | collective-permute-done | bytes 106528 | tf_op jit(solution)/shard_map/ppermute | solution.py:452
  63.1 2.1 %collective-permute-done.8.s2 = bf16[4,104,128]{2,1,0:T(8,128)(2,1)S(1)} collective-permute-done((bf16[4,104,128]{2,1,0:T(8,128)(2,1)S(1)}, bf16[4,104,128]{2,1,0:T(8,128)(2,1)S(1)}, u32[]{:S(2)}, u32[]{:S(2)}) %collective-permute-start.8) | collective-permute-done | bytes 106528 | tf_op jit(solution)/shard_map/ppermute | solution.py:452
  65.2 1.8 %shard_map.179 = (bf16[72,128]{1,0:T(8,128)(2,1)S(1)}, bf16[72,128]{1,0:T(8,128)(2,1)S(1)}, bf16[72,128]{1,0:T(8,128)(2,1)S(1)}, bf16[72,128]{1,0:T(8,128)(2,1)S(1)}) custom-call(bf16[4,104,128]{2,1,0:T(8,128)(2,1)S(1)} %collective-permute-done.7.s1, bf16[4,104,128]{2,1,0:T(8,128)(2,1)S(1)} %collective-permute-done.8.s2, ...), custom_call_target="tpu_custom_call" | custom-call | flops 2000000000 | bytes 5975040 | tf_op jit(solution)/shard_map/pallas_call | solution.py:429
  70.8 3.1 %collective-permute-done.11.s2 = bf16[72,128]{1,0:T(8,128)(2,1)S(1)} collective-permute-done((bf16[72,128]{1,0:T(8,128)(2,1)S(1)}, bf16[72,128]{1,0:T(8,128)(2,1)S(1)}, u32[]{:S(2)}, u32[]{:S(2)}) %collective-permute-start.11) | collective-permute-done | bytes 18464 | tf_op jit(solution)/shard_map/ppermute | solution.py:452
  74.7 1.9 %collective-permute-start.14 = (bf16[72,512]{1,0:T(8,128)(2,1)S(1)}, bf16[72,512]{1,0:T(8,128)(2,1)S(1)}, u32[]{:S(2)}, u32[]{:S(2)}) collective-permute-start(bf16[72,512]{1,0:T(8,128)(2,1)S(1)} %shard_map.180.refs_0_.residual_ref), channel_id=1, source_target_pairs={{0,32},{16,48},{32,0},{48,16},{1,33},{17,49},{33,1},{49,17},{2,34}... | collective-permute-start | bytes 221192 | tf_op jit(solution)/shard_map/ppermute | solution.py:452
  82.0 2.6 %collective-permute-start.18 = (bf16[72,512]{1,0:T(8,128)(2,1)S(1)}, bf16[72,512]{1,0:T(8,128)(2,1)S(1)}, u32[]{:S(2)}, u32[]{:S(2)}) collective-permute-start(bf16[72,512]{1,0:T(8,128)(2,1)S(1)} %shard_map.181.refs_0_), channel_id=1, source_target_pairs={{0,7},{1,0},{2,1},{3,2},{4,3},{5,4},{6,5},{7,6},{8,15},{9,8},{10,9... | collective-permute-start | bytes 221192 | tf_op jit(solution)/shard_map/ppermute | solution.py:462
  84.6 4.1 %collective-permute-start.19 = (bf16[72,512]{1,0:T(8,128)(2,1)S(1)}, bf16[72,512]{1,0:T(8,128)(2,1)S(1)}, u32[]{:S(2)}, u32[]{:S(2)}) collective-permute-start(bf16[72,512]{1,0:T(8,128)(2,1)S(1)} %shard_map.181.refs_0_), channel_id=1, source_target_pairs={{0,6},{1,7},{2,0},{3,1},{4,2},{5,3},{6,4},{7,5},{8,14},{9,15},{10,... | collective-permute-start | bytes 221192 | tf_op jit(solution)/shard_map/ppermute | solution.py:462
  88.7 4.1 %collective-permute-start.21 = (bf16[72,512]{1,0:T(8,128)(2,1)S(1)}, bf16[72,512]{1,0:T(8,128)(2,1)S(1)}, u32[]{:S(2)}, u32[]{:S(2)}) collective-permute-start(bf16[72,512]{1,0:T(8,128)(2,1)S(1)} %collective-permute-done.18.refs_3_), channel_id=1, source_target_pairs={{0,6},{1,7},{2,0},{3,1},{4,2},{5,3},{6,4},{7,5},{8,14},{9,15},{10,... | collective-permute-start | bytes 221192 | tf_op jit(solution)/shard_map/ppermute | solution.py:463
  92.9 2.3 %collective-permute-done.20.refs_5_ = bf16[72,512]{1,0:T(8,128)(2,1)S(1)} collective-permute-done((bf16[72,512]{1,0:T(8,128)(2,1)S(1)}, bf16[72,512]{1,0:T(8,128)(2,1)S(1)}, u32[]{:S(2)}, u32[]{:S(2)}) %collective-permute-start.20) | collective-permute-done | bytes 73760 | tf_op jit(solution)/shard_map/ppermute | solution.py:463
  95.2 4.1 %collective-permute-done.22.refs_7_ = bf16[72,512]{1,0:T(8,128)(2,1)S(1)} collective-permute-done((bf16[72,512]{1,0:T(8,128)(2,1)S(1)}, bf16[72,512]{1,0:T(8,128)(2,1)S(1)}, u32[]{:S(2)}, u32[]{:S(2)}) %collective-permute-start.22) | collective-permute-done | bytes 73760 | tf_op jit(solution)/shard_map/ppermute | solution.py:463
  99.8 1.9 %collective-permute-done.23.refs_5_ = bf16[520,512]{1,0:T(8,128)(2,1)S(1)} collective-permute-done((bf16[520,512]{1,0:T(8,128)(2,1)S(1)}, bf16[520,512]{1,0:T(8,128)(2,1)S(1)}, u32[]{:S(2)}, u32[]{:S(2)}) %collective-permute-start.23) | collective-permute-done | bytes 532512 | tf_op jit(solution)/shard_map/ppermute | solution.py:615
  103.1 2.7 %collective-permute-start.24 = (bf16[64,640]{1,0:T(8,128)(2,1)S(1)}, bf16[64,640]{1,0:T(8,128)(2,1)S(1)}, u32[]{:S(2)}, u32[]{:S(2)}) collective-permute-start(bf16[64,640]{1,0:T(8,128)(2,1)S(1)} %get-tuple-element.36), channel_id=1, source_target_pairs={{0,48},{16,0},{32,16},{48,32},{1,49},{17,1},{33,17},{49,33},{2,50}... | collective-permute-start | bytes 245768 | tf_op jit(solution)/shard_map/ppermute | solution.py:452
  106.8 2.8 %collective-permute-done.24.b1 = bf16[64,640]{1,0:T(8,128)(2,1)S(1)} collective-permute-done((bf16[64,640]{1,0:T(8,128)(2,1)S(1)}, bf16[64,640]{1,0:T(8,128)(2,1)S(1)}, u32[]{:S(2)}, u32[]{:S(2)}) %collective-permute-start.24) | collective-permute-done | bytes 81952 | tf_op jit(solution)/shard_map/ppermute | solution.py:452
  109.6 2.8 %collective-permute-done.25.b2 = bf16[64,640]{1,0:T(8,128)(2,1)S(1)} collective-permute-done((bf16[64,640]{1,0:T(8,128)(2,1)S(1)}, bf16[64,640]{1,0:T(8,128)(2,1)S(1)}, u32[]{:S(2)}, u32[]{:S(2)}) %collective-permute-start.25) | collective-permute-done | bytes 81952 | tf_op jit(solution)/shard_map/ppermute | solution.py:452
  (94 shorter events, 23.5 us)
Async XLA Ops:
  2.2 6.0 %collective-permute-start.1 = (bf16[64,512]{1,0:T(8,128)(2,1)}, bf16[64,512]{1,0:T(8,128)(2,1)S(1)}, u32[]{:S(2)}, u32[]{:S(2)}) collective-permute-start(bf16[64,512]{1,0:T(8,128)(2,1)} %bitcast.10), channel_id=1, source_target_pairs={{0,128},{64,192},{128,0},{192,64},{1,129},{65,193},{129,1},{193,65... | collective-permute-start | bytes 196616 | tf_op jit(solution)/shard_map/ppermute | solution.py:452
  2.9 6.0 %collective-permute-start.2 = (bf16[64,512]{1,0:T(8,128)(2,1)}, bf16[64,512]{1,0:T(8,128)(2,1)S(1)}, u32[]{:S(2)}, u32[]{:S(2)}) collective-permute-start(bf16[64,512]{1,0:T(8,128)(2,1)} %bitcast.11), channel_id=1, source_target_pairs={{0,192},{64,0},{128,64},{192,128},{1,193},{65,1},{129,65},{193,129... | collective-permute-start | bytes 196616 | tf_op jit(solution)/shard_map/ppermute | solution.py:452
  10.2 13.6 %collective-permute-start.3 = (bf16[4,16,512]{2,1,0:T(8,128)(2,1)S(1)}, bf16[4,16,512]{2,1,0:T(8,128)(2,1)S(1)}, u32[]{:S(2)}, u32[]{:S(2)}) collective-permute-start(bf16[4,16,512]{2,1,0:T(8,128)(2,1)S(1)} %get-tuple-element.22), channel_id=1, source_target_pairs={{0,8},{8,16},{16,24},{24,32},{32,40},{40,48},{48,56},{56,0},{1,9},... | collective-permute-start | bytes 196616 | tf_op jit(solution)/shard_map/ppermute | solution.py:469
  10.2 13.6 %collective-permute-start.4 = (bf16[4,16,512]{2,1,0:T(8,128)(2,1)S(1)}, bf16[4,16,512]{2,1,0:T(8,128)(2,1)S(1)}, u32[]{:S(2)}, u32[]{:S(2)}) collective-permute-start(bf16[4,16,512]{2,1,0:T(8,128)(2,1)S(1)} %get-tuple-element.23), channel_id=1, source_target_pairs={{0,56},{8,0},{16,8},{24,16},{32,24},{40,32},{48,40},{56,48},{1,57}... | collective-permute-start | bytes 196616 | tf_op jit(solution)/shard_map/ppermute | solution.py:469
  13.1 20.1 %all-to-all-start = ((f32[64,1,128]{2,1,0:T(1,128)}), f32[64,1,128]{2,1,0:T(1,128)S(1)}, u32[]{:S(2)}, u32[]{:S(2)}) async-start(f32[64,1,128]{2,1,0:T(1,128)} %get-tuple-element.26), calls=%async_computation | async-start | bytes 65536 | tf_op jit(solution)/shard_map/all_to_all | solution.py:473
  23.9 9.3 %collective-permute-start.5 = (bf16[4,24,512]{2,1,0:T(8,128)(2,1)S(1)}, bf16[4,24,512]{2,1,0:T(8,128)(2,1)S(1)}, u32[]{:S(2)}, u32[]{:S(2)}) collective-permute-start(bf16[4,24,512]{2,1,0:T(8,128)(2,1)S(1)} %get-tuple-element.24), channel_id=1, source_target_pairs={{0,1},{1,2},{2,3},{3,4},{4,5},{5,6},{6,7},{7,0},{8,9},{9,10},{10,1... | collective-permute-start | bytes 294920 | tf_op jit(solution)/shard_map/ppermute | solution.py:469
  25.6 7.7 %collective-permute-start.6 = (bf16[4,24,512]{2,1,0:T(8,128)(2,1)S(1)}, bf16[4,24,512]{2,1,0:T(8,128)(2,1)S(1)}, u32[]{:S(2)}, u32[]{:S(2)}) collective-permute-start(bf16[4,24,512]{2,1,0:T(8,128)(2,1)S(1)} %get-tuple-element.25), channel_id=1, source_target_pairs={{0,7},{1,0},{2,1},{3,2},{4,3},{5,4},{6,5},{7,6},{8,15},{9,8},{10,9... | collective-permute-start | bytes 294920 | tf_op jit(solution)/shard_map/ppermute | solution.py:469
  55.6 6.0 %collective-permute-start.9 = (bf16[4,104,128]{2,1,0:T(8,128)(2,1)S(1)}, bf16[4,104,128]{2,1,0:T(8,128)(2,1)S(1)}, u32[]{:S(2)}, u32[]{:S(2)}) collective-permute-start(bf16[4,104,128]{2,1,0:T(8,128)(2,1)S(1)} %shard_map.177.s0), channel_id=1, source_target_pairs={{0,192},{64,0},{128,64},{192,128},{1,193},{65,1},{129,65},{193,129... | collective-permute-start | bytes 319496 | tf_op jit(solution)/shard_map/ppermute | solution.py:452
  55.7 7.3 %collective-permute-start.7 = (bf16[4,104,128]{2,1,0:T(8,128)(2,1)S(1)}, bf16[4,104,128]{2,1,0:T(8,128)(2,1)S(1)}, u32[]{:S(2)}, u32[]{:S(2)}) collective-permute-start(bf16[4,104,128]{2,1,0:T(8,128)(2,1)S(1)} %shard_map.177.s0), channel_id=1, source_target_pairs={{0,64},{64,128},{128,192},{192,0},{1,65},{65,129},{129,193},{193,1... | collective-permute-start | bytes 319496 | tf_op jit(solution)/shard_map/ppermute | solution.py:452
  59.0 6.2 %collective-permute-start.8 = (bf16[4,104,128]{2,1,0:T(8,128)(2,1)S(1)}, bf16[4,104,128]{2,1,0:T(8,128)(2,1)S(1)}, u32[]{:S(2)}, u32[]{:S(2)}) collective-permute-start(bf16[4,104,128]{2,1,0:T(8,128)(2,1)S(1)} %shard_map.177.s0), channel_id=1, source_target_pairs={{0,128},{64,192},{128,0},{192,64},{1,129},{65,193},{129,1},{193,65... | collective-permute-start | bytes 319496 | tf_op jit(solution)/shard_map/ppermute | solution.py:452
  68.6 5.3 %collective-permute-start.11 = (bf16[72,128]{1,0:T(8,128)(2,1)S(1)}, bf16[72,128]{1,0:T(8,128)(2,1)S(1)}, u32[]{:S(2)}, u32[]{:S(2)}) collective-permute-start(bf16[72,128]{1,0:T(8,128)(2,1)S(1)} %get-tuple-element.33), channel_id=1, source_target_pairs={{0,128},{64,192},{128,0},{192,64},{1,129},{65,193},{129,1},{193,65... | collective-permute-start | bytes 55304 | tf_op jit(solution)/shard_map/ppermute | solution.py:452
  68.7 5.2 %collective-permute-start.12 = (bf16[72,128]{1,0:T(8,128)(2,1)S(1)}, bf16[72,128]{1,0:T(8,128)(2,1)S(1)}, u32[]{:S(2)}, u32[]{:S(2)}) collective-permute-start(bf16[72,128]{1,0:T(8,128)(2,1)S(1)} %get-tuple-element.34), channel_id=1, source_target_pairs={{0,192},{64,0},{128,64},{192,128},{1,193},{65,1},{129,65},{193,129... | collective-permute-start | bytes 55304 | tf_op jit(solution)/shard_map/ppermute | solution.py:452
  73.9 5.6 %collective-permute-start.13 = (bf16[72,512]{1,0:T(8,128)(2,1)S(1)}, bf16[72,512]{1,0:T(8,128)(2,1)S(1)}, u32[]{:S(2)}, u32[]{:S(2)}) collective-permute-start(bf16[72,512]{1,0:T(8,128)(2,1)S(1)} %shard_map.180.refs_0_.residual_ref), channel_id=1, source_target_pairs={{0,16},{16,32},{32,48},{48,0},{1,17},{17,33},{33,49},{49,1},{2,18}... | collective-permute-start | bytes 221192 | tf_op jit(solution)/shard_map/ppermute | solution.py:452
  74.7 5.9 %collective-permute-start.14 = (bf16[72,512]{1,0:T(8,128)(2,1)S(1)}, bf16[72,512]{1,0:T(8,128)(2,1)S(1)}, u32[]{:S(2)}, u32[]{:S(2)}) collective-permute-start(bf16[72,512]{1,0:T(8,128)(2,1)S(1)} %shard_map.180.refs_0_.residual_ref), channel_id=1, source_target_pairs={{0,32},{16,48},{32,0},{48,16},{1,33},{17,49},{33,1},{49,17},{2,34}... | collective-permute-start | bytes 221192 | tf_op jit(solution)/shard_map/ppermute | solution.py:452
  81.3 7.5 %collective-permute-start.17 = (bf16[72,512]{1,0:T(8,128)(2,1)S(1)}, bf16[72,512]{1,0:T(8,128)(2,1)S(1)}, u32[]{:S(2)}, u32[]{:S(2)}) collective-permute-start(bf16[72,512]{1,0:T(8,128)(2,1)S(1)} %shard_map.181.refs_0_), channel_id=1, source_target_pairs={{0,1},{1,2},{2,3},{3,4},{4,5},{5,6},{6,7},{7,0},{8,9},{9,10},{10,1... | collective-permute-start | bytes 221192 | tf_op jit(solution)/shard_map/ppermute | solution.py:462
  82.0 6.8 %collective-permute-start.18 = (bf16[72,512]{1,0:T(8,128)(2,1)S(1)}, bf16[72,512]{1,0:T(8,128)(2,1)S(1)}, u32[]{:S(2)}, u32[]{:S(2)}) collective-permute-start(bf16[72,512]{1,0:T(8,128)(2,1)S(1)} %shard_map.181.refs_0_), channel_id=1, source_target_pairs={{0,7},{1,0},{2,1},{3,2},{4,3},{5,4},{6,5},{7,6},{8,15},{9,8},{10,9... | collective-permute-start | bytes 221192 | tf_op jit(solution)/shard_map/ppermute | solution.py:462
  84.6 8.3 %collective-permute-start.16 = (bf16[72,512]{1,0:T(8,128)(2,1)S(1)}, bf16[72,512]{1,0:T(8,128)(2,1)S(1)}, u32[]{:S(2)}, u32[]{:S(2)}) collective-permute-start(bf16[72,512]{1,0:T(8,128)(2,1)S(1)} %shard_map.181.refs_0_), channel_id=1, source_target_pairs={{0,2},{1,3},{2,4},{3,5},{4,6},{5,7},{6,0},{7,1},{8,10},{9,11},{10,... | collective-permute-start | bytes 221192 | tf_op jit(solution)/shard_map/ppermute | solution.py:462
  84.6 8.3 %collective-permute-start.19 = (bf16[72,512]{1,0:T(8,128)(2,1)S(1)}, bf16[72,512]{1,0:T(8,128)(2,1)S(1)}, u32[]{:S(2)}, u32[]{:S(2)}) collective-permute-start(bf16[72,512]{1,0:T(8,128)(2,1)S(1)} %shard_map.181.refs_0_), channel_id=1, source_target_pairs={{0,6},{1,7},{2,0},{3,1},{4,2},{5,3},{6,4},{7,5},{8,14},{9,15},{10,... | collective-permute-start | bytes 221192 | tf_op jit(solution)/shard_map/ppermute | solution.py:462
  88.7 6.5 %collective-permute-start.20 = (bf16[72,512]{1,0:T(8,128)(2,1)S(1)}, bf16[72,512]{1,0:T(8,128)(2,1)S(1)}, u32[]{:S(2)}, u32[]{:S(2)}) collective-permute-start(bf16[72,512]{1,0:T(8,128)(2,1)S(1)} %collective-permute-done.17.refs_2_), channel_id=1, source_target_pairs={{0,2},{1,3},{2,4},{3,5},{4,6},{5,7},{6,0},{7,1},{8,10},{9,11},{10,... | collective-permute-start | bytes 221192 | tf_op jit(solution)/shard_map/ppermute | solution.py:463
  88.7 6.5 %collective-permute-start.21 = (bf16[72,512]{1,0:T(8,128)(2,1)S(1)}, bf16[72,512]{1,0:T(8,128)(2,1)S(1)}, u32[]{:S(2)}, u32[]{:S(2)}) collective-permute-start(bf16[72,512]{1,0:T(8,128)(2,1)S(1)} %collective-permute-done.18.refs_3_), channel_id=1, source_target_pairs={{0,6},{1,7},{2,0},{3,1},{4,2},{5,3},{6,4},{7,5},{8,14},{9,15},{10,... | collective-permute-start | bytes 221192 | tf_op jit(solution)/shard_map/ppermute | solution.py:463
  92.9 6.5 %collective-permute-start.22 = (bf16[72,512]{1,0:T(8,128)(2,1)S(1)}, bf16[72,512]{1,0:T(8,128)(2,1)S(1)}, u32[]{:S(2)}, u32[]{:S(2)}) collective-permute-start(bf16[72,512]{1,0:T(8,128)(2,1)S(1)} %collective-permute-done.16.refs_1_), channel_id=1, source_target_pairs={{0,2},{1,3},{2,4},{3,5},{4,6},{5,7},{6,0},{7,1},{8,10},{9,11},{10,... | collective-permute-start | bytes 221192 | tf_op jit(solution)/shard_map/ppermute | solution.py:463
  103.1 6.5 %collective-permute-start.24 = (bf16[64,640]{1,0:T(8,128)(2,1)S(1)}, bf16[64,640]{1,0:T(8,128)(2,1)S(1)}, u32[]{:S(2)}, u32[]{:S(2)}) collective-permute-start(bf16[64,640]{1,0:T(8,128)(2,1)S(1)} %get-tuple-element.36), channel_id=1, source_target_pairs={{0,48},{16,0},{32,16},{48,32},{1,49},{17,1},{33,17},{49,33},{2,50}... | collective-permute-start | bytes 245768 | tf_op jit(solution)/shard_map/ppermute | solution.py:452
  105.8 6.6 %collective-permute-start.25 = (bf16[64,640]{1,0:T(8,128)(2,1)S(1)}, bf16[64,640]{1,0:T(8,128)(2,1)S(1)}, u32[]{:S(2)}, u32[]{:S(2)}) collective-permute-start(bf16[64,640]{1,0:T(8,128)(2,1)S(1)} %get-tuple-element.37), channel_id=1, source_target_pairs={{0,32},{16,48},{32,0},{48,16},{1,33},{17,49},{33,1},{49,17},{2,34}... | collective-permute-start | bytes 245768 | tf_op jit(solution)/shard_map/ppermute | solution.py:452
  106.5 6.8 %collective-permute-start.26 = (bf16[64,640]{1,0:T(8,128)(2,1)S(1)}, bf16[64,640]{1,0:T(8,128)(2,1)S(1)}, u32[]{:S(2)}, u32[]{:S(2)}) collective-permute-start(bf16[64,640]{1,0:T(8,128)(2,1)S(1)} %get-tuple-element.38), channel_id=1, source_target_pairs={{0,16},{16,32},{32,48},{48,0},{1,17},{17,33},{33,49},{49,1},{2,18}... | collective-permute-start | bytes 245768 | tf_op jit(solution)/shard_map/ppermute | solution.py:452
  (22 other events, 237.7 us)

commit v3 on v2

--- a/solution.py
+++ b/solution.py
@@ -23,12 +23,12 @@
 
 
 def segment_sum(x):
-    lane = lane_in_group(x.shape)
-    for bit in (1, 2, 4, 8):
-        after = pltpu.roll(x, LANES - bit, 1)
-        before = pltpu.roll(x, bit, 1)
-        x = x + jnp.where((lane & bit) == 0, after, before)
-    return x
+    row = lax.broadcasted_iota(jnp.int32, (LANES, LANES), 0)
+    column = lax.broadcasted_iota(jnp.int32, (LANES, LANES), 1)
+    ones = jnp.where((row >> 4) == (column >> 4), 1.0, 0.0).astype(BF)
+    pieces = jnp.concatenate([*thirds(x), jnp.zeros_like(x)], axis=0).astype(BF)
+    sums = jnp.dot(pieces, ones, preferred_element_type=F32)
+    return sums[0:8] + sums[8:16] + sums[16:24]
 
 
 def rows8(x):
@@ -391,14 +391,14 @@
     queries = jnp.dot(normed_q, query_ref[...], preferred_element_type=F32) + wide(small_ref, 24)
     folded = lax.dot_general(
         queries.astype(BF), key_ref[...], (((1,), (1,)), ((), ())), preferred_element_type=F32
-    ).astype(BF)
+    ) * 512 ** (-0.5)
     scores = lax.dot_general(
-        folded, normed[...], (((1,), (1,)), ((), ())), preferred_element_type=F32
-    ) * 512 ** (-0.5)
+        folded.astype(BF), normed[...], (((1,), (1,)), ((), ())), preferred_element_type=F32
+    )
     highest = jnp.max(scores, axis=1, keepdims=True)
     weights = jnp.exp(scores - highest)
     total = jnp.sum(weights, axis=1, keepdims=True)
-    mixed = jnp.dot(weights.astype(BF), normed[...], preferred_element_type=F32) / total
+    mixed = jnp.dot(weights.astype(BF), normed[...], preferred_element_type=F32) * (1.0 / total)
     level = highest + jnp.log(total)
     top, middle, low = thirds(level)
     lane = lax.broadcasted_iota(jnp.int32, (256, LANES), 1)

time: 116 us -> 115 us (level)
  no operation moved by 1% of the time
where the time goes in v3:
time: 115 us; the launch traced here: 113 us
  starting transfers between devices  45.5 us (40%)
  waiting for transfers between devices  37.6 us (33%)
  blocking collectives  16.8 us (15%)
  Pallas kernels  10.4 us (9%)
  local copies, waits for them, and re-layouts  2.72 us (2%)
    ppermute x15, waiting for transfers between devices, spread_out(): arrived[s] = lax.ppermute(blocks[s], axis, ring(count, sign * s))  23.2 us
    all_to_all x1, blocking collectives, over_tiles(): lax.all_to_all(rows, HA + ('z',), split_axis=0, concat_axis=0, tiled=True)  16.8 us
    ppermute x15, starting transfers between devices, spread_out(): arrived[s] = lax.ppermute(blocks[s], axis, ring(count, sign * s))  16.8 us
    all_to_all x1, starting transfers between devices, over_tiles(): lax.all_to_all(rows, HA + ('z',), split_axis=0, concat_axis=0, tiled=True)  10.6 us
    pallas_call x13, Pallas kernels, call(): pl.pallas_call(kernel, out_shape=out_shape, in_specs=specs, out_specs=tup...  10.4 us
    ppermute x4, starting transfers between devices, relayed(): lax.ppermute(block, axis, ring(count, step))  7.45 us
    ppermute x3, waiting for transfers between devices, relayed(): lax.ppermute(after[step], axis, ring(count, move))  6.45 us
    all_to_all x1, waiting for transfers between devices, over_tiles(): lax.all_to_all(rows, HA + ('z',), split_axis=0, concat_axis=0, tiled=True)  6.01 us
  transfers between devices with their start and end apart: 28, of which 18 were waited for; matrix products, arithmetic and copies ran while one was open for 0% of the time, Pallas kernels for 1%

profile of v3, /device:TPU:6, one launch (start us, length us, event | category | flops | bytes accessed | tf_op | source)
XLA Modules:
  0.0 113.4 jit_solution(5884842704057624647)
XLA Ops:
  0.0 2.2 %collective-permute-start = (bf16[64,512]{1,0:T(8,128)(2,1)}, bf16[64,512]{1,0:T(8,128)(2,1)S(1)}, u32[]{:S(2)}, u32[]{:S(2)}) collective-permute-start(bf16[64,512]{1,0:T(8,128)(2,1)} %bitcast.9), channel_id=1, source_target_pairs={{0,64},{64,128},{128,192},{192,0},{1,65},{65,129},{129,193},{193,1... | collective-permute-start | bytes 196616 | tf_op jit(solution)/shard_map/ppermute | solution.py:452
  5.1 3.2 %collective-permute-done.1.s2 = bf16[64,512]{1,0:T(8,128)(2,1)S(1)} collective-permute-done((bf16[64,512]{1,0:T(8,128)(2,1)}, bf16[64,512]{1,0:T(8,128)(2,1)S(1)}, u32[]{:S(2)}, u32[]{:S(2)}) %collective-permute-start.1) | collective-permute-done | bytes 65568 | tf_op jit(solution)/shard_map/ppermute | solution.py:452
  9.9 3.0 %collective-permute-start.4 = (bf16[4,16,512]{2,1,0:T(8,128)(2,1)S(1)}, bf16[4,16,512]{2,1,0:T(8,128)(2,1)S(1)}, u32[]{:S(2)}, u32[]{:S(2)}) collective-permute-start(bf16[4,16,512]{2,1,0:T(8,128)(2,1)S(1)} %get-tuple-element.23), channel_id=1, source_target_pairs={{0,56},{8,0},{16,8},{24,16},{32,24},{40,32},{48,40},{56,48},{1,57}... | collective-permute-start | bytes 196616 | tf_op jit(solution)/shard_map/ppermute | solution.py:469
  12.9 10.6 %all-to-all-start = ((f32[64,1,128]{2,1,0:T(1,128)}), f32[64,1,128]{2,1,0:T(1,128)S(1)}, u32[]{:S(2)}, u32[]{:S(2)}) async-start(f32[64,1,128]{2,1,0:T(1,128)} %get-tuple-element.26), calls=%async_computation | async-start | bytes 65536 | tf_op jit(solution)/shard_map/all_to_all | solution.py:473
  23.6 1.6 %collective-permute-start.5 = (bf16[4,24,512]{2,1,0:T(8,128)(2,1)S(1)}, bf16[4,24,512]{2,1,0:T(8,128)(2,1)S(1)}, u32[]{:S(2)}, u32[]{:S(2)}) collective-permute-start(bf16[4,24,512]{2,1,0:T(8,128)(2,1)S(1)} %get-tuple-element.24), channel_id=1, source_target_pairs={{0,1},{1,2},{2,3},{3,4},{4,5},{5,6},{6,7},{7,0},{8,9},{9,10},{10,1... | collective-permute-start | bytes 294920 | tf_op jit(solution)/shard_map/ppermute | solution.py:469
  25.3 1.7 %collective-permute-start.6 = (bf16[4,24,512]{2,1,0:T(8,128)(2,1)S(1)}, bf16[4,24,512]{2,1,0:T(8,128)(2,1)S(1)}, u32[]{:S(2)}, u32[]{:S(2)}) collective-permute-start(bf16[4,24,512]{2,1,0:T(8,128)(2,1)S(1)} %get-tuple-element.25), channel_id=1, source_target_pairs={{0,7},{1,0},{2,1},{3,2},{4,3},{5,4},{6,5},{7,6},{8,15},{9,8},{10,9... | collective-permute-start | bytes 294920 | tf_op jit(solution)/shard_map/ppermute | solution.py:469
  27.0 6.0 %all-to-all-done.rows_ref = f32[64,1,128]{2,1,0:T(1,128)S(1)} async-done(((f32[64,1,128]{2,1,0:T(1,128)}), f32[64,1,128]{2,1,0:T(1,128)S(1)}, u32[]{:S(2)}, u32[]{:S(2)}) %all-to-all-start) | async-done | bytes 32800 | tf_op jit(solution)/shard_map/all_to_all | solution.py:473
  35.0 2.9 %shard_map.176 = (bf16[4,104,128]{2,1,0:T(8,128)(2,1)S(1)}, f32[64,1,128]{2,1,0:T(1,128)S(1)}) custom-call(bf16[576,1536]{1,0:T(8,128)(2,1)S(1)} %get-tuple-element.27.lhs, f32[38,128]{1,0:T(8,128)S(1)} %bitcast.4, bf16[27,512,128]{2,1,0:T(8,128)(2,1)S(1)} %copy-done.3), custom_call_target="tpu_custom_call" | custom-call | flops 2000000000 | bytes 5467136 | tf_op jit(solution)/shard_map/pallas_call | solution.py:429
  37.9 16.8 %all_to_all.10.rows_ref = f32[64,1,128]{2,1,0:T(1,128)S(1)} all-to-all(f32[64,1,128]{2,1,0:T(1,128)S(1)} %get-tuple-element.29), channel_id=1, replica_groups=mesh['ta'=4,'y'=4,'core'=2,'z'=8] {'y','core','z'}, dimensions={0} | all-to-all | bytes 65536 | tf_op jit(solution)/shard_map/all_to_all | solution.py:473
  55.0 3.2 %collective-permute-start.7 = (bf16[4,104,128]{2,1,0:T(8,128)(2,1)S(1)}, bf16[4,104,128]{2,1,0:T(8,128)(2,1)S(1)}, u32[]{:S(2)}, u32[]{:S(2)}) collective-permute-start(bf16[4,104,128]{2,1,0:T(8,128)(2,1)S(1)} %shard_map.177.s0), channel_id=1, source_target_pairs={{0,64},{64,128},{128,192},{192,0},{1,65},{65,129},{129,193},{193,1... | collective-permute-start | bytes 319496 | tf_op jit(solution)/shard_map/ppermute | solution.py:452
  58.3 2.7 %collective-permute-done.9.s3 = bf16[4,104,128]{2,1,0:T(8,128)(2,1)S(1)} collective-permute-done((bf16[4,104,128]{2,1,0:T(8,128)(2,1)S(1)}, bf16[4,104,128]{2,1,0:T(8,128)(2,1)S(1)}, u32[]{:S(2)}, u32[]{:S(2)}) %collective-permute-start.9) | collective-permute-done | bytes 106528 | tf_op jit(solution)/shard_map/ppermute | solution.py:452
  62.4 2.1 %collective-permute-done.8.s2 = bf16[4,104,128]{2,1,0:T(8,128)(2,1)S(1)} collective-permute-done((bf16[4,104,128]{2,1,0:T(8,128)(2,1)S(1)}, bf16[4,104,128]{2,1,0:T(8,128)(2,1)S(1)}, u32[]{:S(2)}, u32[]{:S(2)}) %collective-permute-start.8) | collective-permute-done | bytes 106528 | tf_op jit(solution)/shard_map/ppermute | solution.py:452
  66.0 1.6 %collective-permute-start.10 = (bf16[72,128]{1,0:T(8,128)(2,1)S(1)}, bf16[72,128]{1,0:T(8,128)(2,1)S(1)}, u32[]{:S(2)}, u32[]{:S(2)}) collective-permute-start(bf16[72,128]{1,0:T(8,128)(2,1)S(1)} %get-tuple-element.32), channel_id=1, source_target_pairs={{0,64},{64,128},{128,192},{192,0},{1,65},{65,129},{129,193},{193,1... | collective-permute-start | bytes 55304 | tf_op jit(solution)/shard_map/ppermute | solution.py:452
  69.9 3.1 %collective-permute-done.11.s2 = bf16[72,128]{1,0:T(8,128)(2,1)S(1)} collective-permute-done((bf16[72,128]{1,0:T(8,128)(2,1)S(1)}, bf16[72,128]{1,0:T(8,128)(2,1)S(1)}, u32[]{:S(2)}, u32[]{:S(2)}) %collective-permute-start.11) | collective-permute-done | bytes 18464 | tf_op jit(solution)/shard_map/ppermute | solution.py:452
  73.7 1.9 %collective-permute-start.14 = (bf16[72,512]{1,0:T(8,128)(2,1)S(1)}, bf16[72,512]{1,0:T(8,128)(2,1)S(1)}, u32[]{:S(2)}, u32[]{:S(2)}) collective-permute-start(bf16[72,512]{1,0:T(8,128)(2,1)S(1)} %shard_map.180.refs_0_.residual_ref), channel_id=1, source_target_pairs={{0,32},{16,48},{32,0},{48,16},{1,33},{17,49},{33,1},{49,17},{2,34}... | collective-permute-start | bytes 221192 | tf_op jit(solution)/shard_map/ppermute | solution.py:452
  81.0 2.6 %collective-permute-start.18 = (bf16[72,512]{1,0:T(8,128)(2,1)S(1)}, bf16[72,512]{1,0:T(8,128)(2,1)S(1)}, u32[]{:S(2)}, u32[]{:S(2)}) collective-permute-start(bf16[72,512]{1,0:T(8,128)(2,1)S(1)} %shard_map.181.refs_0_), channel_id=1, source_target_pairs={{0,7},{1,0},{2,1},{3,2},{4,3},{5,4},{6,5},{7,6},{8,15},{9,8},{10,9... | collective-permute-start | bytes 221192 | tf_op jit(solution)/shard_map/ppermute | solution.py:462
  83.6 4.1 %collective-permute-start.19 = (bf16[72,512]{1,0:T(8,128)(2,1)S(1)}, bf16[72,512]{1,0:T(8,128)(2,1)S(1)}, u32[]{:S(2)}, u32[]{:S(2)}) collective-permute-start(bf16[72,512]{1,0:T(8,128)(2,1)S(1)} %shard_map.181.refs_0_), channel_id=1, source_target_pairs={{0,6},{1,7},{2,0},{3,1},{4,2},{5,3},{6,4},{7,5},{8,14},{9,15},{10,... | collective-permute-start | bytes 221192 | tf_op jit(solution)/shard_map/ppermute | solution.py:462
  87.8 4.1 %collective-permute-start.21 = (bf16[72,512]{1,0:T(8,128)(2,1)S(1)}, bf16[72,512]{1,0:T(8,128)(2,1)S(1)}, u32[]{:S(2)}, u32[]{:S(2)}) collective-permute-start(bf16[72,512]{1,0:T(8,128)(2,1)S(1)} %collective-permute-done.18.refs_3_), channel_id=1, source_target_pairs={{0,6},{1,7},{2,0},{3,1},{4,2},{5,3},{6,4},{7,5},{8,14},{9,15},{10,... | collective-permute-start | bytes 221192 | tf_op jit(solution)/shard_map/ppermute | solution.py:463
  91.9 2.3 %collective-permute-done.20.refs_5_ = bf16[72,512]{1,0:T(8,128)(2,1)S(1)} collective-permute-done((bf16[72,512]{1,0:T(8,128)(2,1)S(1)}, bf16[72,512]{1,0:T(8,128)(2,1)S(1)}, u32[]{:S(2)}, u32[]{:S(2)}) %collective-permute-start.20) | collective-permute-done | bytes 73760 | tf_op jit(solution)/shard_map/ppermute | solution.py:463
  94.2 4.1 %collective-permute-done.22.refs_7_ = bf16[72,512]{1,0:T(8,128)(2,1)S(1)} collective-permute-done((bf16[72,512]{1,0:T(8,128)(2,1)S(1)}, bf16[72,512]{1,0:T(8,128)(2,1)S(1)}, u32[]{:S(2)}, u32[]{:S(2)}) %collective-permute-start.22) | collective-permute-done | bytes 73760 | tf_op jit(solution)/shard_map/ppermute | solution.py:463
  98.8 1.9 %collective-permute-done.23.refs_5_ = bf16[520,512]{1,0:T(8,128)(2,1)S(1)} collective-permute-done((bf16[520,512]{1,0:T(8,128)(2,1)S(1)}, bf16[520,512]{1,0:T(8,128)(2,1)S(1)}, u32[]{:S(2)}, u32[]{:S(2)}) %collective-permute-start.23) | collective-permute-done | bytes 532512 | tf_op jit(solution)/shard_map/ppermute | solution.py:615
  102.1 2.8 %collective-permute-start.24 = (bf16[64,640]{1,0:T(8,128)(2,1)S(1)}, bf16[64,640]{1,0:T(8,128)(2,1)S(1)}, u32[]{:S(2)}, u32[]{:S(2)}) collective-permute-start(bf16[64,640]{1,0:T(8,128)(2,1)S(1)} %get-tuple-element.36), channel_id=1, source_target_pairs={{0,48},{16,0},{32,16},{48,32},{1,49},{17,1},{33,17},{49,33},{2,50}... | collective-permute-start | bytes 245768 | tf_op jit(solution)/shard_map/ppermute | solution.py:452
  105.8 2.8 %collective-permute-done.24.b1 = bf16[64,640]{1,0:T(8,128)(2,1)S(1)} collective-permute-done((bf16[64,640]{1,0:T(8,128)(2,1)S(1)}, bf16[64,640]{1,0:T(8,128)(2,1)S(1)}, u32[]{:S(2)}, u32[]{:S(2)}) %collective-permute-start.24) | collective-permute-done | bytes 81952 | tf_op jit(solution)/shard_map/ppermute | solution.py:452
  108.6 2.8 %collective-permute-done.25.b2 = bf16[64,640]{1,0:T(8,128)(2,1)S(1)} collective-permute-done((bf16[64,640]{1,0:T(8,128)(2,1)S(1)}, bf16[64,640]{1,0:T(8,128)(2,1)S(1)}, u32[]{:S(2)}, u32[]{:S(2)}) %collective-permute-start.25) | collective-permute-done | bytes 81952 | tf_op jit(solution)/shard_map/ppermute | solution.py:452
  (94 shorter events, 23.0 us)
Async XLA Ops:
  2.2 6.0 %collective-permute-start.1 = (bf16[64,512]{1,0:T(8,128)(2,1)}, bf16[64,512]{1,0:T(8,128)(2,1)S(1)}, u32[]{:S(2)}, u32[]{:S(2)}) collective-permute-start(bf16[64,512]{1,0:T(8,128)(2,1)} %bitcast.10), channel_id=1, source_target_pairs={{0,128},{64,192},{128,0},{192,64},{1,129},{65,193},{129,1},{193,65... | collective-permute-start | bytes 196616 | tf_op jit(solution)/shard_map/ppermute | solution.py:452
  2.9 6.0 %collective-permute-start.2 = (bf16[64,512]{1,0:T(8,128)(2,1)}, bf16[64,512]{1,0:T(8,128)(2,1)S(1)}, u32[]{:S(2)}, u32[]{:S(2)}) collective-permute-start(bf16[64,512]{1,0:T(8,128)(2,1)} %bitcast.11), channel_id=1, source_target_pairs={{0,192},{64,0},{128,64},{192,128},{1,193},{65,1},{129,65},{193,129... | collective-permute-start | bytes 196616 | tf_op jit(solution)/shard_map/ppermute | solution.py:452
  9.9 13.6 %collective-permute-start.3 = (bf16[4,16,512]{2,1,0:T(8,128)(2,1)S(1)}, bf16[4,16,512]{2,1,0:T(8,128)(2,1)S(1)}, u32[]{:S(2)}, u32[]{:S(2)}) collective-permute-start(bf16[4,16,512]{2,1,0:T(8,128)(2,1)S(1)} %get-tuple-element.22), channel_id=1, source_target_pairs={{0,8},{8,16},{16,24},{24,32},{32,40},{40,48},{48,56},{56,0},{1,9},... | collective-permute-start | bytes 196616 | tf_op jit(solution)/shard_map/ppermute | solution.py:469
  9.9 13.6 %collective-permute-start.4 = (bf16[4,16,512]{2,1,0:T(8,128)(2,1)S(1)}, bf16[4,16,512]{2,1,0:T(8,128)(2,1)S(1)}, u32[]{:S(2)}, u32[]{:S(2)}) collective-permute-start(bf16[4,16,512]{2,1,0:T(8,128)(2,1)S(1)} %get-tuple-element.23), channel_id=1, source_target_pairs={{0,56},{8,0},{16,8},{24,16},{32,24},{40,32},{48,40},{56,48},{1,57}... | collective-permute-start | bytes 196616 | tf_op jit(solution)/shard_map/ppermute | solution.py:469
  12.9 20.1 %all-to-all-start = ((f32[64,1,128]{2,1,0:T(1,128)}), f32[64,1,128]{2,1,0:T(1,128)S(1)}, u32[]{:S(2)}, u32[]{:S(2)}) async-start(f32[64,1,128]{2,1,0:T(1,128)} %get-tuple-element.26), calls=%async_computation | async-start | bytes 65536 | tf_op jit(solution)/shard_map/all_to_all | solution.py:473
  23.6 9.3 %collective-permute-start.5 = (bf16[4,24,512]{2,1,0:T(8,128)(2,1)S(1)}, bf16[4,24,512]{2,1,0:T(8,128)(2,1)S(1)}, u32[]{:S(2)}, u32[]{:S(2)}) collective-permute-start(bf16[4,24,512]{2,1,0:T(8,128)(2,1)S(1)} %get-tuple-element.24), channel_id=1, source_target_pairs={{0,1},{1,2},{2,3},{3,4},{4,5},{5,6},{6,7},{7,0},{8,9},{9,10},{10,1... | collective-permute-start | bytes 294920 | tf_op jit(solution)/shard_map/ppermute | solution.py:469
  25.3 7.7 %collective-permute-start.6 = (bf16[4,24,512]{2,1,0:T(8,128)(2,1)S(1)}, bf16[4,24,512]{2,1,0:T(8,128)(2,1)S(1)}, u32[]{:S(2)}, u32[]{:S(2)}) collective-permute-start(bf16[4,24,512]{2,1,0:T(8,128)(2,1)S(1)} %get-tuple-element.25), channel_id=1, source_target_pairs={{0,7},{1,0},{2,1},{3,2},{4,3},{5,4},{6,5},{7,6},{8,15},{9,8},{10,9... | collective-permute-start | bytes 294920 | tf_op jit(solution)/shard_map/ppermute | solution.py:469
  55.0 6.0 %collective-permute-start.9 = (bf16[4,104,128]{2,1,0:T(8,128)(2,1)S(1)}, bf16[4,104,128]{2,1,0:T(8,128)(2,1)S(1)}, u32[]{:S(2)}, u32[]{:S(2)}) collective-permute-start(bf16[4,104,128]{2,1,0:T(8,128)(2,1)S(1)} %shard_map.177.s0), channel_id=1, source_target_pairs={{0,192},{64,0},{128,64},{192,128},{1,193},{65,1},{129,65},{193,129... | collective-permute-start | bytes 319496 | tf_op jit(solution)/shard_map/ppermute | solution.py:452
  55.0 7.3 %collective-permute-start.7 = (bf16[4,104,128]{2,1,0:T(8,128)(2,1)S(1)}, bf16[4,104,128]{2,1,0:T(8,128)(2,1)S(1)}, u32[]{:S(2)}, u32[]{:S(2)}) collective-permute-start(bf16[4,104,128]{2,1,0:T(8,128)(2,1)S(1)} %shard_map.177.s0), channel_id=1, source_target_pairs={{0,64},{64,128},{128,192},{192,0},{1,65},{65,129},{129,193},{193,1... | collective-permute-start | bytes 319496 | tf_op jit(solution)/shard_map/ppermute | solution.py:452
  58.3 6.2 %collective-permute-start.8 = (bf16[4,104,128]{2,1,0:T(8,128)(2,1)S(1)}, bf16[4,104,128]{2,1,0:T(8,128)(2,1)S(1)}, u32[]{:S(2)}, u32[]{:S(2)}) collective-permute-start(bf16[4,104,128]{2,1,0:T(8,128)(2,1)S(1)} %shard_map.177.s0), channel_id=1, source_target_pairs={{0,128},{64,192},{128,0},{192,64},{1,129},{65,193},{129,1},{193,65... | collective-permute-start | bytes 319496 | tf_op jit(solution)/shard_map/ppermute | solution.py:452
  67.6 5.3 %collective-permute-start.11 = (bf16[72,128]{1,0:T(8,128)(2,1)S(1)}, bf16[72,128]{1,0:T(8,128)(2,1)S(1)}, u32[]{:S(2)}, u32[]{:S(2)}) collective-permute-start(bf16[72,128]{1,0:T(8,128)(2,1)S(1)} %get-tuple-element.33), channel_id=1, source_target_pairs={{0,128},{64,192},{128,0},{192,64},{1,129},{65,193},{129,1},{193,65... | collective-permute-start | bytes 55304 | tf_op jit(solution)/shard_map/ppermute | solution.py:452
  67.7 5.2 %collective-permute-start.12 = (bf16[72,128]{1,0:T(8,128)(2,1)S(1)}, bf16[72,128]{1,0:T(8,128)(2,1)S(1)}, u32[]{:S(2)}, u32[]{:S(2)}) collective-permute-start(bf16[72,128]{1,0:T(8,128)(2,1)S(1)} %get-tuple-element.34), channel_id=1, source_target_pairs={{0,192},{64,0},{128,64},{192,128},{1,193},{65,1},{129,65},{193,129... | collective-permute-start | bytes 55304 | tf_op jit(solution)/shard_map/ppermute | solution.py:452
  73.0 5.6 %collective-permute-start.13 = (bf16[72,512]{1,0:T(8,128)(2,1)S(1)}, bf16[72,512]{1,0:T(8,128)(2,1)S(1)}, u32[]{:S(2)}, u32[]{:S(2)}) collective-permute-start(bf16[72,512]{1,0:T(8,128)(2,1)S(1)} %shard_map.180.refs_0_.residual_ref), channel_id=1, source_target_pairs={{0,16},{16,32},{32,48},{48,0},{1,17},{17,33},{33,49},{49,1},{2,18}... | collective-permute-start | bytes 221192 | tf_op jit(solution)/shard_map/ppermute | solution.py:452
  73.7 5.9 %collective-permute-start.14 = (bf16[72,512]{1,0:T(8,128)(2,1)S(1)}, bf16[72,512]{1,0:T(8,128)(2,1)S(1)}, u32[]{:S(2)}, u32[]{:S(2)}) collective-permute-start(bf16[72,512]{1,0:T(8,128)(2,1)S(1)} %shard_map.180.refs_0_.residual_ref), channel_id=1, source_target_pairs={{0,32},{16,48},{32,0},{48,16},{1,33},{17,49},{33,1},{49,17},{2,34}... | collective-permute-start | bytes 221192 | tf_op jit(solution)/shard_map/ppermute | solution.py:452
  80.3 7.5 %collective-permute-start.17 = (bf16[72,512]{1,0:T(8,128)(2,1)S(1)}, bf16[72,512]{1,0:T(8,128)(2,1)S(1)}, u32[]{:S(2)}, u32[]{:S(2)}) collective-permute-start(bf16[72,512]{1,0:T(8,128)(2,1)S(1)} %shard_map.181.refs_0_), channel_id=1, source_target_pairs={{0,1},{1,2},{2,3},{3,4},{4,5},{5,6},{6,7},{7,0},{8,9},{9,10},{10,1... | collective-permute-start | bytes 221192 | tf_op jit(solution)/shard_map/ppermute | solution.py:462
  81.0 6.7 %collective-permute-start.18 = (bf16[72,512]{1,0:T(8,128)(2,1)S(1)}, bf16[72,512]{1,0:T(8,128)(2,1)S(1)}, u32[]{:S(2)}, u32[]{:S(2)}) collective-permute-start(bf16[72,512]{1,0:T(8,128)(2,1)S(1)} %shard_map.181.refs_0_), channel_id=1, source_target_pairs={{0,7},{1,0},{2,1},{3,2},{4,3},{5,4},{6,5},{7,6},{8,15},{9,8},{10,9... | collective-permute-start | bytes 221192 | tf_op jit(solution)/shard_map/ppermute | solution.py:462
  83.6 8.3 %collective-permute-start.16 = (bf16[72,512]{1,0:T(8,128)(2,1)S(1)}, bf16[72,512]{1,0:T(8,128)(2,1)S(1)}, u32[]{:S(2)}, u32[]{:S(2)}) collective-permute-start(bf16[72,512]{1,0:T(8,128)(2,1)S(1)} %shard_map.181.refs_0_), channel_id=1, source_target_pairs={{0,2},{1,3},{2,4},{3,5},{4,6},{5,7},{6,0},{7,1},{8,10},{9,11},{10,... | collective-permute-start | bytes 221192 | tf_op jit(solution)/shard_map/ppermute | solution.py:462
  83.6 8.3 %collective-permute-start.19 = (bf16[72,512]{1,0:T(8,128)(2,1)S(1)}, bf16[72,512]{1,0:T(8,128)(2,1)S(1)}, u32[]{:S(2)}, u32[]{:S(2)}) collective-permute-start(bf16[72,512]{1,0:T(8,128)(2,1)S(1)} %shard_map.181.refs_0_), channel_id=1, source_target_pairs={{0,6},{1,7},{2,0},{3,1},{4,2},{5,3},{6,4},{7,5},{8,14},{9,15},{10,... | collective-permute-start | bytes 221192 | tf_op jit(solution)/shard_map/ppermute | solution.py:462
  87.7 6.5 %collective-permute-start.20 = (bf16[72,512]{1,0:T(8,128)(2,1)S(1)}, bf16[72,512]{1,0:T(8,128)(2,1)S(1)}, u32[]{:S(2)}, u32[]{:S(2)}) collective-permute-start(bf16[72,512]{1,0:T(8,128)(2,1)S(1)} %collective-permute-done.17.refs_2_), channel_id=1, source_target_pairs={{0,2},{1,3},{2,4},{3,5},{4,6},{5,7},{6,0},{7,1},{8,10},{9,11},{10,... | collective-permute-start | bytes 221192 | tf_op jit(solution)/shard_map/ppermute | solution.py:463
  87.8 6.5 %collective-permute-start.21 = (bf16[72,512]{1,0:T(8,128)(2,1)S(1)}, bf16[72,512]{1,0:T(8,128)(2,1)S(1)}, u32[]{:S(2)}, u32[]{:S(2)}) collective-permute-start(bf16[72,512]{1,0:T(8,128)(2,1)S(1)} %collective-permute-done.18.refs_3_), channel_id=1, source_target_pairs={{0,6},{1,7},{2,0},{3,1},{4,2},{5,3},{6,4},{7,5},{8,14},{9,15},{10,... | collective-permute-start | bytes 221192 | tf_op jit(solution)/shard_map/ppermute | solution.py:463
  91.9 6.5 %collective-permute-start.22 = (bf16[72,512]{1,0:T(8,128)(2,1)S(1)}, bf16[72,512]{1,0:T(8,128)(2,1)S(1)}, u32[]{:S(2)}, u32[]{:S(2)}) collective-permute-start(bf16[72,512]{1,0:T(8,128)(2,1)S(1)} %collective-permute-done.16.refs_1_), channel_id=1, source_target_pairs={{0,2},{1,3},{2,4},{3,5},{4,6},{5,7},{6,0},{7,1},{8,10},{9,11},{10,... | collective-permute-start | bytes 221192 | tf_op jit(solution)/shard_map/ppermute | solution.py:463
  102.1 6.6 %collective-permute-start.24 = (bf16[64,640]{1,0:T(8,128)(2,1)S(1)}, bf16[64,640]{1,0:T(8,128)(2,1)S(1)}, u32[]{:S(2)}, u32[]{:S(2)}) collective-permute-start(bf16[64,640]{1,0:T(8,128)(2,1)S(1)} %get-tuple-element.36), channel_id=1, source_target_pairs={{0,48},{16,0},{32,16},{48,32},{1,49},{17,1},{33,17},{49,33},{2,50}... | collective-permute-start | bytes 245768 | tf_op jit(solution)/shard_map/ppermute | solution.py:452
  104.9 6.6 %collective-permute-start.25 = (bf16[64,640]{1,0:T(8,128)(2,1)S(1)}, bf16[64,640]{1,0:T(8,128)(2,1)S(1)}, u32[]{:S(2)}, u32[]{:S(2)}) collective-permute-start(bf16[64,640]{1,0:T(8,128)(2,1)S(1)} %get-tuple-element.37), channel_id=1, source_target_pairs={{0,32},{16,48},{32,0},{48,16},{1,33},{17,49},{33,1},{49,17},{2,34}... | collective-permute-start | bytes 245768 | tf_op jit(solution)/shard_map/ppermute | solution.py:452
  105.5 6.8 %collective-permute-start.26 = (bf16[64,640]{1,0:T(8,128)(2,1)S(1)}, bf16[64,640]{1,0:T(8,128)(2,1)S(1)}, u32[]{:S(2)}, u32[]{:S(2)}) collective-permute-start(bf16[64,640]{1,0:T(8,128)(2,1)S(1)} %get-tuple-element.38), channel_id=1, source_target_pairs={{0,16},{16,32},{32,48},{48,0},{1,17},{17,33},{33,49},{49,1},{2,18}... | collective-permute-start | bytes 245768 | tf_op jit(solution)/shard_map/ppermute | solution.py:452
  (22 other events, 236.4 us)

commit v4 on v3

--- a/solution.py
+++ b/solution.py
@@ -14,6 +14,7 @@
 F32 = jnp.float32
 LANES = 128
 LIMIT = 32 * 1024 * 1024
+SHIFTS = (0, 2, 1, 3)
 PAIRS = ((0, 1), (2, 3), (4, 5), (6, 7), (8,))
 VMEM = pl.BlockSpec(memory_space=pltpu.VMEM)
 
@@ -152,13 +153,13 @@
         )
         stats.append((block,) + channel_stats(x, None, x.shape[0]))
     encode(out_ref, stats)
-    for s, ref in enumerate(slots):
+    for s, ref in zip(SHIFTS, slots):
         first_ref[s] = ref[0:16, :]
         last_ref[s] = ref[48:64, :]
 
 
 def columns_kernel(s0, s1, s2, s3, top_ref, bottom_ref, first_ref, last_ref, tall, sides):
-    for s, ref in enumerate((s0, s1, s2, s3)):
+    for s, ref in zip(SHIFTS, (s0, s1, s2, s3)):
         for b in range(4):
             lanes = slice(b * LANES, (b + 1) * LANES)
             tall[b, 0:16, :] = top_ref[s, :, lanes].astype(F32)
@@ -182,7 +183,7 @@
 
 
 def residual_kernel(s0, s1, s2, s3, out_ref, parts):
-    for s, ref in enumerate((s0, s1, s2, s3)):
+    for s, ref in zip(SHIFTS, (s0, s1, s2, s3)):
         parts[turned(lax.axis_index("ta"), s)] = ref[...]
     out_ref[...] = jnp.concatenate([parts[b] for b in range(4)], axis=1)
 
@@ -247,7 +248,7 @@
     ta = lax.axis_index("ta")
     coefficients = decode(rows_ref, small_ref, 0)
     keep = inside(8 * lax.axis_index(HA) - 2, 8 * lax.axis_index("z") - 2, 144, 12, grid)
-    for s, ref in enumerate((s0, s1, s2, s3)):
+    for s, ref in zip(SHIFTS, (s0, s1, s2, s3)):
         frames[turned(ta, s)] = ref[...]
     for frame in range(4):
         s = turned(ta, frame)
@@ -327,13 +328,13 @@
         product[:, lanes] = part if before is None else before[:, lanes] + part
 
 
-def second_conv_first_kernel(s0, s3, kernel_ref, out_ref, lhs):
-    add_blocks((s0, s3), (0, 3), kernel_ref, lhs, out_ref)
+def second_conv_first_kernel(s0, s1, kernel_ref, out_ref, lhs):
+    add_blocks((s0, s1), SHIFTS[:2], kernel_ref, lhs, out_ref)
 
 
 def second_conv_kernel(
-    s1,
     s2,
+    s3,
     before_ref,
     small_ref,
     own_ref,
@@ -348,7 +349,7 @@
     parts,
 ):
     ta = lax.axis_index("ta")
-    add_blocks((s1, s2), (1, 2), kernel_ref, lhs, product, before_ref)
+    add_blocks((s2, s3), SHIFTS[2:], kernel_ref, lhs, product, before_ref)
     totals = shifted_sums(product, 112, 10, 80)
     bias = small_ref[37:38, :]
     tiles = []
@@ -361,7 +362,7 @@
         tiles.append(residual.astype(F32))
     mean, spread = channel_stats(jnp.concatenate(tiles, axis=0), None, 256)
     packed = pack_stats(mean, spread)
-    for s, ref in enumerate((out0, out1, out2, out3)):
+    for s, ref in zip(SHIFTS, (out0, out1, out2, out3)):
         ref[0:64, :] = parts[lax.rem(ta + s, 4)]
         ref[64:72, :] = packed
 
@@ -441,26 +442,18 @@
     return [(i, (i + step) % count) for i in range(count)]
 
 
-def long_first(count):
-    return sorted(range(1, count), key=lambda s: -min(s, count - s))
-
-
 def spread_out(blocks, axis, sign=1):
-    count = lax.axis_size(axis)
-    arrived = {0: blocks[0]}
-    for s in long_first(count):
-        arrived[s] = lax.ppermute(blocks[s], axis, ring(count, sign * s))
-    return [arrived[s] for s in range(count)]
+    return [blocks[0]] + [lax.ppermute(b, axis, ring(4, sign * s)) for b, s in zip(blocks[1:], SHIFTS[1:])]
 
 
 def around(block, axis):
-    return spread_out([block] * lax.axis_size(axis), axis)
+    return spread_out([block] * 4, axis)
 
 
 def relayed(block, axis):
     count = lax.axis_size(axis)
     after = {step: lax.ppermute(block, axis, ring(count, step)) for step in (2, 1, -1, -2)}
-    further = [lax.ppermute(after[step], axis, ring(count, move)) for step, move in ((1, 2), (-1, -2), (2, 2))]
+    further = [lax.ppermute(after[step], axis, ring(count, move)) for step, move in ((2, 2), (1, 2), (-1, -2))]
     return [block, *after.values(), *further]
 
 
@@ -570,8 +563,7 @@
         [VMEM] * 3,
         [pltpu.VMEM((448, 768), BF)],
         10**9,
-        blocks[0],
-        blocks[3],
+        *blocks[:2],
         conv2_kernel,
     )
     parts = call(
@@ -585,8 +577,7 @@
             pltpu.VMEM((4, cells, LANES), BF),
         ],
         2 * 10**9,
-        blocks[1],
-        blocks[2],
+        *blocks[2:],
         before,
         small,
         own,

time: 115 us -> 110 us (0.957)
  waiting for transfers between devices: 37.6 us -> 33.5 us
    ppermute x15, waiting for transfers between devices: 23.2 us -> 20.3 us  [spread_out(): lax.ppermute(b, axis, ring(4, sign * s))]
    ppermute x3, waiting for transfers between devices: 6.45 us -> 3.82 us  [relayed(): lax.ppermute(after[step], axis, ring(count, move))]
    ppermute x4, waiting for transfers between devices: 0.01 us -> 1.51 us  [relayed(): lax.ppermute(block, axis, ring(count, step))]
    ppermute x4, starting transfers between devices: 7.45 us -> 6.24 us  [relayed(): lax.ppermute(block, axis, ring(count, step))]
  transfers between devices with their start and end apart: 28 -> 28, of which waited for: 18 -> 15; matrix products, arithmetic and copies ran while one was open for 0% -> 0% of each run, Pallas kernels for 1% -> 1%
where the time goes in v4:
time: 110 us; the launch traced here: 109 us
  starting transfers between devices  45.3 us (41%)
  waiting for transfers between devices  33.5 us (30%)
  blocking collectives  16.8 us (15%)
  Pallas kernels  10.4 us (9%)
  local copies, waits for them, and re-layouts  2.75 us (2%)
    ppermute x15, waiting for transfers between devices, spread_out(): lax.ppermute(b, axis, ring(4, sign * s))  20.3 us
    ppermute x15, starting transfers between devices, spread_out(): lax.ppermute(b, axis, ring(4, sign * s))  17.4 us
    all_to_all x1, blocking collectives, over_tiles(): lax.all_to_all(rows, HA + ('z',), split_axis=0, concat_axis=0, tiled=True)  16.8 us
    all_to_all x1, starting transfers between devices, over_tiles(): lax.all_to_all(rows, HA + ('z',), split_axis=0, concat_axis=0, tiled=True)  10.9 us
    pallas_call x13, Pallas kernels, call(): pl.pallas_call(kernel, out_shape=out_shape, in_specs=specs, out_specs=tup...  10.4 us
    ppermute x4, starting transfers between devices, relayed(): lax.ppermute(block, axis, ring(count, step))  6.24 us
    all_to_all x1, waiting for transfers between devices, over_tiles(): lax.all_to_all(rows, HA + ('z',), split_axis=0, concat_axis=0, tiled=True)  6.01 us
    ppermute x2, starting transfers between devices, both_sides(): lax.ppermute(low, axis, ring(count, -1))  4.62 us
  transfers between devices with their start and end apart: 28, of which 15 were waited for; matrix products, arithmetic and copies ran while one was open for 0% of the time, Pallas kernels for 1%

profile of v4, /device:TPU:6, one launch (start us, length us, event | category | flops | bytes accessed | tf_op | source)
XLA Modules:
  0.0 109.2 jit_solution(14206201124592585315)
XLA Ops:
  1.4 2.1 %collective-permute-start.1 = (bf16[64,512]{1,0:T(8,128)(2,1)}, bf16[64,512]{1,0:T(8,128)(2,1)S(1)}, u32[]{:S(2)}, u32[]{:S(2)}) collective-permute-start(bf16[64,512]{1,0:T(8,128)(2,1)} %bitcast.10), channel_id=1, source_target_pairs={{0,64},{64,128},{128,192},{192,0},{1,65},{65,129},{129,193},{193,1... | collective-permute-start | bytes 196616 | tf_op jit(solution)/shard_map/ppermute | solution.py:446
  6.4 2.8 %collective-permute-done.2.s3 = bf16[64,512]{1,0:T(8,128)(2,1)S(1)} collective-permute-done((bf16[64,512]{1,0:T(8,128)(2,1)}, bf16[64,512]{1,0:T(8,128)(2,1)S(1)}, u32[]{:S(2)}, u32[]{:S(2)}) %collective-permute-start.2) | collective-permute-done | bytes 65568 | tf_op jit(solution)/shard_map/ppermute | solution.py:446
  10.2 3.0 %collective-permute-start.4 = (bf16[4,16,512]{2,1,0:T(8,128)(2,1)S(1)}, bf16[4,16,512]{2,1,0:T(8,128)(2,1)S(1)}, u32[]{:S(2)}, u32[]{:S(2)}) collective-permute-start(bf16[4,16,512]{2,1,0:T(8,128)(2,1)S(1)} %get-tuple-element.23), channel_id=1, source_target_pairs={{0,56},{8,0},{16,8},{24,16},{32,24},{40,32},{48,40},{56,48},{1,57}... | collective-permute-start | bytes 196616 | tf_op jit(solution)/shard_map/ppermute | solution.py:462
  13.2 10.9 %all-to-all-start = ((f32[64,1,128]{2,1,0:T(1,128)}), f32[64,1,128]{2,1,0:T(1,128)S(1)}, u32[]{:S(2)}, u32[]{:S(2)}) async-start(f32[64,1,128]{2,1,0:T(1,128)} %get-tuple-element.26), calls=%async_computation | async-start | bytes 65536 | tf_op jit(solution)/shard_map/all_to_all | solution.py:466
  24.2 1.6 %collective-permute-start.5 = (bf16[4,24,512]{2,1,0:T(8,128)(2,1)S(1)}, bf16[4,24,512]{2,1,0:T(8,128)(2,1)S(1)}, u32[]{:S(2)}, u32[]{:S(2)}) collective-permute-start(bf16[4,24,512]{2,1,0:T(8,128)(2,1)S(1)} %get-tuple-element.24), channel_id=1, source_target_pairs={{0,1},{1,2},{2,3},{3,4},{4,5},{5,6},{6,7},{7,0},{8,9},{9,10},{10,1... | collective-permute-start | bytes 294920 | tf_op jit(solution)/shard_map/ppermute | solution.py:462
  25.9 1.7 %collective-permute-start.6 = (bf16[4,24,512]{2,1,0:T(8,128)(2,1)S(1)}, bf16[4,24,512]{2,1,0:T(8,128)(2,1)S(1)}, u32[]{:S(2)}, u32[]{:S(2)}) collective-permute-start(bf16[4,24,512]{2,1,0:T(8,128)(2,1)S(1)} %get-tuple-element.25), channel_id=1, source_target_pairs={{0,7},{1,0},{2,1},{3,2},{4,3},{5,4},{6,5},{7,6},{8,15},{9,8},{10,9... | collective-permute-start | bytes 294920 | tf_op jit(solution)/shard_map/ppermute | solution.py:462
  27.6 6.0 %all-to-all-done.rows_ref = f32[64,1,128]{2,1,0:T(1,128)S(1)} async-done(((f32[64,1,128]{2,1,0:T(1,128)}), f32[64,1,128]{2,1,0:T(1,128)S(1)}, u32[]{:S(2)}, u32[]{:S(2)}) %all-to-all-start) | async-done | bytes 32800 | tf_op jit(solution)/shard_map/all_to_all | solution.py:466
  35.6 2.9 %shard_map.176 = (bf16[4,104,128]{2,1,0:T(8,128)(2,1)S(1)}, f32[64,1,128]{2,1,0:T(1,128)S(1)}) custom-call(bf16[576,1536]{1,0:T(8,128)(2,1)S(1)} %get-tuple-element.27.lhs, f32[38,128]{1,0:T(8,128)S(1)} %bitcast.4, bf16[27,512,128]{2,1,0:T(8,128)(2,1)S(1)} %copy-done.3), custom_call_target="tpu_custom_call" | custom-call | flops 2000000000 | bytes 5467136 | tf_op jit(solution)/shard_map/pallas_call | solution.py:430
  38.5 16.8 %all_to_all.10.rows_ref = f32[64,1,128]{2,1,0:T(1,128)S(1)} all-to-all(f32[64,1,128]{2,1,0:T(1,128)S(1)} %get-tuple-element.29), channel_id=1, replica_groups=mesh['ta'=4,'y'=4,'core'=2,'z'=8] {'y','core','z'}, dimensions={0} | all-to-all | bytes 65536 | tf_op jit(solution)/shard_map/all_to_all | solution.py:466
  55.7 1.5 %collective-permute-start.7 = (bf16[4,104,128]{2,1,0:T(8,128)(2,1)S(1)}, bf16[4,104,128]{2,1,0:T(8,128)(2,1)S(1)}, u32[]{:S(2)}, u32[]{:S(2)}) collective-permute-start(bf16[4,104,128]{2,1,0:T(8,128)(2,1)S(1)} %shard_map.177.s0), channel_id=1, source_target_pairs={{0,64},{64,128},{128,192},{192,0},{1,65},{65,129},{129,193},{193,1... | collective-permute-start | bytes 319496 | tf_op jit(solution)/shard_map/ppermute | solution.py:446
  57.8 5.1 %collective-permute-done.9.s1 = bf16[4,104,128]{2,1,0:T(8,128)(2,1)S(1)} collective-permute-done((bf16[4,104,128]{2,1,0:T(8,128)(2,1)S(1)}, bf16[4,104,128]{2,1,0:T(8,128)(2,1)S(1)}, u32[]{:S(2)}, u32[]{:S(2)}) %collective-permute-start.9) | collective-permute-done | bytes 106528 | tf_op jit(solution)/shard_map/ppermute | solution.py:446
  64.0 1.5 %shard_map.179 = (bf16[72,128]{1,0:T(8,128)(2,1)S(1)}, bf16[72,128]{1,0:T(8,128)(2,1)S(1)}, bf16[72,128]{1,0:T(8,128)(2,1)S(1)}, bf16[72,128]{1,0:T(8,128)(2,1)S(1)}) custom-call(bf16[4,104,128]{2,1,0:T(8,128)(2,1)S(1)} %collective-permute-done.7.s2, bf16[4,104,128]{2,1,0:T(8,128)(2,1)S(1)} %collective-permute-done.8.s3, ...), custom_call_target="tpu_custom_call" | custom-call | flops 2000000000 | bytes 5975040 | tf_op jit(solution)/shard_map/pallas_call | solution.py:430
  67.9 3.0 %collective-permute-done.10.s1 = bf16[72,128]{1,0:T(8,128)(2,1)S(1)} collective-permute-done((bf16[72,128]{1,0:T(8,128)(2,1)S(1)}, bf16[72,128]{1,0:T(8,128)(2,1)S(1)}, u32[]{:S(2)}, u32[]{:S(2)}) %collective-permute-start.10) | collective-permute-done | bytes 18464 | tf_op jit(solution)/shard_map/ppermute | solution.py:446
  74.1 2.7 %collective-permute-start.15 = (bf16[72,512]{1,0:T(8,128)(2,1)S(1)}, bf16[72,512]{1,0:T(8,128)(2,1)S(1)}, u32[]{:S(2)}, u32[]{:S(2)}) collective-permute-start(bf16[72,512]{1,0:T(8,128)(2,1)S(1)} %shard_map.180.refs_0_.residual_ref), channel_id=1, source_target_pairs={{0,48},{16,0},{32,16},{48,32},{1,49},{17,1},{33,17},{49,33},{2,50}... | collective-permute-start | bytes 221192 | tf_op jit(solution)/shard_map/ppermute | solution.py:446
  80.5 2.6 %collective-permute-start.18 = (bf16[72,512]{1,0:T(8,128)(2,1)S(1)}, bf16[72,512]{1,0:T(8,128)(2,1)S(1)}, u32[]{:S(2)}, u32[]{:S(2)}) collective-permute-start(bf16[72,512]{1,0:T(8,128)(2,1)S(1)} %shard_map.181.refs_0_), channel_id=1, source_target_pairs={{0,7},{1,0},{2,1},{3,2},{4,3},{5,4},{6,5},{7,6},{8,15},{9,8},{10,9... | collective-permute-start | bytes 221192 | tf_op jit(solution)/shard_map/ppermute | solution.py:455
  83.1 2.3 %collective-permute-start.19 = (bf16[72,512]{1,0:T(8,128)(2,1)S(1)}, bf16[72,512]{1,0:T(8,128)(2,1)S(1)}, u32[]{:S(2)}, u32[]{:S(2)}) collective-permute-start(bf16[72,512]{1,0:T(8,128)(2,1)S(1)} %shard_map.181.refs_0_), channel_id=1, source_target_pairs={{0,6},{1,7},{2,0},{3,1},{4,2},{5,3},{6,4},{7,5},{8,14},{9,15},{10,... | collective-permute-start | bytes 221192 | tf_op jit(solution)/shard_map/ppermute | solution.py:455
  85.4 1.5 %collective-permute-done.16.refs_1_ = bf16[72,512]{1,0:T(8,128)(2,1)S(1)} collective-permute-done((bf16[72,512]{1,0:T(8,128)(2,1)S(1)}, bf16[72,512]{1,0:T(8,128)(2,1)S(1)}, u32[]{:S(2)}, u32[]{:S(2)}) %collective-permute-start.16) | collective-permute-done | bytes 73760 | tf_op jit(solution)/shard_map/ppermute | solution.py:455
  87.2 4.0 %collective-permute-start.22 = (bf16[72,512]{1,0:T(8,128)(2,1)S(1)}, bf16[72,512]{1,0:T(8,128)(2,1)S(1)}, u32[]{:S(2)}, u32[]{:S(2)}) collective-permute-start(bf16[72,512]{1,0:T(8,128)(2,1)S(1)} %collective-permute-done.18.refs_3_), channel_id=1, source_target_pairs={{0,6},{1,7},{2,0},{3,1},{4,2},{5,3},{6,4},{7,5},{8,14},{9,15},{10,... | collective-permute-start | bytes 221192 | tf_op jit(solution)/shard_map/ppermute | solution.py:456
  91.2 2.2 %collective-permute-done.20.refs_5_ = bf16[72,512]{1,0:T(8,128)(2,1)S(1)} collective-permute-done((bf16[72,512]{1,0:T(8,128)(2,1)S(1)}, bf16[72,512]{1,0:T(8,128)(2,1)S(1)}, u32[]{:S(2)}, u32[]{:S(2)}) %collective-permute-start.20) | collective-permute-done | bytes 73760 | tf_op jit(solution)/shard_map/ppermute | solution.py:456
  93.4 1.6 %collective-permute-done.21.refs_6_ = bf16[72,512]{1,0:T(8,128)(2,1)S(1)} collective-permute-done((bf16[72,512]{1,0:T(8,128)(2,1)S(1)}, bf16[72,512]{1,0:T(8,128)(2,1)S(1)}, u32[]{:S(2)}, u32[]{:S(2)}) %collective-permute-start.21) | collective-permute-done | bytes 73760 | tf_op jit(solution)/shard_map/ppermute | solution.py:456
  95.4 1.9 %collective-permute-done.23.refs_5_ = bf16[520,512]{1,0:T(8,128)(2,1)S(1)} collective-permute-done((bf16[520,512]{1,0:T(8,128)(2,1)S(1)}, bf16[520,512]{1,0:T(8,128)(2,1)S(1)}, u32[]{:S(2)}, u32[]{:S(2)}) %collective-permute-start.23) | collective-permute-done | bytes 532512 | tf_op jit(solution)/shard_map/ppermute | solution.py:606
  98.7 2.6 %collective-permute-start.24 = (bf16[64,640]{1,0:T(8,128)(2,1)S(1)}, bf16[64,640]{1,0:T(8,128)(2,1)S(1)}, u32[]{:S(2)}, u32[]{:S(2)}) collective-permute-start(bf16[64,640]{1,0:T(8,128)(2,1)S(1)} %get-tuple-element.36), channel_id=1, source_target_pairs={{0,32},{16,48},{32,0},{48,16},{1,33},{17,49},{33,1},{49,17},{2,34}... | collective-permute-start | bytes 245768 | tf_op jit(solution)/shard_map/ppermute | solution.py:446
  103.3 1.5 %collective-permute-done.24.b1 = bf16[64,640]{1,0:T(8,128)(2,1)S(1)} collective-permute-done((bf16[64,640]{1,0:T(8,128)(2,1)S(1)}, bf16[64,640]{1,0:T(8,128)(2,1)S(1)}, u32[]{:S(2)}, u32[]{:S(2)}) %collective-permute-start.24) | collective-permute-done | bytes 81952 | tf_op jit(solution)/shard_map/ppermute | solution.py:446
  104.8 2.1 %collective-permute-done.25.b2 = bf16[64,640]{1,0:T(8,128)(2,1)S(1)} collective-permute-done((bf16[64,640]{1,0:T(8,128)(2,1)S(1)}, bf16[64,640]{1,0:T(8,128)(2,1)S(1)}, u32[]{:S(2)}, u32[]{:S(2)}) %collective-permute-start.25) | collective-permute-done | bytes 81952 | tf_op jit(solution)/shard_map/ppermute | solution.py:446
  (94 shorter events, 24.9 us)
Async XLA Ops:
  0.0 6.3 %collective-permute-start = (bf16[64,512]{1,0:T(8,128)(2,1)}, bf16[64,512]{1,0:T(8,128)(2,1)S(1)}, u32[]{:S(2)}, u32[]{:S(2)}) collective-permute-start(bf16[64,512]{1,0:T(8,128)(2,1)} %bitcast.9), channel_id=1, source_target_pairs={{0,128},{64,192},{128,0},{192,64},{1,129},{65,193},{129,1},{193,65... | collective-permute-start | bytes 196616 | tf_op jit(solution)/shard_map/ppermute | solution.py:446
  3.5 5.7 %collective-permute-start.2 = (bf16[64,512]{1,0:T(8,128)(2,1)}, bf16[64,512]{1,0:T(8,128)(2,1)S(1)}, u32[]{:S(2)}, u32[]{:S(2)}) collective-permute-start(bf16[64,512]{1,0:T(8,128)(2,1)} %bitcast.11), channel_id=1, source_target_pairs={{0,192},{64,0},{128,64},{192,128},{1,193},{65,1},{129,65},{193,129... | collective-permute-start | bytes 196616 | tf_op jit(solution)/shard_map/ppermute | solution.py:446
  10.2 13.9 %collective-permute-start.3 = (bf16[4,16,512]{2,1,0:T(8,128)(2,1)S(1)}, bf16[4,16,512]{2,1,0:T(8,128)(2,1)S(1)}, u32[]{:S(2)}, u32[]{:S(2)}) collective-permute-start(bf16[4,16,512]{2,1,0:T(8,128)(2,1)S(1)} %get-tuple-element.22), channel_id=1, source_target_pairs={{0,8},{8,16},{16,24},{24,32},{32,40},{40,48},{48,56},{56,0},{1,9},... | collective-permute-start | bytes 196616 | tf_op jit(solution)/shard_map/ppermute | solution.py:462
  10.2 13.9 %collective-permute-start.4 = (bf16[4,16,512]{2,1,0:T(8,128)(2,1)S(1)}, bf16[4,16,512]{2,1,0:T(8,128)(2,1)S(1)}, u32[]{:S(2)}, u32[]{:S(2)}) collective-permute-start(bf16[4,16,512]{2,1,0:T(8,128)(2,1)S(1)} %get-tuple-element.23), channel_id=1, source_target_pairs={{0,56},{8,0},{16,8},{24,16},{32,24},{40,32},{48,40},{56,48},{1,57}... | collective-permute-start | bytes 196616 | tf_op jit(solution)/shard_map/ppermute | solution.py:462
  13.2 20.4 %all-to-all-start = ((f32[64,1,128]{2,1,0:T(1,128)}), f32[64,1,128]{2,1,0:T(1,128)S(1)}, u32[]{:S(2)}, u32[]{:S(2)}) async-start(f32[64,1,128]{2,1,0:T(1,128)} %get-tuple-element.26), calls=%async_computation | async-start | bytes 65536 | tf_op jit(solution)/shard_map/all_to_all | solution.py:466
  24.2 9.3 %collective-permute-start.5 = (bf16[4,24,512]{2,1,0:T(8,128)(2,1)S(1)}, bf16[4,24,512]{2,1,0:T(8,128)(2,1)S(1)}, u32[]{:S(2)}, u32[]{:S(2)}) collective-permute-start(bf16[4,24,512]{2,1,0:T(8,128)(2,1)S(1)} %get-tuple-element.24), channel_id=1, source_target_pairs={{0,1},{1,2},{2,3},{3,4},{4,5},{5,6},{6,7},{7,0},{8,9},{9,10},{10,1... | collective-permute-start | bytes 294920 | tf_op jit(solution)/shard_map/ppermute | solution.py:462
  25.9 7.7 %collective-permute-start.6 = (bf16[4,24,512]{2,1,0:T(8,128)(2,1)S(1)}, bf16[4,24,512]{2,1,0:T(8,128)(2,1)S(1)}, u32[]{:S(2)}, u32[]{:S(2)}) collective-permute-start(bf16[4,24,512]{2,1,0:T(8,128)(2,1)S(1)} %get-tuple-element.25), channel_id=1, source_target_pairs={{0,7},{1,0},{2,1},{3,2},{4,3},{5,4},{6,5},{7,6},{8,15},{9,8},{10,9... | collective-permute-start | bytes 294920 | tf_op jit(solution)/shard_map/ppermute | solution.py:462
  55.6 7.3 %collective-permute-start.9 = (bf16[4,104,128]{2,1,0:T(8,128)(2,1)S(1)}, bf16[4,104,128]{2,1,0:T(8,128)(2,1)S(1)}, u32[]{:S(2)}, u32[]{:S(2)}) collective-permute-start(bf16[4,104,128]{2,1,0:T(8,128)(2,1)S(1)} %shard_map.177.s0), channel_id=1, source_target_pairs={{0,128},{64,192},{128,0},{192,64},{1,129},{65,193},{129,1},{193,65... | collective-permute-start | bytes 319496 | tf_op jit(solution)/shard_map/ppermute | solution.py:446
  55.7 8.3 %collective-permute-start.7 = (bf16[4,104,128]{2,1,0:T(8,128)(2,1)S(1)}, bf16[4,104,128]{2,1,0:T(8,128)(2,1)S(1)}, u32[]{:S(2)}, u32[]{:S(2)}) collective-permute-start(bf16[4,104,128]{2,1,0:T(8,128)(2,1)S(1)} %shard_map.177.s0), channel_id=1, source_target_pairs={{0,64},{64,128},{128,192},{192,0},{1,65},{65,129},{129,193},{193,1... | collective-permute-start | bytes 319496 | tf_op jit(solution)/shard_map/ppermute | solution.py:446
  57.1 6.8 %collective-permute-start.8 = (bf16[4,104,128]{2,1,0:T(8,128)(2,1)S(1)}, bf16[4,104,128]{2,1,0:T(8,128)(2,1)S(1)}, u32[]{:S(2)}, u32[]{:S(2)}) collective-permute-start(bf16[4,104,128]{2,1,0:T(8,128)(2,1)S(1)} %shard_map.177.s0), channel_id=1, source_target_pairs={{0,192},{64,0},{128,64},{192,128},{1,193},{65,1},{129,65},{193,129... | collective-permute-start | bytes 319496 | tf_op jit(solution)/shard_map/ppermute | solution.py:446
  65.5 5.4 %collective-permute-start.10 = (bf16[72,128]{1,0:T(8,128)(2,1)S(1)}, bf16[72,128]{1,0:T(8,128)(2,1)S(1)}, u32[]{:S(2)}, u32[]{:S(2)}) collective-permute-start(bf16[72,128]{1,0:T(8,128)(2,1)S(1)} %get-tuple-element.32), channel_id=1, source_target_pairs={{0,128},{64,192},{128,0},{192,64},{1,129},{65,193},{129,1},{193,65... | collective-permute-start | bytes 55304 | tf_op jit(solution)/shard_map/ppermute | solution.py:446
  65.9 5.1 %collective-permute-start.11 = (bf16[72,128]{1,0:T(8,128)(2,1)S(1)}, bf16[72,128]{1,0:T(8,128)(2,1)S(1)}, u32[]{:S(2)}, u32[]{:S(2)}) collective-permute-start(bf16[72,128]{1,0:T(8,128)(2,1)S(1)} %get-tuple-element.33), channel_id=1, source_target_pairs={{0,64},{64,128},{128,192},{192,0},{1,65},{65,129},{129,193},{193,1... | collective-permute-start | bytes 55304 | tf_op jit(solution)/shard_map/ppermute | solution.py:446
  72.1 5.9 %collective-permute-start.13 = (bf16[72,512]{1,0:T(8,128)(2,1)S(1)}, bf16[72,512]{1,0:T(8,128)(2,1)S(1)}, u32[]{:S(2)}, u32[]{:S(2)}) collective-permute-start(bf16[72,512]{1,0:T(8,128)(2,1)S(1)} %shard_map.180.refs_0_.residual_ref), channel_id=1, source_target_pairs={{0,32},{16,48},{32,0},{48,16},{1,33},{17,49},{33,1},{49,17},{2,34}... | collective-permute-start | bytes 221192 | tf_op jit(solution)/shard_map/ppermute | solution.py:446
  73.6 5.6 %collective-permute-start.14 = (bf16[72,512]{1,0:T(8,128)(2,1)S(1)}, bf16[72,512]{1,0:T(8,128)(2,1)S(1)}, u32[]{:S(2)}, u32[]{:S(2)}) collective-permute-start(bf16[72,512]{1,0:T(8,128)(2,1)S(1)} %shard_map.180.refs_0_.residual_ref), channel_id=1, source_target_pairs={{0,16},{16,32},{32,48},{48,0},{1,17},{17,33},{33,49},{49,1},{2,18}... | collective-permute-start | bytes 221192 | tf_op jit(solution)/shard_map/ppermute | solution.py:446
  79.2 7.7 %collective-permute-start.16 = (bf16[72,512]{1,0:T(8,128)(2,1)S(1)}, bf16[72,512]{1,0:T(8,128)(2,1)S(1)}, u32[]{:S(2)}, u32[]{:S(2)}) collective-permute-start(bf16[72,512]{1,0:T(8,128)(2,1)S(1)} %shard_map.181.refs_0_), channel_id=1, source_target_pairs={{0,2},{1,3},{2,4},{3,5},{4,6},{5,7},{6,0},{7,1},{8,10},{9,11},{10,... | collective-permute-start | bytes 221192 | tf_op jit(solution)/shard_map/ppermute | solution.py:455
  79.9 7.0 %collective-permute-start.17 = (bf16[72,512]{1,0:T(8,128)(2,1)S(1)}, bf16[72,512]{1,0:T(8,128)(2,1)S(1)}, u32[]{:S(2)}, u32[]{:S(2)}) collective-permute-start(bf16[72,512]{1,0:T(8,128)(2,1)S(1)} %shard_map.181.refs_0_), channel_id=1, source_target_pairs={{0,1},{1,2},{2,3},{3,4},{4,5},{5,6},{6,7},{7,0},{8,9},{9,10},{10,1... | collective-permute-start | bytes 221192 | tf_op jit(solution)/shard_map/ppermute | solution.py:455
  80.5 6.6 %collective-permute-start.18 = (bf16[72,512]{1,0:T(8,128)(2,1)S(1)}, bf16[72,512]{1,0:T(8,128)(2,1)S(1)}, u32[]{:S(2)}, u32[]{:S(2)}) collective-permute-start(bf16[72,512]{1,0:T(8,128)(2,1)S(1)} %shard_map.181.refs_0_), channel_id=1, source_target_pairs={{0,7},{1,0},{2,1},{3,2},{4,3},{5,4},{6,5},{7,6},{8,15},{9,8},{10,9... | collective-permute-start | bytes 221192 | tf_op jit(solution)/shard_map/ppermute | solution.py:455
  83.1 8.0 %collective-permute-start.19 = (bf16[72,512]{1,0:T(8,128)(2,1)S(1)}, bf16[72,512]{1,0:T(8,128)(2,1)S(1)}, u32[]{:S(2)}, u32[]{:S(2)}) collective-permute-start(bf16[72,512]{1,0:T(8,128)(2,1)S(1)} %shard_map.181.refs_0_), channel_id=1, source_target_pairs={{0,6},{1,7},{2,0},{3,1},{4,2},{5,3},{6,4},{7,5},{8,14},{9,15},{10,... | collective-permute-start | bytes 221192 | tf_op jit(solution)/shard_map/ppermute | solution.py:455
  86.9 6.5 %collective-permute-start.20 = (bf16[72,512]{1,0:T(8,128)(2,1)S(1)}, bf16[72,512]{1,0:T(8,128)(2,1)S(1)}, u32[]{:S(2)}, u32[]{:S(2)}) collective-permute-start(bf16[72,512]{1,0:T(8,128)(2,1)S(1)} %collective-permute-done.16.refs_1_), channel_id=1, source_target_pairs={{0,2},{1,3},{2,4},{3,5},{4,6},{5,7},{6,0},{7,1},{8,10},{9,11},{10,... | collective-permute-start | bytes 221192 | tf_op jit(solution)/shard_map/ppermute | solution.py:456
  86.9 8.0 %collective-permute-start.21 = (bf16[72,512]{1,0:T(8,128)(2,1)S(1)}, bf16[72,512]{1,0:T(8,128)(2,1)S(1)}, u32[]{:S(2)}, u32[]{:S(2)}) collective-permute-start(bf16[72,512]{1,0:T(8,128)(2,1)S(1)} %collective-permute-done.17.refs_2_), channel_id=1, source_target_pairs={{0,2},{1,3},{2,4},{3,5},{4,6},{5,7},{6,0},{7,1},{8,10},{9,11},{10,... | collective-permute-start | bytes 221192 | tf_op jit(solution)/shard_map/ppermute | solution.py:456
  87.2 7.8 %collective-permute-start.22 = (bf16[72,512]{1,0:T(8,128)(2,1)S(1)}, bf16[72,512]{1,0:T(8,128)(2,1)S(1)}, u32[]{:S(2)}, u32[]{:S(2)}) collective-permute-start(bf16[72,512]{1,0:T(8,128)(2,1)S(1)} %collective-permute-done.18.refs_3_), channel_id=1, source_target_pairs={{0,6},{1,7},{2,0},{3,1},{4,2},{5,3},{6,4},{7,5},{8,14},{9,15},{10,... | collective-permute-start | bytes 221192 | tf_op jit(solution)/shard_map/ppermute | solution.py:456
  98.7 6.1 %collective-permute-start.24 = (bf16[64,640]{1,0:T(8,128)(2,1)S(1)}, bf16[64,640]{1,0:T(8,128)(2,1)S(1)}, u32[]{:S(2)}, u32[]{:S(2)}) collective-permute-start(bf16[64,640]{1,0:T(8,128)(2,1)S(1)} %get-tuple-element.36), channel_id=1, source_target_pairs={{0,32},{16,48},{32,0},{48,16},{1,33},{17,49},{33,1},{49,17},{2,34}... | collective-permute-start | bytes 245768 | tf_op jit(solution)/shard_map/ppermute | solution.py:446
  101.3 5.6 %collective-permute-start.25 = (bf16[64,640]{1,0:T(8,128)(2,1)S(1)}, bf16[64,640]{1,0:T(8,128)(2,1)S(1)}, u32[]{:S(2)}, u32[]{:S(2)}) collective-permute-start(bf16[64,640]{1,0:T(8,128)(2,1)S(1)} %get-tuple-element.37), channel_id=1, source_target_pairs={{0,48},{16,0},{32,16},{48,32},{1,49},{17,1},{33,17},{49,33},{2,50}... | collective-permute-start | bytes 245768 | tf_op jit(solution)/shard_map/ppermute | solution.py:446
  102.4 5.7 %collective-permute-start.26 = (bf16[64,640]{1,0:T(8,128)(2,1)S(1)}, bf16[64,640]{1,0:T(8,128)(2,1)S(1)}, u32[]{:S(2)}, u32[]{:S(2)}) collective-permute-start(bf16[64,640]{1,0:T(8,128)(2,1)S(1)} %get-tuple-element.38), channel_id=1, source_target_pairs={{0,16},{16,32},{32,48},{48,0},{1,17},{17,33},{33,49},{49,1},{2,18}... | collective-permute-start | bytes 245768 | tf_op jit(solution)/shard_map/ppermute | solution.py:446
  (22 other events, 226.8 us)

commit v5 on v4

--- a/solution.py
+++ b/solution.py
@@ -450,10 +450,13 @@
     return spread_out([block] * 4, axis)
 
 
-def relayed(block, axis):
-    count = lax.axis_size(axis)
-    after = {step: lax.ppermute(block, axis, ring(count, step)) for step in (2, 1, -1, -2)}
-    further = [lax.ppermute(after[step], axis, ring(count, move)) for step, move in ((2, 2), (1, 2), (-1, -2))]
+def relayed(block):
+    def moved(x, step):
+        pairs = [(z, (z + step) % 8) for z in range(8)] + [(8 + z, 8 + (z - step) % 8) for z in range(8)]
+        return lax.ppermute(x, ("core", "z"), pairs)
+
+    after = {step: moved(block, step) for step in (2, 1, -1, -2)}
+    further = [moved(after[step], move) for step, move in ((2, 2), (1, 2), (-1, -2))]
     return [block, *after.values(), *further]
 
 
@@ -594,7 +597,7 @@
     )
     asked = around(residual, "y")
     told = call(merge_kernel, bf(cells + 8, channels), [VMEM] * 4, [], 10**6, *asked)
-    told = call(merge_kernel, bf(8 * cells + 8, channels), [VMEM] * 8, [], 10**6, *relayed(told, "z"))
+    told = call(merge_kernel, bf(8 * cells + 8, channels), [VMEM] * 8, [], 10**6, *relayed(told))
     packed = call(
         attention_kernel,
         (bf(cells, channels + LANES),) * 4,

time: 110 us -> 110 us (level)
  no operation moved by 1% of the time
where the time goes in v5:
time: 110 us; the launch traced here: 109 us
  starting transfers between devices  44.8 us (41%)
  waiting for transfers between devices  33.9 us (31%)
  blocking collectives  16.8 us (15%)
  Pallas kernels  10.4 us (9%)
  local copies, waits for them, and re-layouts  2.75 us (2%)
    ppermute x15, waiting for transfers between devices, spread_out(): lax.ppermute(b, axis, ring(4, sign * s))  20.5 us
    ppermute x15, starting transfers between devices, spread_out(): lax.ppermute(b, axis, ring(4, sign * s))  16.9 us
    all_to_all x1, blocking collectives, over_tiles(): lax.all_to_all(rows, HA + ('z',), split_axis=0, concat_axis=0, tiled=True)  16.8 us
    all_to_all x1, starting transfers between devices, over_tiles(): lax.all_to_all(rows, HA + ('z',), split_axis=0, concat_axis=0, tiled=True)  10.9 us
    ppermute x7, starting transfers between devices, moved(): return lax.ppermute(x, ('core', 'z'), pairs)  10.5 us
    pallas_call x13, Pallas kernels, call(): pl.pallas_call(kernel, out_shape=out_shape, in_specs=specs, out_specs=tup...  10.4 us
    all_to_all x1, waiting for transfers between devices, over_tiles(): lax.all_to_all(rows, HA + ('z',), split_axis=0, concat_axis=0, tiled=True)  6.01 us
    ppermute x7, waiting for transfers between devices, moved(): return lax.ppermute(x, ('core', 'z'), pairs)  5.49 us
  transfers between devices with their start and end apart: 28, of which 15 were waited for; matrix products, arithmetic and copies ran while one was open for 0% of the time, Pallas kernels for 1%

profile of v5, /device:TPU:6, one launch (start us, length us, event | category | flops | bytes accessed | tf_op | source)
XLA Modules:
  0.0 109.0 jit_solution(4893315224646413343)
XLA Ops:
  1.4 2.1 %collective-permute-start.1 = (bf16[64,512]{1,0:T(8,128)(2,1)}, bf16[64,512]{1,0:T(8,128)(2,1)S(1)}, u32[]{:S(2)}, u32[]{:S(2)}) collective-permute-start(bf16[64,512]{1,0:T(8,128)(2,1)} %bitcast.10), channel_id=1, source_target_pairs={{0,64},{64,128},{128,192},{192,0},{1,65},{65,129},{129,193},{193,1... | collective-permute-start | bytes 196616 | tf_op jit(solution)/shard_map/ppermute | solution.py:446
  6.4 2.8 %collective-permute-done.2.s3 = bf16[64,512]{1,0:T(8,128)(2,1)S(1)} collective-permute-done((bf16[64,512]{1,0:T(8,128)(2,1)}, bf16[64,512]{1,0:T(8,128)(2,1)S(1)}, u32[]{:S(2)}, u32[]{:S(2)}) %collective-permute-start.2) | collective-permute-done | bytes 65568 | tf_op jit(solution)/shard_map/ppermute | solution.py:446
  10.2 3.0 %collective-permute-start.4 = (bf16[4,16,512]{2,1,0:T(8,128)(2,1)S(1)}, bf16[4,16,512]{2,1,0:T(8,128)(2,1)S(1)}, u32[]{:S(2)}, u32[]{:S(2)}) collective-permute-start(bf16[4,16,512]{2,1,0:T(8,128)(2,1)S(1)} %get-tuple-element.23), channel_id=1, source_target_pairs={{0,56},{8,0},{16,8},{24,16},{32,24},{40,32},{48,40},{56,48},{1,57}... | collective-permute-start | bytes 196616 | tf_op jit(solution)/shard_map/ppermute | solution.py:465
  13.2 10.9 %all-to-all-start = ((f32[64,1,128]{2,1,0:T(1,128)}), f32[64,1,128]{2,1,0:T(1,128)S(1)}, u32[]{:S(2)}, u32[]{:S(2)}) async-start(f32[64,1,128]{2,1,0:T(1,128)} %get-tuple-element.26), calls=%async_computation | async-start | bytes 65536 | tf_op jit(solution)/shard_map/all_to_all | solution.py:469
  24.2 1.6 %collective-permute-start.5 = (bf16[4,24,512]{2,1,0:T(8,128)(2,1)S(1)}, bf16[4,24,512]{2,1,0:T(8,128)(2,1)S(1)}, u32[]{:S(2)}, u32[]{:S(2)}) collective-permute-start(bf16[4,24,512]{2,1,0:T(8,128)(2,1)S(1)} %get-tuple-element.24), channel_id=1, source_target_pairs={{0,1},{1,2},{2,3},{3,4},{4,5},{5,6},{6,7},{7,0},{8,9},{9,10},{10,1... | collective-permute-start | bytes 294920 | tf_op jit(solution)/shard_map/ppermute | solution.py:465
  25.9 1.7 %collective-permute-start.6 = (bf16[4,24,512]{2,1,0:T(8,128)(2,1)S(1)}, bf16[4,24,512]{2,1,0:T(8,128)(2,1)S(1)}, u32[]{:S(2)}, u32[]{:S(2)}) collective-permute-start(bf16[4,24,512]{2,1,0:T(8,128)(2,1)S(1)} %get-tuple-element.25), channel_id=1, source_target_pairs={{0,7},{1,0},{2,1},{3,2},{4,3},{5,4},{6,5},{7,6},{8,15},{9,8},{10,9... | collective-permute-start | bytes 294920 | tf_op jit(solution)/shard_map/ppermute | solution.py:465
  27.6 6.0 %all-to-all-done.rows_ref = f32[64,1,128]{2,1,0:T(1,128)S(1)} async-done(((f32[64,1,128]{2,1,0:T(1,128)}), f32[64,1,128]{2,1,0:T(1,128)S(1)}, u32[]{:S(2)}, u32[]{:S(2)}) %all-to-all-start) | async-done | bytes 32800 | tf_op jit(solution)/shard_map/all_to_all | solution.py:469
  35.6 2.9 %shard_map.176 = (bf16[4,104,128]{2,1,0:T(8,128)(2,1)S(1)}, f32[64,1,128]{2,1,0:T(1,128)S(1)}) custom-call(bf16[576,1536]{1,0:T(8,128)(2,1)S(1)} %get-tuple-element.27.lhs, f32[38,128]{1,0:T(8,128)S(1)} %bitcast.4, bf16[27,512,128]{2,1,0:T(8,128)(2,1)S(1)} %copy-done.3), custom_call_target="tpu_custom_call" | custom-call | flops 2000000000 | bytes 5467136 | tf_op jit(solution)/shard_map/pallas_call | solution.py:430
  38.5 16.8 %all_to_all.10.rows_ref = f32[64,1,128]{2,1,0:T(1,128)S(1)} all-to-all(f32[64,1,128]{2,1,0:T(1,128)S(1)} %get-tuple-element.29), channel_id=1, replica_groups=mesh['ta'=4,'y'=4,'core'=2,'z'=8] {'y','core','z'}, dimensions={0} | all-to-all | bytes 65536 | tf_op jit(solution)/shard_map/all_to_all | solution.py:469
  55.7 1.5 %collective-permute-start.7 = (bf16[4,104,128]{2,1,0:T(8,128)(2,1)S(1)}, bf16[4,104,128]{2,1,0:T(8,128)(2,1)S(1)}, u32[]{:S(2)}, u32[]{:S(2)}) collective-permute-start(bf16[4,104,128]{2,1,0:T(8,128)(2,1)S(1)} %shard_map.177.s0), channel_id=1, source_target_pairs={{0,64},{64,128},{128,192},{192,0},{1,65},{65,129},{129,193},{193,1... | collective-permute-start | bytes 319496 | tf_op jit(solution)/shard_map/ppermute | solution.py:446
  57.8 5.1 %collective-permute-done.9.s1 = bf16[4,104,128]{2,1,0:T(8,128)(2,1)S(1)} collective-permute-done((bf16[4,104,128]{2,1,0:T(8,128)(2,1)S(1)}, bf16[4,104,128]{2,1,0:T(8,128)(2,1)S(1)}, u32[]{:S(2)}, u32[]{:S(2)}) %collective-permute-start.9) | collective-permute-done | bytes 106528 | tf_op jit(solution)/shard_map/ppermute | solution.py:446
  64.0 1.5 %shard_map.179 = (bf16[72,128]{1,0:T(8,128)(2,1)S(1)}, bf16[72,128]{1,0:T(8,128)(2,1)S(1)}, bf16[72,128]{1,0:T(8,128)(2,1)S(1)}, bf16[72,128]{1,0:T(8,128)(2,1)S(1)}) custom-call(bf16[4,104,128]{2,1,0:T(8,128)(2,1)S(1)} %collective-permute-done.7.s2, bf16[4,104,128]{2,1,0:T(8,128)(2,1)S(1)} %collective-permute-done.8.s3, ...), custom_call_target="tpu_custom_call" | custom-call | flops 2000000000 | bytes 5975040 | tf_op jit(solution)/shard_map/pallas_call | solution.py:430
  67.9 3.0 %collective-permute-done.10.s1 = bf16[72,128]{1,0:T(8,128)(2,1)S(1)} collective-permute-done((bf16[72,128]{1,0:T(8,128)(2,1)S(1)}, bf16[72,128]{1,0:T(8,128)(2,1)S(1)}, u32[]{:S(2)}, u32[]{:S(2)}) %collective-permute-start.10) | collective-permute-done | bytes 18464 | tf_op jit(solution)/shard_map/ppermute | solution.py:446
  74.1 2.7 %collective-permute-start.15 = (bf16[72,512]{1,0:T(8,128)(2,1)S(1)}, bf16[72,512]{1,0:T(8,128)(2,1)S(1)}, u32[]{:S(2)}, u32[]{:S(2)}) collective-permute-start(bf16[72,512]{1,0:T(8,128)(2,1)S(1)} %shard_map.180.refs_0_.residual_ref), channel_id=1, source_target_pairs={{0,48},{16,0},{32,16},{48,32},{1,49},{17,1},{33,17},{49,33},{2,50}... | collective-permute-start | bytes 221192 | tf_op jit(solution)/shard_map/ppermute | solution.py:446
  80.5 2.6 %collective-permute-start.18 = (bf16[72,512]{1,0:T(8,128)(2,1)S(1)}, bf16[72,512]{1,0:T(8,128)(2,1)S(1)}, u32[]{:S(2)}, u32[]{:S(2)}) collective-permute-start(bf16[72,512]{1,0:T(8,128)(2,1)S(1)} %shard_map.181.refs_0_), channel_id=1, source_target_pairs={{0,7},{1,0},{2,1},{3,2},{4,3},{5,4},{6,5},{7,6},{8,9},{9,10},{10,1... | collective-permute-start | bytes 221192 | tf_op jit(solution)/shard_map/ppermute | solution.py:456
  83.1 2.3 %collective-permute-start.19 = (bf16[72,512]{1,0:T(8,128)(2,1)S(1)}, bf16[72,512]{1,0:T(8,128)(2,1)S(1)}, u32[]{:S(2)}, u32[]{:S(2)}) collective-permute-start(bf16[72,512]{1,0:T(8,128)(2,1)S(1)} %shard_map.181.refs_0_), channel_id=1, source_target_pairs={{0,6},{1,7},{2,0},{3,1},{4,2},{5,3},{6,4},{7,5},{8,10},{9,11},{10,... | collective-permute-start | bytes 221192 | tf_op jit(solution)/shard_map/ppermute | solution.py:456
  85.4 1.6 %collective-permute-done.16.refs_1_ = bf16[72,512]{1,0:T(8,128)(2,1)S(1)} collective-permute-done((bf16[72,512]{1,0:T(8,128)(2,1)S(1)}, bf16[72,512]{1,0:T(8,128)(2,1)S(1)}, u32[]{:S(2)}, u32[]{:S(2)}) %collective-permute-start.16) | collective-permute-done | bytes 73760 | tf_op jit(solution)/shard_map/ppermute | solution.py:456
  87.5 3.8 %collective-permute-start.22 = (bf16[72,512]{1,0:T(8,128)(2,1)S(1)}, bf16[72,512]{1,0:T(8,128)(2,1)S(1)}, u32[]{:S(2)}, u32[]{:S(2)}) collective-permute-start(bf16[72,512]{1,0:T(8,128)(2,1)S(1)} %collective-permute-done.18.refs_3_), channel_id=1, source_target_pairs={{0,6},{1,7},{2,0},{3,1},{4,2},{5,3},{6,4},{7,5},{8,10},{9,11},{10,... | collective-permute-start | bytes 221192 | tf_op jit(solution)/shard_map/ppermute | solution.py:456
  91.3 2.3 %collective-permute-done.20.refs_5_ = bf16[72,512]{1,0:T(8,128)(2,1)S(1)} collective-permute-done((bf16[72,512]{1,0:T(8,128)(2,1)S(1)}, bf16[72,512]{1,0:T(8,128)(2,1)S(1)}, u32[]{:S(2)}, u32[]{:S(2)}) %collective-permute-start.20) | collective-permute-done | bytes 73760 | tf_op jit(solution)/shard_map/ppermute | solution.py:456
  93.6 1.5 %collective-permute-done.21.refs_6_ = bf16[72,512]{1,0:T(8,128)(2,1)S(1)} collective-permute-done((bf16[72,512]{1,0:T(8,128)(2,1)S(1)}, bf16[72,512]{1,0:T(8,128)(2,1)S(1)}, u32[]{:S(2)}, u32[]{:S(2)}) %collective-permute-start.21) | collective-permute-done | bytes 73760 | tf_op jit(solution)/shard_map/ppermute | solution.py:456
  95.6 1.9 %collective-permute-done.23.refs_5_ = bf16[520,512]{1,0:T(8,128)(2,1)S(1)} collective-permute-done((bf16[520,512]{1,0:T(8,128)(2,1)S(1)}, bf16[520,512]{1,0:T(8,128)(2,1)S(1)}, u32[]{:S(2)}, u32[]{:S(2)}) %collective-permute-start.23) | collective-permute-done | bytes 532512 | tf_op jit(solution)/shard_map/ppermute | solution.py:609
  98.9 2.1 %collective-permute-start.24 = (bf16[64,640]{1,0:T(8,128)(2,1)S(1)}, bf16[64,640]{1,0:T(8,128)(2,1)S(1)}, u32[]{:S(2)}, u32[]{:S(2)}) collective-permute-start(bf16[64,640]{1,0:T(8,128)(2,1)S(1)} %get-tuple-element.36), channel_id=1, source_target_pairs={{0,32},{16,48},{32,0},{48,16},{1,33},{17,49},{33,1},{49,17},{2,34}... | collective-permute-start | bytes 245768 | tf_op jit(solution)/shard_map/ppermute | solution.py:446
  103.0 2.0 %collective-permute-done.24.b1 = bf16[64,640]{1,0:T(8,128)(2,1)S(1)} collective-permute-done((bf16[64,640]{1,0:T(8,128)(2,1)S(1)}, bf16[64,640]{1,0:T(8,128)(2,1)S(1)}, u32[]{:S(2)}, u32[]{:S(2)}) %collective-permute-start.24) | collective-permute-done | bytes 81952 | tf_op jit(solution)/shard_map/ppermute | solution.py:446
  105.0 2.2 %collective-permute-done.25.b2 = bf16[64,640]{1,0:T(8,128)(2,1)S(1)} collective-permute-done((bf16[64,640]{1,0:T(8,128)(2,1)S(1)}, bf16[64,640]{1,0:T(8,128)(2,1)S(1)}, u32[]{:S(2)}, u32[]{:S(2)}) %collective-permute-start.25) | collective-permute-done | bytes 81952 | tf_op jit(solution)/shard_map/ppermute | solution.py:446
  (94 shorter events, 24.8 us)
Async XLA Ops:
  0.0 6.3 %collective-permute-start = (bf16[64,512]{1,0:T(8,128)(2,1)}, bf16[64,512]{1,0:T(8,128)(2,1)S(1)}, u32[]{:S(2)}, u32[]{:S(2)}) collective-permute-start(bf16[64,512]{1,0:T(8,128)(2,1)} %bitcast.9), channel_id=1, source_target_pairs={{0,128},{64,192},{128,0},{192,64},{1,129},{65,193},{129,1},{193,65... | collective-permute-start | bytes 196616 | tf_op jit(solution)/shard_map/ppermute | solution.py:446
  3.5 5.7 %collective-permute-start.2 = (bf16[64,512]{1,0:T(8,128)(2,1)}, bf16[64,512]{1,0:T(8,128)(2,1)S(1)}, u32[]{:S(2)}, u32[]{:S(2)}) collective-permute-start(bf16[64,512]{1,0:T(8,128)(2,1)} %bitcast.11), channel_id=1, source_target_pairs={{0,192},{64,0},{128,64},{192,128},{1,193},{65,1},{129,65},{193,129... | collective-permute-start | bytes 196616 | tf_op jit(solution)/shard_map/ppermute | solution.py:446
  10.2 13.9 %collective-permute-start.3 = (bf16[4,16,512]{2,1,0:T(8,128)(2,1)S(1)}, bf16[4,16,512]{2,1,0:T(8,128)(2,1)S(1)}, u32[]{:S(2)}, u32[]{:S(2)}) collective-permute-start(bf16[4,16,512]{2,1,0:T(8,128)(2,1)S(1)} %get-tuple-element.22), channel_id=1, source_target_pairs={{0,8},{8,16},{16,24},{24,32},{32,40},{40,48},{48,56},{56,0},{1,9},... | collective-permute-start | bytes 196616 | tf_op jit(solution)/shard_map/ppermute | solution.py:465
  10.2 13.9 %collective-permute-start.4 = (bf16[4,16,512]{2,1,0:T(8,128)(2,1)S(1)}, bf16[4,16,512]{2,1,0:T(8,128)(2,1)S(1)}, u32[]{:S(2)}, u32[]{:S(2)}) collective-permute-start(bf16[4,16,512]{2,1,0:T(8,128)(2,1)S(1)} %get-tuple-element.23), channel_id=1, source_target_pairs={{0,56},{8,0},{16,8},{24,16},{32,24},{40,32},{48,40},{56,48},{1,57}... | collective-permute-start | bytes 196616 | tf_op jit(solution)/shard_map/ppermute | solution.py:465
  13.2 20.4 %all-to-all-start = ((f32[64,1,128]{2,1,0:T(1,128)}), f32[64,1,128]{2,1,0:T(1,128)S(1)}, u32[]{:S(2)}, u32[]{:S(2)}) async-start(f32[64,1,128]{2,1,0:T(1,128)} %get-tuple-element.26), calls=%async_computation | async-start | bytes 65536 | tf_op jit(solution)/shard_map/all_to_all | solution.py:469
  24.2 9.3 %collective-permute-start.5 = (bf16[4,24,512]{2,1,0:T(8,128)(2,1)S(1)}, bf16[4,24,512]{2,1,0:T(8,128)(2,1)S(1)}, u32[]{:S(2)}, u32[]{:S(2)}) collective-permute-start(bf16[4,24,512]{2,1,0:T(8,128)(2,1)S(1)} %get-tuple-element.24), channel_id=1, source_target_pairs={{0,1},{1,2},{2,3},{3,4},{4,5},{5,6},{6,7},{7,0},{8,9},{9,10},{10,1... | collective-permute-start | bytes 294920 | tf_op jit(solution)/shard_map/ppermute | solution.py:465
  25.9 7.7 %collective-permute-start.6 = (bf16[4,24,512]{2,1,0:T(8,128)(2,1)S(1)}, bf16[4,24,512]{2,1,0:T(8,128)(2,1)S(1)}, u32[]{:S(2)}, u32[]{:S(2)}) collective-permute-start(bf16[4,24,512]{2,1,0:T(8,128)(2,1)S(1)} %get-tuple-element.25), channel_id=1, source_target_pairs={{0,7},{1,0},{2,1},{3,2},{4,3},{5,4},{6,5},{7,6},{8,15},{9,8},{10,9... | collective-permute-start | bytes 294920 | tf_op jit(solution)/shard_map/ppermute | solution.py:465
  55.6 7.3 %collective-permute-start.9 = (bf16[4,104,128]{2,1,0:T(8,128)(2,1)S(1)}, bf16[4,104,128]{2,1,0:T(8,128)(2,1)S(1)}, u32[]{:S(2)}, u32[]{:S(2)}) collective-permute-start(bf16[4,104,128]{2,1,0:T(8,128)(2,1)S(1)} %shard_map.177.s0), channel_id=1, source_target_pairs={{0,128},{64,192},{128,0},{192,64},{1,129},{65,193},{129,1},{193,65... | collective-permute-start | bytes 319496 | tf_op jit(solution)/shard_map/ppermute | solution.py:446
  55.7 8.3 %collective-permute-start.7 = (bf16[4,104,128]{2,1,0:T(8,128)(2,1)S(1)}, bf16[4,104,128]{2,1,0:T(8,128)(2,1)S(1)}, u32[]{:S(2)}, u32[]{:S(2)}) collective-permute-start(bf16[4,104,128]{2,1,0:T(8,128)(2,1)S(1)} %shard_map.177.s0), channel_id=1, source_target_pairs={{0,64},{64,128},{128,192},{192,0},{1,65},{65,129},{129,193},{193,1... | collective-permute-start | bytes 319496 | tf_op jit(solution)/shard_map/ppermute | solution.py:446
  57.1 6.8 %collective-permute-start.8 = (bf16[4,104,128]{2,1,0:T(8,128)(2,1)S(1)}, bf16[4,104,128]{2,1,0:T(8,128)(2,1)S(1)}, u32[]{:S(2)}, u32[]{:S(2)}) collective-permute-start(bf16[4,104,128]{2,1,0:T(8,128)(2,1)S(1)} %shard_map.177.s0), channel_id=1, source_target_pairs={{0,192},{64,0},{128,64},{192,128},{1,193},{65,1},{129,65},{193,129... | collective-permute-start | bytes 319496 | tf_op jit(solution)/shard_map/ppermute | solution.py:446
  65.5 5.4 %collective-permute-start.10 = (bf16[72,128]{1,0:T(8,128)(2,1)S(1)}, bf16[72,128]{1,0:T(8,128)(2,1)S(1)}, u32[]{:S(2)}, u32[]{:S(2)}) collective-permute-start(bf16[72,128]{1,0:T(8,128)(2,1)S(1)} %get-tuple-element.32), channel_id=1, source_target_pairs={{0,128},{64,192},{128,0},{192,64},{1,129},{65,193},{129,1},{193,65... | collective-permute-start | bytes 55304 | tf_op jit(solution)/shard_map/ppermute | solution.py:446
  65.9 5.1 %collective-permute-start.11 = (bf16[72,128]{1,0:T(8,128)(2,1)S(1)}, bf16[72,128]{1,0:T(8,128)(2,1)S(1)}, u32[]{:S(2)}, u32[]{:S(2)}) collective-permute-start(bf16[72,128]{1,0:T(8,128)(2,1)S(1)} %get-tuple-element.33), channel_id=1, source_target_pairs={{0,64},{64,128},{128,192},{192,0},{1,65},{65,129},{129,193},{193,1... | collective-permute-start | bytes 55304 | tf_op jit(solution)/shard_map/ppermute | solution.py:446
  72.1 5.9 %collective-permute-start.13 = (bf16[72,512]{1,0:T(8,128)(2,1)S(1)}, bf16[72,512]{1,0:T(8,128)(2,1)S(1)}, u32[]{:S(2)}, u32[]{:S(2)}) collective-permute-start(bf16[72,512]{1,0:T(8,128)(2,1)S(1)} %shard_map.180.refs_0_.residual_ref), channel_id=1, source_target_pairs={{0,32},{16,48},{32,0},{48,16},{1,33},{17,49},{33,1},{49,17},{2,34}... | collective-permute-start | bytes 221192 | tf_op jit(solution)/shard_map/ppermute | solution.py:446
  73.6 5.6 %collective-permute-start.14 = (bf16[72,512]{1,0:T(8,128)(2,1)S(1)}, bf16[72,512]{1,0:T(8,128)(2,1)S(1)}, u32[]{:S(2)}, u32[]{:S(2)}) collective-permute-start(bf16[72,512]{1,0:T(8,128)(2,1)S(1)} %shard_map.180.refs_0_.residual_ref), channel_id=1, source_target_pairs={{0,16},{16,32},{32,48},{48,0},{1,17},{17,33},{33,49},{49,1},{2,18}... | collective-permute-start | bytes 221192 | tf_op jit(solution)/shard_map/ppermute | solution.py:446
  79.2 7.9 %collective-permute-start.16 = (bf16[72,512]{1,0:T(8,128)(2,1)S(1)}, bf16[72,512]{1,0:T(8,128)(2,1)S(1)}, u32[]{:S(2)}, u32[]{:S(2)}) collective-permute-start(bf16[72,512]{1,0:T(8,128)(2,1)S(1)} %shard_map.181.refs_0_), channel_id=1, source_target_pairs={{0,2},{1,3},{2,4},{3,5},{4,6},{5,7},{6,0},{7,1},{8,14},{9,15},{10,... | collective-permute-start | bytes 221192 | tf_op jit(solution)/shard_map/ppermute | solution.py:456
  79.9 7.2 %collective-permute-start.17 = (bf16[72,512]{1,0:T(8,128)(2,1)S(1)}, bf16[72,512]{1,0:T(8,128)(2,1)S(1)}, u32[]{:S(2)}, u32[]{:S(2)}) collective-permute-start(bf16[72,512]{1,0:T(8,128)(2,1)S(1)} %shard_map.181.refs_0_), channel_id=1, source_target_pairs={{0,1},{1,2},{2,3},{3,4},{4,5},{5,6},{6,7},{7,0},{8,15},{9,8},{10,9... | collective-permute-start | bytes 221192 | tf_op jit(solution)/shard_map/ppermute | solution.py:456
  80.5 7.0 %collective-permute-start.18 = (bf16[72,512]{1,0:T(8,128)(2,1)S(1)}, bf16[72,512]{1,0:T(8,128)(2,1)S(1)}, u32[]{:S(2)}, u32[]{:S(2)}) collective-permute-start(bf16[72,512]{1,0:T(8,128)(2,1)S(1)} %shard_map.181.refs_0_), channel_id=1, source_target_pairs={{0,7},{1,0},{2,1},{3,2},{4,3},{5,4},{6,5},{7,6},{8,9},{9,10},{10,1... | collective-permute-start | bytes 221192 | tf_op jit(solution)/shard_map/ppermute | solution.py:456
  83.1 8.1 %collective-permute-start.19 = (bf16[72,512]{1,0:T(8,128)(2,1)S(1)}, bf16[72,512]{1,0:T(8,128)(2,1)S(1)}, u32[]{:S(2)}, u32[]{:S(2)}) collective-permute-start(bf16[72,512]{1,0:T(8,128)(2,1)S(1)} %shard_map.181.refs_0_), channel_id=1, source_target_pairs={{0,6},{1,7},{2,0},{3,1},{4,2},{5,3},{6,4},{7,5},{8,10},{9,11},{10,... | collective-permute-start | bytes 221192 | tf_op jit(solution)/shard_map/ppermute | solution.py:456
  87.0 6.6 %collective-permute-start.20 = (bf16[72,512]{1,0:T(8,128)(2,1)S(1)}, bf16[72,512]{1,0:T(8,128)(2,1)S(1)}, u32[]{:S(2)}, u32[]{:S(2)}) collective-permute-start(bf16[72,512]{1,0:T(8,128)(2,1)S(1)} %collective-permute-done.16.refs_1_), channel_id=1, source_target_pairs={{0,2},{1,3},{2,4},{3,5},{4,6},{5,7},{6,0},{7,1},{8,14},{9,15},{10,... | collective-permute-start | bytes 221192 | tf_op jit(solution)/shard_map/ppermute | solution.py:456
  87.1 8.1 %collective-permute-start.21 = (bf16[72,512]{1,0:T(8,128)(2,1)S(1)}, bf16[72,512]{1,0:T(8,128)(2,1)S(1)}, u32[]{:S(2)}, u32[]{:S(2)}) collective-permute-start(bf16[72,512]{1,0:T(8,128)(2,1)S(1)} %collective-permute-done.17.refs_2_), channel_id=1, source_target_pairs={{0,2},{1,3},{2,4},{3,5},{4,6},{5,7},{6,0},{7,1},{8,14},{9,15},{10,... | collective-permute-start | bytes 221192 | tf_op jit(solution)/shard_map/ppermute | solution.py:456
  87.5 7.7 %collective-permute-start.22 = (bf16[72,512]{1,0:T(8,128)(2,1)S(1)}, bf16[72,512]{1,0:T(8,128)(2,1)S(1)}, u32[]{:S(2)}, u32[]{:S(2)}) collective-permute-start(bf16[72,512]{1,0:T(8,128)(2,1)S(1)} %collective-permute-done.18.refs_3_), channel_id=1, source_target_pairs={{0,6},{1,7},{2,0},{3,1},{4,2},{5,3},{6,4},{7,5},{8,10},{9,11},{10,... | collective-permute-start | bytes 221192 | tf_op jit(solution)/shard_map/ppermute | solution.py:456
  98.9 6.1 %collective-permute-start.24 = (bf16[64,640]{1,0:T(8,128)(2,1)S(1)}, bf16[64,640]{1,0:T(8,128)(2,1)S(1)}, u32[]{:S(2)}, u32[]{:S(2)}) collective-permute-start(bf16[64,640]{1,0:T(8,128)(2,1)S(1)} %get-tuple-element.36), channel_id=1, source_target_pairs={{0,32},{16,48},{32,0},{48,16},{1,33},{17,49},{33,1},{49,17},{2,34}... | collective-permute-start | bytes 245768 | tf_op jit(solution)/shard_map/ppermute | solution.py:446
  101.0 6.2 %collective-permute-start.25 = (bf16[64,640]{1,0:T(8,128)(2,1)S(1)}, bf16[64,640]{1,0:T(8,128)(2,1)S(1)}, u32[]{:S(2)}, u32[]{:S(2)}) collective-permute-start(bf16[64,640]{1,0:T(8,128)(2,1)S(1)} %get-tuple-element.37), channel_id=1, source_target_pairs={{0,48},{16,0},{32,16},{48,32},{1,49},{17,1},{33,17},{49,33},{2,50}... | collective-permute-start | bytes 245768 | tf_op jit(solution)/shard_map/ppermute | solution.py:446
  102.3 5.7 %collective-permute-start.26 = (bf16[64,640]{1,0:T(8,128)(2,1)S(1)}, bf16[64,640]{1,0:T(8,128)(2,1)S(1)}, u32[]{:S(2)}, u32[]{:S(2)}) collective-permute-start(bf16[64,640]{1,0:T(8,128)(2,1)S(1)} %get-tuple-element.38), channel_id=1, source_target_pairs={{0,16},{16,32},{32,48},{48,0},{1,17},{17,33},{33,49},{49,1},{2,18}... | collective-permute-start | bytes 245768 | tf_op jit(solution)/shard_map/ppermute | solution.py:446
  (22 other events, 226.8 us)

commit v6 on v4

--- a/solution.py
+++ b/solution.py
@@ -16,6 +16,7 @@
 LIMIT = 32 * 1024 * 1024
 SHIFTS = (0, 2, 1, 3)
 PAIRS = ((0, 1), (2, 3), (4, 5), (6, 7), (8,))
+FOURS = ((0, 1, 2, 3), (4, 5, 6, 7), (8,))
 VMEM = pl.BlockSpec(memory_space=pltpu.VMEM)
 
 
@@ -198,11 +199,11 @@
 
 
 def convolve(lhs, weights, product, frame_rows, pitch, out_rows):
-    for pair in PAIRS:
+    for four in FOURS:
         rhs = jnp.concatenate(
-            [jnp.concatenate([weights[9 * d + s] for s in pair], axis=1) for d in range(3)], axis=0
+            [jnp.concatenate([weights[9 * d + s] for s in four], axis=1) for d in range(3)], axis=0
         )
-        lane = pair[0] * LANES
+        lane = four[0] * LANES
         product[0 : 4 * frame_rows, lane : lane + rhs.shape[1]] = jnp.dot(
             lhs[...], rhs, preferred_element_type=F32
         )
@@ -329,7 +330,7 @@
 
 
 def second_conv_first_kernel(s0, s1, kernel_ref, out_ref, lhs):
-    add_blocks((s0, s1), SHIFTS[:2], kernel_ref, lhs, out_ref)
+    add_blocks((s0, s1), (0, 1), kernel_ref, lhs, out_ref)
 
 
 def second_conv_kernel(
@@ -349,7 +350,7 @@
     parts,
 ):
     ta = lax.axis_index("ta")
-    add_blocks((s2, s3), SHIFTS[2:], kernel_ref, lhs, product, before_ref)
+    add_blocks((s2, s3), (2, 3), kernel_ref, lhs, product, before_ref)
     totals = shifted_sums(product, 112, 10, 80)
     bias = small_ref[37:38, :]
     tiles = []
@@ -556,7 +557,7 @@
         over_tiles(rows2),
         small,
     )
-    blocks = around(act, "ta")
+    blocks = [act] + [lax.ppermute(act, "ta", ring(4, shift)) for shift in (1, 2, 3)]
     before = call(
         second_conv_first_kernel,
         jax.ShapeDtypeStruct((448, 1152), F32),

time: 110 us -> 112 us (1.018)
  waiting for transfers between devices: 33.5 us -> 35.8 us
    ppermute x0 -> x3, waiting for transfers between devices: none -> 5.3 us  [body(): lax.ppermute(act, 'ta', ring(4, shift))]
    ppermute x15 -> x12, waiting for transfers between devices: 20.3 us -> 15.9 us  [spread_out(): lax.ppermute(b, axis, ring(4, sign * s))]
    ppermute x0 -> x3, starting transfers between devices: none -> 2.1 us  [body(): lax.ppermute(act, 'ta', ring(4, shift))]
    ppermute x15 -> x12, starting transfers between devices: 17.4 us -> 15.8 us  [spread_out(): lax.ppermute(b, axis, ring(4, sign * s))]
    ppermute x4, waiting for transfers between devices: 1.51 us -> 2.87 us  [relayed(): lax.ppermute(block, axis, ring(count, step))]
  transfers between devices with their start and end apart: 28 -> 28, of which waited for: 15 -> 17; matrix products, arithmetic and copies ran while one was open for 0% -> 0% of each run, Pallas kernels for 1% -> 1%
where the time goes in v6:
time: 112 us
  starting transfers between devices  45.8 us (41%)
  waiting for transfers between devices  35.8 us (32%)
  blocking collectives  16.8 us (15%)
  Pallas kernels  10.5 us (9%)
  local copies, waits for them, and re-layouts  2.75 us (2%)
    all_to_all x1, blocking collectives, over_tiles(): lax.all_to_all(rows, HA + ('z',), split_axis=0, concat_axis=0, tiled=True)  16.8 us
    ppermute x12, waiting for transfers between devices, spread_out(): lax.ppermute(b, axis, ring(4, sign * s))  15.9 us
    ppermute x12, starting transfers between devices, spread_out(): lax.ppermute(b, axis, ring(4, sign * s))  15.8 us
    all_to_all x1, starting transfers between devices, over_tiles(): lax.all_to_all(rows, HA + ('z',), split_axis=0, concat_axis=0, tiled=True)  10.9 us
    pallas_call x13, Pallas kernels, call(): pl.pallas_call(kernel, out_shape=out_shape, in_specs=specs, out_specs=tup...  10.5 us
    ppermute x4, starting transfers between devices, relayed(): lax.ppermute(block, axis, ring(count, step))  6.24 us
    all_to_all x1, waiting for transfers between devices, over_tiles(): lax.all_to_all(rows, HA + ('z',), split_axis=0, concat_axis=0, tiled=True)  6.01 us
    ppermute x3, waiting for transfers between devices, body(): lax.ppermute(act, 'ta', ring(4, shift))  5.3 us
  transfers between devices with their start and end apart: 28, of which 17 were waited for; matrix products, arithmetic and copies ran while one was open for 0% of the time, Pallas kernels for 1%

profile of v6, /device:TPU:6, one launch (start us, length us, event | category | flops | bytes accessed | tf_op | source)
XLA Modules:
  0.0 111.9 jit_solution(11254992737088948556)
XLA Ops:
  1.4 2.1 %collective-permute-start.1 = (bf16[64,512]{1,0:T(8,128)(2,1)}, bf16[64,512]{1,0:T(8,128)(2,1)S(1)}, u32[]{:S(2)}, u32[]{:S(2)}) collective-permute-start(bf16[64,512]{1,0:T(8,128)(2,1)} %bitcast.10), channel_id=1, source_target_pairs={{0,64},{64,128},{128,192},{192,0},{1,65},{65,129},{129,193},{193,1... | collective-permute-start | bytes 196616 | tf_op jit(solution)/shard_map/ppermute | solution.py:447
  6.4 2.8 %collective-permute-done.2.s3 = bf16[64,512]{1,0:T(8,128)(2,1)S(1)} collective-permute-done((bf16[64,512]{1,0:T(8,128)(2,1)}, bf16[64,512]{1,0:T(8,128)(2,1)S(1)}, u32[]{:S(2)}, u32[]{:S(2)}) %collective-permute-start.2) | collective-permute-done | bytes 65568 | tf_op jit(solution)/shard_map/ppermute | solution.py:447
  10.2 3.0 %collective-permute-start.4 = (bf16[4,16,512]{2,1,0:T(8,128)(2,1)S(1)}, bf16[4,16,512]{2,1,0:T(8,128)(2,1)S(1)}, u32[]{:S(2)}, u32[]{:S(2)}) collective-permute-start(bf16[4,16,512]{2,1,0:T(8,128)(2,1)S(1)} %get-tuple-element.23), channel_id=1, source_target_pairs={{0,56},{8,0},{16,8},{24,16},{32,24},{40,32},{48,40},{56,48},{1,57}... | collective-permute-start | bytes 196616 | tf_op jit(solution)/shard_map/ppermute | solution.py:463
  13.2 10.9 %all-to-all-start = ((f32[64,1,128]{2,1,0:T(1,128)}), f32[64,1,128]{2,1,0:T(1,128)S(1)}, u32[]{:S(2)}, u32[]{:S(2)}) async-start(f32[64,1,128]{2,1,0:T(1,128)} %get-tuple-element.26), calls=%async_computation | async-start | bytes 65536 | tf_op jit(solution)/shard_map/all_to_all | solution.py:467
  24.2 1.6 %collective-permute-start.5 = (bf16[4,24,512]{2,1,0:T(8,128)(2,1)S(1)}, bf16[4,24,512]{2,1,0:T(8,128)(2,1)S(1)}, u32[]{:S(2)}, u32[]{:S(2)}) collective-permute-start(bf16[4,24,512]{2,1,0:T(8,128)(2,1)S(1)} %get-tuple-element.24), channel_id=1, source_target_pairs={{0,1},{1,2},{2,3},{3,4},{4,5},{5,6},{6,7},{7,0},{8,9},{9,10},{10,1... | collective-permute-start | bytes 294920 | tf_op jit(solution)/shard_map/ppermute | solution.py:463
  25.9 1.7 %collective-permute-start.6 = (bf16[4,24,512]{2,1,0:T(8,128)(2,1)S(1)}, bf16[4,24,512]{2,1,0:T(8,128)(2,1)S(1)}, u32[]{:S(2)}, u32[]{:S(2)}) collective-permute-start(bf16[4,24,512]{2,1,0:T(8,128)(2,1)S(1)} %get-tuple-element.25), channel_id=1, source_target_pairs={{0,7},{1,0},{2,1},{3,2},{4,3},{5,4},{6,5},{7,6},{8,15},{9,8},{10,9... | collective-permute-start | bytes 294920 | tf_op jit(solution)/shard_map/ppermute | solution.py:463
  27.6 6.0 %all-to-all-done.rows_ref = f32[64,1,128]{2,1,0:T(1,128)S(1)} async-done(((f32[64,1,128]{2,1,0:T(1,128)}), f32[64,1,128]{2,1,0:T(1,128)S(1)}, u32[]{:S(2)}, u32[]{:S(2)}) %all-to-all-start) | async-done | bytes 32800 | tf_op jit(solution)/shard_map/all_to_all | solution.py:467
  35.6 2.9 %shard_map.176 = (bf16[4,104,128]{2,1,0:T(8,128)(2,1)S(1)}, f32[64,1,128]{2,1,0:T(1,128)S(1)}) custom-call(bf16[576,1536]{1,0:T(8,128)(2,1)S(1)} %get-tuple-element.27.lhs, f32[38,128]{1,0:T(8,128)S(1)} %bitcast.4, bf16[27,512,128]{2,1,0:T(8,128)(2,1)S(1)} %copy-done.3), custom_call_target="tpu_custom_call" | custom-call | flops 2000000000 | bytes 5467136 | tf_op jit(solution)/shard_map/pallas_call | solution.py:431
  38.5 16.8 %all_to_all.10.rows_ref = f32[64,1,128]{2,1,0:T(1,128)S(1)} all-to-all(f32[64,1,128]{2,1,0:T(1,128)S(1)} %get-tuple-element.29), channel_id=1, replica_groups=mesh['ta'=4,'y'=4,'core'=2,'z'=8] {'y','core','z'}, dimensions={0} | all-to-all | bytes 65536 | tf_op jit(solution)/shard_map/all_to_all | solution.py:467
  57.7 3.7 %collective-permute-done.9.s1 = bf16[4,104,128]{2,1,0:T(8,128)(2,1)S(1)} collective-permute-done((bf16[4,104,128]{2,1,0:T(8,128)(2,1)S(1)}, bf16[4,104,128]{2,1,0:T(8,128)(2,1)S(1)}, u32[]{:S(2)}, u32[]{:S(2)}) %collective-permute-start.9) | collective-permute-done | bytes 106528 | tf_op jit(solution)/shard_map/ppermute | solution.py:560
  62.5 1.6 %collective-permute-done.8.s3 = bf16[4,104,128]{2,1,0:T(8,128)(2,1)S(1)} collective-permute-done((bf16[4,104,128]{2,1,0:T(8,128)(2,1)S(1)}, bf16[4,104,128]{2,1,0:T(8,128)(2,1)S(1)}, u32[]{:S(2)}, u32[]{:S(2)}) %collective-permute-start.8) | collective-permute-done | bytes 106528 | tf_op jit(solution)/shard_map/ppermute | solution.py:560
  64.1 1.5 %shard_map.179 = (bf16[72,128]{1,0:T(8,128)(2,1)S(1)}, bf16[72,128]{1,0:T(8,128)(2,1)S(1)}, bf16[72,128]{1,0:T(8,128)(2,1)S(1)}, bf16[72,128]{1,0:T(8,128)(2,1)S(1)}) custom-call(bf16[4,104,128]{2,1,0:T(8,128)(2,1)S(1)} %collective-permute-done.7.s2, bf16[4,104,128]{2,1,0:T(8,128)(2,1)S(1)} %collective-permute-done.8.s3, ...), custom_call_target="tpu_custom_call" | custom-call | flops 2000000000 | bytes 5975040 | tf_op jit(solution)/shard_map/pallas_call | solution.py:431
  66.3 1.9 %collective-permute-start.11 = (bf16[72,128]{1,0:T(8,128)(2,1)S(1)}, bf16[72,128]{1,0:T(8,128)(2,1)S(1)}, u32[]{:S(2)}, u32[]{:S(2)}) collective-permute-start(bf16[72,128]{1,0:T(8,128)(2,1)S(1)} %get-tuple-element.33), channel_id=1, source_target_pairs={{0,64},{64,128},{128,192},{192,0},{1,65},{65,129},{129,193},{193,1... | collective-permute-start | bytes 55304 | tf_op jit(solution)/shard_map/ppermute | solution.py:447
  68.4 2.6 %collective-permute-done.10.s1 = bf16[72,128]{1,0:T(8,128)(2,1)S(1)} collective-permute-done((bf16[72,128]{1,0:T(8,128)(2,1)S(1)}, bf16[72,128]{1,0:T(8,128)(2,1)S(1)}, u32[]{:S(2)}, u32[]{:S(2)}) %collective-permute-start.10) | collective-permute-done | bytes 18464 | tf_op jit(solution)/shard_map/ppermute | solution.py:447
  71.0 2.2 %collective-permute-done.12.s3 = bf16[72,128]{1,0:T(8,128)(2,1)S(1)} collective-permute-done((bf16[72,128]{1,0:T(8,128)(2,1)S(1)}, bf16[72,128]{1,0:T(8,128)(2,1)S(1)}, u32[]{:S(2)}, u32[]{:S(2)}) %collective-permute-start.12) | collective-permute-done | bytes 18464 | tf_op jit(solution)/shard_map/ppermute | solution.py:447
  75.2 2.7 %collective-permute-start.15 = (bf16[72,512]{1,0:T(8,128)(2,1)S(1)}, bf16[72,512]{1,0:T(8,128)(2,1)S(1)}, u32[]{:S(2)}, u32[]{:S(2)}) collective-permute-start(bf16[72,512]{1,0:T(8,128)(2,1)S(1)} %shard_map.180.refs_0_.residual_ref), channel_id=1, source_target_pairs={{0,48},{16,0},{32,16},{48,32},{1,49},{17,1},{33,17},{49,33},{2,50}... | collective-permute-start | bytes 221192 | tf_op jit(solution)/shard_map/ppermute | solution.py:447
  81.5 2.7 %collective-permute-start.18 = (bf16[72,512]{1,0:T(8,128)(2,1)S(1)}, bf16[72,512]{1,0:T(8,128)(2,1)S(1)}, u32[]{:S(2)}, u32[]{:S(2)}) collective-permute-start(bf16[72,512]{1,0:T(8,128)(2,1)S(1)} %shard_map.181.refs_0_), channel_id=1, source_target_pairs={{0,7},{1,0},{2,1},{3,2},{4,3},{5,4},{6,5},{7,6},{8,15},{9,8},{10,9... | collective-permute-start | bytes 221192 | tf_op jit(solution)/shard_map/ppermute | solution.py:456
  84.2 2.4 %collective-permute-start.19 = (bf16[72,512]{1,0:T(8,128)(2,1)S(1)}, bf16[72,512]{1,0:T(8,128)(2,1)S(1)}, u32[]{:S(2)}, u32[]{:S(2)}) collective-permute-start(bf16[72,512]{1,0:T(8,128)(2,1)S(1)} %shard_map.181.refs_0_), channel_id=1, source_target_pairs={{0,6},{1,7},{2,0},{3,1},{4,2},{5,3},{6,4},{7,5},{8,14},{9,15},{10,... | collective-permute-start | bytes 221192 | tf_op jit(solution)/shard_map/ppermute | solution.py:456
  86.5 2.7 %collective-permute-done.16.refs_1_ = bf16[72,512]{1,0:T(8,128)(2,1)S(1)} collective-permute-done((bf16[72,512]{1,0:T(8,128)(2,1)S(1)}, bf16[72,512]{1,0:T(8,128)(2,1)S(1)}, u32[]{:S(2)}, u32[]{:S(2)}) %collective-permute-start.16) | collective-permute-done | bytes 73760 | tf_op jit(solution)/shard_map/ppermute | solution.py:456
  89.6 3.9 %collective-permute-start.22 = (bf16[72,512]{1,0:T(8,128)(2,1)S(1)}, bf16[72,512]{1,0:T(8,128)(2,1)S(1)}, u32[]{:S(2)}, u32[]{:S(2)}) collective-permute-start(bf16[72,512]{1,0:T(8,128)(2,1)S(1)} %collective-permute-done.18.refs_3_), channel_id=1, source_target_pairs={{0,6},{1,7},{2,0},{3,1},{4,2},{5,3},{6,4},{7,5},{8,14},{9,15},{10,... | collective-permute-start | bytes 221192 | tf_op jit(solution)/shard_map/ppermute | solution.py:457
  93.6 3.0 %collective-permute-done.20.refs_5_ = bf16[72,512]{1,0:T(8,128)(2,1)S(1)} collective-permute-done((bf16[72,512]{1,0:T(8,128)(2,1)S(1)}, bf16[72,512]{1,0:T(8,128)(2,1)S(1)}, u32[]{:S(2)}, u32[]{:S(2)}) %collective-permute-start.20) | collective-permute-done | bytes 73760 | tf_op jit(solution)/shard_map/ppermute | solution.py:457
  97.7 1.9 %collective-permute-done.23.refs_5_ = bf16[520,512]{1,0:T(8,128)(2,1)S(1)} collective-permute-done((bf16[520,512]{1,0:T(8,128)(2,1)S(1)}, bf16[520,512]{1,0:T(8,128)(2,1)S(1)}, u32[]{:S(2)}, u32[]{:S(2)}) %collective-permute-start.23) | collective-permute-done | bytes 532512 | tf_op jit(solution)/shard_map/ppermute | solution.py:607
  101.0 2.9 %collective-permute-start.24 = (bf16[64,640]{1,0:T(8,128)(2,1)S(1)}, bf16[64,640]{1,0:T(8,128)(2,1)S(1)}, u32[]{:S(2)}, u32[]{:S(2)}) collective-permute-start(bf16[64,640]{1,0:T(8,128)(2,1)S(1)} %get-tuple-element.36), channel_id=1, source_target_pairs={{0,32},{16,48},{32,0},{48,16},{1,33},{17,49},{33,1},{49,17},{2,34}... | collective-permute-start | bytes 245768 | tf_op jit(solution)/shard_map/ppermute | solution.py:447
  107.1 2.4 %collective-permute-done.25.b2 = bf16[64,640]{1,0:T(8,128)(2,1)S(1)} collective-permute-done((bf16[64,640]{1,0:T(8,128)(2,1)S(1)}, bf16[64,640]{1,0:T(8,128)(2,1)S(1)}, u32[]{:S(2)}, u32[]{:S(2)}) %collective-permute-start.25) | collective-permute-done | bytes 81952 | tf_op jit(solution)/shard_map/ppermute | solution.py:447
  (94 shorter events, 25.9 us)
Async XLA Ops:
  0.0 6.3 %collective-permute-start = (bf16[64,512]{1,0:T(8,128)(2,1)}, bf16[64,512]{1,0:T(8,128)(2,1)S(1)}, u32[]{:S(2)}, u32[]{:S(2)}) collective-permute-start(bf16[64,512]{1,0:T(8,128)(2,1)} %bitcast.9), channel_id=1, source_target_pairs={{0,128},{64,192},{128,0},{192,64},{1,129},{65,193},{129,1},{193,65... | collective-permute-start | bytes 196616 | tf_op jit(solution)/shard_map/ppermute | solution.py:447
  3.5 5.7 %collective-permute-start.2 = (bf16[64,512]{1,0:T(8,128)(2,1)}, bf16[64,512]{1,0:T(8,128)(2,1)S(1)}, u32[]{:S(2)}, u32[]{:S(2)}) collective-permute-start(bf16[64,512]{1,0:T(8,128)(2,1)} %bitcast.11), channel_id=1, source_target_pairs={{0,192},{64,0},{128,64},{192,128},{1,193},{65,1},{129,65},{193,129... | collective-permute-start | bytes 196616 | tf_op jit(solution)/shard_map/ppermute | solution.py:447
  10.2 13.9 %collective-permute-start.3 = (bf16[4,16,512]{2,1,0:T(8,128)(2,1)S(1)}, bf16[4,16,512]{2,1,0:T(8,128)(2,1)S(1)}, u32[]{:S(2)}, u32[]{:S(2)}) collective-permute-start(bf16[4,16,512]{2,1,0:T(8,128)(2,1)S(1)} %get-tuple-element.22), channel_id=1, source_target_pairs={{0,8},{8,16},{16,24},{24,32},{32,40},{40,48},{48,56},{56,0},{1,9},... | collective-permute-start | bytes 196616 | tf_op jit(solution)/shard_map/ppermute | solution.py:463
  10.2 13.9 %collective-permute-start.4 = (bf16[4,16,512]{2,1,0:T(8,128)(2,1)S(1)}, bf16[4,16,512]{2,1,0:T(8,128)(2,1)S(1)}, u32[]{:S(2)}, u32[]{:S(2)}) collective-permute-start(bf16[4,16,512]{2,1,0:T(8,128)(2,1)S(1)} %get-tuple-element.23), channel_id=1, source_target_pairs={{0,56},{8,0},{16,8},{24,16},{32,24},{40,32},{48,40},{56,48},{1,57}... | collective-permute-start | bytes 196616 | tf_op jit(solution)/shard_map/ppermute | solution.py:463
  13.2 20.4 %all-to-all-start = ((f32[64,1,128]{2,1,0:T(1,128)}), f32[64,1,128]{2,1,0:T(1,128)S(1)}, u32[]{:S(2)}, u32[]{:S(2)}) async-start(f32[64,1,128]{2,1,0:T(1,128)} %get-tuple-element.26), calls=%async_computation | async-start | bytes 65536 | tf_op jit(solution)/shard_map/all_to_all | solution.py:467
  24.2 9.3 %collective-permute-start.5 = (bf16[4,24,512]{2,1,0:T(8,128)(2,1)S(1)}, bf16[4,24,512]{2,1,0:T(8,128)(2,1)S(1)}, u32[]{:S(2)}, u32[]{:S(2)}) collective-permute-start(bf16[4,24,512]{2,1,0:T(8,128)(2,1)S(1)} %get-tuple-element.24), channel_id=1, source_target_pairs={{0,1},{1,2},{2,3},{3,4},{4,5},{5,6},{6,7},{7,0},{8,9},{9,10},{10,1... | collective-permute-start | bytes 294920 | tf_op jit(solution)/shard_map/ppermute | solution.py:463
  25.9 7.7 %collective-permute-start.6 = (bf16[4,24,512]{2,1,0:T(8,128)(2,1)S(1)}, bf16[4,24,512]{2,1,0:T(8,128)(2,1)S(1)}, u32[]{:S(2)}, u32[]{:S(2)}) collective-permute-start(bf16[4,24,512]{2,1,0:T(8,128)(2,1)S(1)} %get-tuple-element.25), channel_id=1, source_target_pairs={{0,7},{1,0},{2,1},{3,2},{4,3},{5,4},{6,5},{7,6},{8,15},{9,8},{10,9... | collective-permute-start | bytes 294920 | tf_op jit(solution)/shard_map/ppermute | solution.py:463
  55.6 5.8 %collective-permute-start.9 = (bf16[4,104,128]{2,1,0:T(8,128)(2,1)S(1)}, bf16[4,104,128]{2,1,0:T(8,128)(2,1)S(1)}, u32[]{:S(2)}, u32[]{:S(2)}) collective-permute-start(bf16[4,104,128]{2,1,0:T(8,128)(2,1)S(1)} %shard_map.177.s0), channel_id=1, source_target_pairs={{0,64},{64,128},{128,192},{192,0},{1,65},{65,129},{129,193},{193,1... | collective-permute-start | bytes 319496 | tf_op jit(solution)/shard_map/ppermute | solution.py:560
  55.7 6.8 %collective-permute-start.7 = (bf16[4,104,128]{2,1,0:T(8,128)(2,1)S(1)}, bf16[4,104,128]{2,1,0:T(8,128)(2,1)S(1)}, u32[]{:S(2)}, u32[]{:S(2)}) collective-permute-start(bf16[4,104,128]{2,1,0:T(8,128)(2,1)S(1)} %shard_map.177.s0), channel_id=1, source_target_pairs={{0,128},{64,192},{128,0},{192,64},{1,129},{65,193},{129,1},{193,65... | collective-permute-start | bytes 319496 | tf_op jit(solution)/shard_map/ppermute | solution.py:560
  56.6 7.5 %collective-permute-start.8 = (bf16[4,104,128]{2,1,0:T(8,128)(2,1)S(1)}, bf16[4,104,128]{2,1,0:T(8,128)(2,1)S(1)}, u32[]{:S(2)}, u32[]{:S(2)}) collective-permute-start(bf16[4,104,128]{2,1,0:T(8,128)(2,1)S(1)} %shard_map.177.s0), channel_id=1, source_target_pairs={{0,192},{64,0},{128,64},{192,128},{1,193},{65,1},{129,65},{193,129... | collective-permute-start | bytes 319496 | tf_op jit(solution)/shard_map/ppermute | solution.py:560
  65.6 5.4 %collective-permute-start.10 = (bf16[72,128]{1,0:T(8,128)(2,1)S(1)}, bf16[72,128]{1,0:T(8,128)(2,1)S(1)}, u32[]{:S(2)}, u32[]{:S(2)}) collective-permute-start(bf16[72,128]{1,0:T(8,128)(2,1)S(1)} %get-tuple-element.32), channel_id=1, source_target_pairs={{0,128},{64,192},{128,0},{192,64},{1,129},{65,193},{129,1},{193,65... | collective-permute-start | bytes 55304 | tf_op jit(solution)/shard_map/ppermute | solution.py:447
  73.2 5.9 %collective-permute-start.13 = (bf16[72,512]{1,0:T(8,128)(2,1)S(1)}, bf16[72,512]{1,0:T(8,128)(2,1)S(1)}, u32[]{:S(2)}, u32[]{:S(2)}) collective-permute-start(bf16[72,512]{1,0:T(8,128)(2,1)S(1)} %shard_map.180.refs_0_.residual_ref), channel_id=1, source_target_pairs={{0,32},{16,48},{32,0},{48,16},{1,33},{17,49},{33,1},{49,17},{2,34}... | collective-permute-start | bytes 221192 | tf_op jit(solution)/shard_map/ppermute | solution.py:447
  74.7 5.6 %collective-permute-start.14 = (bf16[72,512]{1,0:T(8,128)(2,1)S(1)}, bf16[72,512]{1,0:T(8,128)(2,1)S(1)}, u32[]{:S(2)}, u32[]{:S(2)}) collective-permute-start(bf16[72,512]{1,0:T(8,128)(2,1)S(1)} %shard_map.180.refs_0_.residual_ref), channel_id=1, source_target_pairs={{0,16},{16,32},{32,48},{48,0},{1,17},{17,33},{33,49},{49,1},{2,18}... | collective-permute-start | bytes 221192 | tf_op jit(solution)/shard_map/ppermute | solution.py:447
  75.2 5.0 %collective-permute-start.15 = (bf16[72,512]{1,0:T(8,128)(2,1)S(1)}, bf16[72,512]{1,0:T(8,128)(2,1)S(1)}, u32[]{:S(2)}, u32[]{:S(2)}) collective-permute-start(bf16[72,512]{1,0:T(8,128)(2,1)S(1)} %shard_map.180.refs_0_.residual_ref), channel_id=1, source_target_pairs={{0,48},{16,0},{32,16},{48,32},{1,49},{17,1},{33,17},{49,33},{2,50}... | collective-permute-start | bytes 221192 | tf_op jit(solution)/shard_map/ppermute | solution.py:447
  80.3 8.9 %collective-permute-start.16 = (bf16[72,512]{1,0:T(8,128)(2,1)S(1)}, bf16[72,512]{1,0:T(8,128)(2,1)S(1)}, u32[]{:S(2)}, u32[]{:S(2)}) collective-permute-start(bf16[72,512]{1,0:T(8,128)(2,1)S(1)} %shard_map.181.refs_0_), channel_id=1, source_target_pairs={{0,2},{1,3},{2,4},{3,5},{4,6},{5,7},{6,0},{7,1},{8,10},{9,11},{10,... | collective-permute-start | bytes 221192 | tf_op jit(solution)/shard_map/ppermute | solution.py:456
  80.9 8.5 %collective-permute-start.17 = (bf16[72,512]{1,0:T(8,128)(2,1)S(1)}, bf16[72,512]{1,0:T(8,128)(2,1)S(1)}, u32[]{:S(2)}, u32[]{:S(2)}) collective-permute-start(bf16[72,512]{1,0:T(8,128)(2,1)S(1)} %shard_map.181.refs_0_), channel_id=1, source_target_pairs={{0,1},{1,2},{2,3},{3,4},{4,5},{5,6},{6,7},{7,0},{8,9},{9,10},{10,1... | collective-permute-start | bytes 221192 | tf_op jit(solution)/shard_map/ppermute | solution.py:456
  81.5 8.1 %collective-permute-start.18 = (bf16[72,512]{1,0:T(8,128)(2,1)S(1)}, bf16[72,512]{1,0:T(8,128)(2,1)S(1)}, u32[]{:S(2)}, u32[]{:S(2)}) collective-permute-start(bf16[72,512]{1,0:T(8,128)(2,1)S(1)} %shard_map.181.refs_0_), channel_id=1, source_target_pairs={{0,7},{1,0},{2,1},{3,2},{4,3},{5,4},{6,5},{7,6},{8,15},{9,8},{10,9... | collective-permute-start | bytes 221192 | tf_op jit(solution)/shard_map/ppermute | solution.py:456
  84.2 9.4 %collective-permute-start.19 = (bf16[72,512]{1,0:T(8,128)(2,1)S(1)}, bf16[72,512]{1,0:T(8,128)(2,1)S(1)}, u32[]{:S(2)}, u32[]{:S(2)}) collective-permute-start(bf16[72,512]{1,0:T(8,128)(2,1)S(1)} %shard_map.181.refs_0_), channel_id=1, source_target_pairs={{0,6},{1,7},{2,0},{3,1},{4,2},{5,3},{6,4},{7,5},{8,14},{9,15},{10,... | collective-permute-start | bytes 221192 | tf_op jit(solution)/shard_map/ppermute | solution.py:456
  89.3 7.3 %collective-permute-start.20 = (bf16[72,512]{1,0:T(8,128)(2,1)S(1)}, bf16[72,512]{1,0:T(8,128)(2,1)S(1)}, u32[]{:S(2)}, u32[]{:S(2)}) collective-permute-start(bf16[72,512]{1,0:T(8,128)(2,1)S(1)} %collective-permute-done.16.refs_1_), channel_id=1, source_target_pairs={{0,2},{1,3},{2,4},{3,5},{4,6},{5,7},{6,0},{7,1},{8,10},{9,11},{10,... | collective-permute-start | bytes 221192 | tf_op jit(solution)/shard_map/ppermute | solution.py:457
  89.4 7.9 %collective-permute-start.21 = (bf16[72,512]{1,0:T(8,128)(2,1)S(1)}, bf16[72,512]{1,0:T(8,128)(2,1)S(1)}, u32[]{:S(2)}, u32[]{:S(2)}) collective-permute-start(bf16[72,512]{1,0:T(8,128)(2,1)S(1)} %collective-permute-done.17.refs_2_), channel_id=1, source_target_pairs={{0,2},{1,3},{2,4},{3,5},{4,6},{5,7},{6,0},{7,1},{8,10},{9,11},{10,... | collective-permute-start | bytes 221192 | tf_op jit(solution)/shard_map/ppermute | solution.py:457
  89.6 7.7 %collective-permute-start.22 = (bf16[72,512]{1,0:T(8,128)(2,1)S(1)}, bf16[72,512]{1,0:T(8,128)(2,1)S(1)}, u32[]{:S(2)}, u32[]{:S(2)}) collective-permute-start(bf16[72,512]{1,0:T(8,128)(2,1)S(1)} %collective-permute-done.18.refs_3_), channel_id=1, source_target_pairs={{0,6},{1,7},{2,0},{3,1},{4,2},{5,3},{6,4},{7,5},{8,14},{9,15},{10,... | collective-permute-start | bytes 221192 | tf_op jit(solution)/shard_map/ppermute | solution.py:457
  101.0 6.1 %collective-permute-start.24 = (bf16[64,640]{1,0:T(8,128)(2,1)S(1)}, bf16[64,640]{1,0:T(8,128)(2,1)S(1)}, u32[]{:S(2)}, u32[]{:S(2)}) collective-permute-start(bf16[64,640]{1,0:T(8,128)(2,1)S(1)} %get-tuple-element.36), channel_id=1, source_target_pairs={{0,32},{16,48},{32,0},{48,16},{1,33},{17,49},{33,1},{49,17},{2,34}... | collective-permute-start | bytes 245768 | tf_op jit(solution)/shard_map/ppermute | solution.py:447
  103.9 5.6 %collective-permute-start.25 = (bf16[64,640]{1,0:T(8,128)(2,1)S(1)}, bf16[64,640]{1,0:T(8,128)(2,1)S(1)}, u32[]{:S(2)}, u32[]{:S(2)}) collective-permute-start(bf16[64,640]{1,0:T(8,128)(2,1)S(1)} %get-tuple-element.37), channel_id=1, source_target_pairs={{0,48},{16,0},{32,16},{48,32},{1,49},{17,1},{33,17},{49,33},{2,50}... | collective-permute-start | bytes 245768 | tf_op jit(solution)/shard_map/ppermute | solution.py:447
  105.2 5.7 %collective-permute-start.26 = (bf16[64,640]{1,0:T(8,128)(2,1)S(1)}, bf16[64,640]{1,0:T(8,128)(2,1)S(1)}, u32[]{:S(2)}, u32[]{:S(2)}) collective-permute-start(bf16[64,640]{1,0:T(8,128)(2,1)S(1)} %get-tuple-element.38), channel_id=1, source_target_pairs={{0,16},{16,32},{32,48},{48,0},{1,17},{17,33},{33,49},{49,1},{2,18}... | collective-permute-start | bytes 245768 | tf_op jit(solution)/shard_map/ppermute | solution.py:447
  (22 other events, 234.5 us)

commit v7 on v4

--- a/solution.py
+++ b/solution.py
@@ -137,14 +137,14 @@
 
 
 def turned(ta, s):
-    return lax.rem(ta - s + 4, 4)
+    return ta ^ s
 
 
 def first_kernel(latent_ref, out_ref):
     out_ref[...] = latent_ref[...]
 
 
-def frame_moments_kernel(s0, s1, s2, s3, out_ref, first_ref, last_ref):
+def frame_moments_kernel(s0, s1, s2, s3, out_ref, outer_ref, inner_ref):
     slots = (s0, s1, s2, s3)
     stats = []
     for block in range(4):
@@ -154,21 +154,30 @@
         stats.append((block,) + channel_stats(x, None, x.shape[0]))
     encode(out_ref, stats)
     for s, ref in zip(SHIFTS, slots):
-        first_ref[s] = ref[0:16, :]
-        last_ref[s] = ref[48:64, :]
-
-
-def columns_kernel(s0, s1, s2, s3, top_ref, bottom_ref, first_ref, last_ref, tall, sides):
+        start = 48 * lax.axis_index("core")
+        outer_ref[s] = ref[pl.ds(pl.multiple_of(start, 16), 16), :]
+        inner_ref[s] = ref[pl.ds(pl.multiple_of(48 - start, 16), 16), :]
+
+
+def above_and_below(outer_ref, inner_ref, s, lanes):
+    outer, inner = outer_ref[s, :, lanes].astype(F32), inner_ref[s, :, lanes].astype(F32)
+    upper = lax.axis_index("core") == 0
+    return jnp.where(upper, outer, inner), jnp.where(upper, inner, outer)
+
+
+def columns_kernel(s0, s1, s2, s3, outer_rows, inner_rows, outer_ref, inner_ref, tall, sides):
+    odd = lax.rem(lax.axis_index("z"), 2) == 1
     for s, ref in zip(SHIFTS, (s0, s1, s2, s3)):
         for b in range(4):
             lanes = slice(b * LANES, (b + 1) * LANES)
-            tall[b, 0:16, :] = top_ref[s, :, lanes].astype(F32)
+            tall[b, 0:16, :], tall[b, 80:96, :] = above_and_below(outer_rows, inner_rows, s, lanes)
             tall[b, 16:80, :] = ref[:, lanes].astype(F32)
-            tall[b, 80:96, :] = bottom_ref[s, :, lanes].astype(F32)
-            for k, out_ref in ((0, first_ref), (6, last_ref)):
+            for k in range(2):
                 for j in range(2):
-                    sides[b, 12 * j : 12 * j + 12, :] = tall[b, pl.ds(j + k, 12, stride=8), :]
-                out_ref[s, :, lanes] = sides[b].astype(BF)
+                    sides[k, b, 12 * j : 12 * j + 12, :] = tall[b, pl.ds(j + 6 * k, 12, stride=8), :]
+            first, last = sides[0, b], sides[1, b]
+            outer_ref[s, :, lanes] = jnp.where(odd, last, first).astype(BF)
+            inner_ref[s, :, lanes] = jnp.where(odd, first, last).astype(BF)
 
 
 def activate_kernel(grid, hidden_ref, rows_ref, small_ref, out_ref):
@@ -233,10 +242,10 @@
     s1,
     s2,
     s3,
-    top_ref,
-    bottom_ref,
-    left_ref,
-    right_ref,
+    outer_rows,
+    inner_rows,
+    outer_columns,
+    inner_columns,
     rows_ref,
     small_ref,
     lhs_ref,
@@ -246,6 +255,7 @@
     sides,
 ):
     ta = lax.axis_index("ta")
+    odd = lax.rem(lax.axis_index("z"), 2) == 1
     coefficients = decode(rows_ref, small_ref, 0)
     keep = inside(8 * lax.axis_index(HA) - 2, 8 * lax.axis_index("z") - 2, 144, 12, grid)
     for s, ref in zip(SHIFTS, (s0, s1, s2, s3)):
@@ -257,7 +267,7 @@
             lanes = slice(b * LANES, (b + 1) * LANES)
             middle = frames[frame, :, lanes].astype(F32)
             own = jnp.where(ta == b, middle, own)
-            top, bottom = top_ref[s, :, lanes].astype(F32), bottom_ref[s, :, lanes].astype(F32)
+            top, bottom = above_and_below(outer_rows, inner_rows, s, lanes)
             for r in range(12):
                 if r < 2:
                     piece = top[8 * r : 8 * r + 8]
@@ -266,10 +276,12 @@
                 else:
                     piece = bottom[8 * (r - 10) : 8 * (r - 10) + 8]
                 tile[b, 12 * r + 2 : 12 * r + 10, :] = piece
-            for k, side_ref in ((0, left_ref), (10, right_ref)):
-                sides[b] = side_ref[s, :, lanes].astype(F32)
+            outer, inner = outer_columns[s, :, lanes].astype(F32), inner_columns[s, :, lanes].astype(F32)
+            sides[0, b] = jnp.where(odd, inner, outer)
+            sides[1, b] = jnp.where(odd, outer, inner)
+            for k in range(2):
                 for j in range(2):
-                    tile[b, pl.ds(j + k, 12, stride=12), :] = sides[b, 12 * j : 12 * j + 12, :]
+                    tile[b, pl.ds(j + 10 * k, 12, stride=12), :] = sides[k, b, 12 * j : 12 * j + 12, :]
             mean, scale, shift = coefficients[b]
             v = (tile[b] - mean) * scale + shift
             act = jnp.where(keep, silu(v), 0.0).astype(BF)
@@ -363,7 +375,7 @@
     mean, spread = channel_stats(jnp.concatenate(tiles, axis=0), None, 256)
     packed = pack_stats(mean, spread)
     for s, ref in zip(SHIFTS, (out0, out1, out2, out3)):
-        ref[0:64, :] = parts[lax.rem(ta + s, 4)]
+        ref[0:64, :] = parts[turned(ta, s)]
         ref[64:72, :] = packed
 
 
@@ -442,8 +454,10 @@
     return [(i, (i + step) % count) for i in range(count)]
 
 
-def spread_out(blocks, axis, sign=1):
-    return [blocks[0]] + [lax.ppermute(b, axis, ring(4, sign * s)) for b, s in zip(blocks[1:], SHIFTS[1:])]
+def spread_out(blocks, axis):
+    return [blocks[0]] + [
+        lax.ppermute(block, axis, [(i, i ^ shift) for i in range(4)]) for block, shift in zip(blocks[1:], SHIFTS[1:])
+    ]
 
 
 def around(block, axis):
@@ -457,9 +471,9 @@
     return [block, *after.values(), *further]
 
 
-def both_sides(low, high, axis):
-    count = lax.axis_size(axis)
-    return lax.ppermute(high, axis, ring(count, 1)), lax.ppermute(low, axis, ring(count, -1))
+def both_sides(outer, inner, axis):
+    across = [(i, (i + (1 if i % 2 else -1)) % 8) for i in range(8)]
+    return lax.ppermute(outer, axis, across), lax.ppermute(inner, axis, [(i, i ^ 1) for i in range(8)])
 
 
 def over_tiles(rows):
@@ -501,33 +515,33 @@
 
     slots = around(latent[0].reshape(cells, channels), "ta")
     slots[0] = call(first_kernel, bf(cells, channels), [VMEM], [], 4 * 10**9, slots[0])
-    rows1, low, high = call(
+    rows1, outer, inner = call(
         frame_moments_kernel, (rows, bf(4, 16, channels), bf(4, 16, channels)), [VMEM] * 4, [], 10**6, *slots
     )
-    top, bottom = both_sides(low, high, HA)
+    outer_rows, inner_rows = both_sides(outer, inner, HA)
     rows1 = over_tiles(rows1)
-    low, high = call(
+    outer, inner = call(
         columns_kernel,
         (bf(4, 24, channels), bf(4, 24, channels)),
         [VMEM] * 6,
-        [pltpu.VMEM((4, 96, LANES), F32), pltpu.VMEM((4, 24, LANES), F32)],
+        [pltpu.VMEM((4, 96, LANES), F32), pltpu.VMEM((2, 4, 24, LANES), F32)],
         10**6,
         *slots,
-        top,
-        bottom,
-    )
-    left, right = both_sides(low, high, "z")
+        outer_rows,
+        inner_rows,
+    )
+    outer_columns, inner_columns = both_sides(outer, inner, "z")
     lhs, own = call(
         functools.partial(rimmed_kernel, grid),
         (bf(576, 1536), bf(4, cells, LANES)),
         [VMEM] * 10,
-        [pltpu.VMEM((4, cells, channels), BF), pltpu.VMEM((4, 144, LANES), F32), pltpu.VMEM((4, 24, LANES), F32)],
+        [pltpu.VMEM((4, cells, channels), BF), pltpu.VMEM((4, 144, LANES), F32), pltpu.VMEM((2, 4, 24, LANES), F32)],
         4 * 10**9,
         *slots,
-        top,
-        bottom,
-        left,
-        right,
+        outer_rows,
+        inner_rows,
+        outer_columns,
+        inner_columns,
         rows1,
         small,
     )
@@ -615,7 +629,7 @@
         [VMEM] * 8,
         [],
         10**8,
-        *spread_out(packed, "y", -1),
+        *spread_out(packed, "y"),
         residual,
         small,
         value_weight,

time: 110 us -> 111 us (level); the launches traced: 109 us -> 109 us
  starting transfers between devices: 45.3 us -> 46.6 us
  waiting for transfers between devices: 33.5 us -> 32.3 us
    ppermute x19, waiting for transfers between devices: 20.3 us -> 18.3 us  [the longest x15 18.3 us: spread_out(): lax.ppermute(block, axis, [(i, i ^ shift) for i in range(4)])]
  transfers between devices with their start and end apart: 28 -> 28, of which waited for: 15 -> 17; matrix products, arithmetic and copies ran while one was open for 0% -> 0% of each run, Pallas kernels for 1% -> 1%
where the time goes in v7:
time: 111 us; the launch traced here: 109 us
  starting transfers between devices  46.6 us (42%)
  waiting for transfers between devices  32.3 us (29%)
  blocking collectives  16.5 us (15%)
  Pallas kernels  10.4 us (9%)
  local copies, waits for them, and re-layouts  2.72 us (2%)
    ppermute x15, starting transfers between devices, spread_out(): lax.ppermute(block, axis, [(i, i ^ shift) for i in range(4)])  20.8 us
    ppermute x15, waiting for transfers between devices, spread_out(): lax.ppermute(block, axis, [(i, i ^ shift) for i in range(4)])  18.3 us
    all_to_all x1, blocking collectives, over_tiles(): lax.all_to_all(rows, HA + ('z',), split_axis=0, concat_axis=0, tiled=True)  16.5 us
    all_to_all x1, starting transfers between devices, over_tiles(): lax.all_to_all(rows, HA + ('z',), split_axis=0, concat_axis=0, tiled=True)  11.8 us
    pallas_call x13, Pallas kernels, call(): pl.pallas_call(kernel, out_shape=out_shape, in_specs=specs, out_specs=tup...  10.4 us
    ppermute x4, starting transfers between devices, relayed(): lax.ppermute(block, axis, ring(count, step))  6.24 us
    all_to_all x1, waiting for transfers between devices, over_tiles(): lax.all_to_all(rows, HA + ('z',), split_axis=0, concat_axis=0, tiled=True)  6.21 us
    ppermute x3, starting transfers between devices, relayed(): lax.ppermute(after[step], axis, ring(count, move))  4.14 us
  transfers between devices with their start and end apart: 28, of which 17 were waited for; matrix products, arithmetic and copies ran while one was open for 0% of the time, Pallas kernels for 1%

profile of v7, /device:TPU:6, one launch (start us, length us, event | category | flops | bytes accessed | tf_op | source)
XLA Modules:
  0.0 108.8 jit_solution(6383012013431962739)
XLA Ops:
  1.4 1.7 %collective-permute-start.1 = (bf16[64,512]{1,0:T(8,128)(2,1)}, bf16[64,512]{1,0:T(8,128)(2,1)S(1)}, u32[]{:S(2)}, u32[]{:S(2)}) collective-permute-start(bf16[64,512]{1,0:T(8,128)(2,1)} %bitcast.10), channel_id=1, source_target_pairs={{0,64},{64,0},{128,192},{192,128},{1,65},{65,1},{129,193},{193,129... | collective-permute-start | bytes 196616 | tf_op jit(solution)/shard_map/ppermute | solution.py:459
  6.7 2.1 %collective-permute-done.2.s3 = bf16[64,512]{1,0:T(8,128)(2,1)S(1)} collective-permute-done((bf16[64,512]{1,0:T(8,128)(2,1)}, bf16[64,512]{1,0:T(8,128)(2,1)S(1)}, u32[]{:S(2)}, u32[]{:S(2)}) %collective-permute-start.2) | collective-permute-done | bytes 65568 | tf_op jit(solution)/shard_map/ppermute | solution.py:459
  9.9 11.8 %all-to-all-start = ((f32[64,1,128]{2,1,0:T(1,128)}), f32[64,1,128]{2,1,0:T(1,128)S(1)}, u32[]{:S(2)}, u32[]{:S(2)}) async-start(f32[64,1,128]{2,1,0:T(1,128)} %get-tuple-element.26), calls=%async_computation | async-start | bytes 65536 | tf_op jit(solution)/shard_map/all_to_all | solution.py:480
  21.9 2.9 %collective-permute-start.5 = (bf16[4,24,512]{2,1,0:T(8,128)(2,1)S(1)}, bf16[4,24,512]{2,1,0:T(8,128)(2,1)S(1)}, u32[]{:S(2)}, u32[]{:S(2)}) collective-permute-start(bf16[4,24,512]{2,1,0:T(8,128)(2,1)S(1)} %get-tuple-element.24), channel_id=1, source_target_pairs={{0,7},{1,2},{2,1},{3,4},{4,3},{5,6},{6,5},{7,0},{8,15},{9,10},{10,... | collective-permute-start | bytes 294920 | tf_op jit(solution)/shard_map/ppermute | solution.py:476
  25.1 6.2 %all-to-all-done.rows_ref = f32[64,1,128]{2,1,0:T(1,128)S(1)} async-done(((f32[64,1,128]{2,1,0:T(1,128)}), f32[64,1,128]{2,1,0:T(1,128)S(1)}, u32[]{:S(2)}, u32[]{:S(2)}) %all-to-all-start) | async-done | bytes 32800 | tf_op jit(solution)/shard_map/all_to_all | solution.py:480
  33.3 2.9 %shard_map.176 = (bf16[4,104,128]{2,1,0:T(8,128)(2,1)S(1)}, f32[64,1,128]{2,1,0:T(1,128)S(1)}) custom-call(bf16[576,1536]{1,0:T(8,128)(2,1)S(1)} %get-tuple-element.27.lhs, f32[38,128]{1,0:T(8,128)S(1)} %bitcast.4, bf16[27,512,128]{2,1,0:T(8,128)(2,1)S(1)} %copy-done.3), custom_call_target="tpu_custom_call" | custom-call | flops 2000000000 | bytes 5467136 | tf_op jit(solution)/shard_map/pallas_call | solution.py:442
  36.2 16.5 %all_to_all.10.rows_ref = f32[64,1,128]{2,1,0:T(1,128)S(1)} all-to-all(f32[64,1,128]{2,1,0:T(1,128)S(1)} %get-tuple-element.29), channel_id=1, replica_groups=mesh['ta'=4,'y'=4,'core'=2,'z'=8] {'y','core','z'}, dimensions={0} | all-to-all | bytes 65536 | tf_op jit(solution)/shard_map/all_to_all | solution.py:480
  53.0 2.3 %collective-permute-start.9 = (bf16[4,104,128]{2,1,0:T(8,128)(2,1)S(1)}, bf16[4,104,128]{2,1,0:T(8,128)(2,1)S(1)}, u32[]{:S(2)}, u32[]{:S(2)}) collective-permute-start(bf16[4,104,128]{2,1,0:T(8,128)(2,1)S(1)} %shard_map.177.s0), channel_id=1, source_target_pairs={{0,128},{64,192},{128,0},{192,64},{1,129},{65,193},{129,1},{193,65... | collective-permute-start | bytes 319496 | tf_op jit(solution)/shard_map/ppermute | solution.py:459
  57.1 3.2 %collective-permute-done.9.s1 = bf16[4,104,128]{2,1,0:T(8,128)(2,1)S(1)} collective-permute-done((bf16[4,104,128]{2,1,0:T(8,128)(2,1)S(1)}, bf16[4,104,128]{2,1,0:T(8,128)(2,1)S(1)}, u32[]{:S(2)}, u32[]{:S(2)}) %collective-permute-start.9) | collective-permute-done | bytes 106528 | tf_op jit(solution)/shard_map/ppermute | solution.py:459
  62.4 1.5 %shard_map.179 = (bf16[72,128]{1,0:T(8,128)(2,1)S(1)}, bf16[72,128]{1,0:T(8,128)(2,1)S(1)}, bf16[72,128]{1,0:T(8,128)(2,1)S(1)}, bf16[72,128]{1,0:T(8,128)(2,1)S(1)}) custom-call(bf16[4,104,128]{2,1,0:T(8,128)(2,1)S(1)} %collective-permute-done.7.s2, bf16[4,104,128]{2,1,0:T(8,128)(2,1)S(1)} %collective-permute-done.8.s3, ...), custom_call_target="tpu_custom_call" | custom-call | flops 2000000000 | bytes 5975040 | tf_op jit(solution)/shard_map/pallas_call | solution.py:442
  66.4 1.7 %collective-permute-start.12 = (bf16[72,128]{1,0:T(8,128)(2,1)S(1)}, bf16[72,128]{1,0:T(8,128)(2,1)S(1)}, u32[]{:S(2)}, u32[]{:S(2)}) collective-permute-start(bf16[72,128]{1,0:T(8,128)(2,1)S(1)} %get-tuple-element.34), channel_id=1, source_target_pairs={{0,192},{64,128},{128,64},{192,0},{1,193},{65,129},{129,65},{193,1... | collective-permute-start | bytes 55304 | tf_op jit(solution)/shard_map/ppermute | solution.py:459
  69.3 2.1 %collective-permute-done.12.s3 = bf16[72,128]{1,0:T(8,128)(2,1)S(1)} collective-permute-done((bf16[72,128]{1,0:T(8,128)(2,1)S(1)}, bf16[72,128]{1,0:T(8,128)(2,1)S(1)}, u32[]{:S(2)}, u32[]{:S(2)}) %collective-permute-start.12) | collective-permute-done | bytes 18464 | tf_op jit(solution)/shard_map/ppermute | solution.py:459
  73.4 2.2 %collective-permute-start.15 = (bf16[72,512]{1,0:T(8,128)(2,1)S(1)}, bf16[72,512]{1,0:T(8,128)(2,1)S(1)}, u32[]{:S(2)}, u32[]{:S(2)}) collective-permute-start(bf16[72,512]{1,0:T(8,128)(2,1)S(1)} %shard_map.180.refs_0_.residual_ref), channel_id=1, source_target_pairs={{0,48},{16,32},{32,16},{48,0},{1,49},{17,33},{33,17},{49,1},{2,50}... | collective-permute-start | bytes 221192 | tf_op jit(solution)/shard_map/ppermute | solution.py:459
  75.6 1.8 %collective-permute-done.13.refs_1_ = bf16[72,512]{1,0:T(8,128)(2,1)S(1)} collective-permute-done((bf16[72,512]{1,0:T(8,128)(2,1)S(1)}, bf16[72,512]{1,0:T(8,128)(2,1)S(1)}, u32[]{:S(2)}, u32[]{:S(2)}) %collective-permute-start.13) | collective-permute-done | bytes 73760 | tf_op jit(solution)/shard_map/ppermute | solution.py:459
  77.4 1.6 %collective-permute-done.15.refs_3_ = bf16[72,512]{1,0:T(8,128)(2,1)S(1)} collective-permute-done((bf16[72,512]{1,0:T(8,128)(2,1)S(1)}, bf16[72,512]{1,0:T(8,128)(2,1)S(1)}, u32[]{:S(2)}, u32[]{:S(2)}) %collective-permute-start.15) | collective-permute-done | bytes 73760 | tf_op jit(solution)/shard_map/ppermute | solution.py:459
  80.3 2.6 %collective-permute-start.18 = (bf16[72,512]{1,0:T(8,128)(2,1)S(1)}, bf16[72,512]{1,0:T(8,128)(2,1)S(1)}, u32[]{:S(2)}, u32[]{:S(2)}) collective-permute-start(bf16[72,512]{1,0:T(8,128)(2,1)S(1)} %shard_map.181.refs_0_), channel_id=1, source_target_pairs={{0,7},{1,0},{2,1},{3,2},{4,3},{5,4},{6,5},{7,6},{8,15},{9,8},{10,9... | collective-permute-start | bytes 221192 | tf_op jit(solution)/shard_map/ppermute | solution.py:469
  83.0 2.3 %collective-permute-start.19 = (bf16[72,512]{1,0:T(8,128)(2,1)S(1)}, bf16[72,512]{1,0:T(8,128)(2,1)S(1)}, u32[]{:S(2)}, u32[]{:S(2)}) collective-permute-start(bf16[72,512]{1,0:T(8,128)(2,1)S(1)} %shard_map.181.refs_0_), channel_id=1, source_target_pairs={{0,6},{1,7},{2,0},{3,1},{4,2},{5,3},{6,4},{7,5},{8,14},{9,15},{10,... | collective-permute-start | bytes 221192 | tf_op jit(solution)/shard_map/ppermute | solution.py:469
  85.3 1.9 %collective-permute-done.16.refs_1_ = bf16[72,512]{1,0:T(8,128)(2,1)S(1)} collective-permute-done((bf16[72,512]{1,0:T(8,128)(2,1)S(1)}, bf16[72,512]{1,0:T(8,128)(2,1)S(1)}, u32[]{:S(2)}, u32[]{:S(2)}) %collective-permute-start.16) | collective-permute-done | bytes 73760 | tf_op jit(solution)/shard_map/ppermute | solution.py:469
  88.6 3.2 %collective-permute-start.22 = (bf16[72,512]{1,0:T(8,128)(2,1)S(1)}, bf16[72,512]{1,0:T(8,128)(2,1)S(1)}, u32[]{:S(2)}, u32[]{:S(2)}) collective-permute-start(bf16[72,512]{1,0:T(8,128)(2,1)S(1)} %collective-permute-done.18.refs_3_), channel_id=1, source_target_pairs={{0,6},{1,7},{2,0},{3,1},{4,2},{5,3},{6,4},{7,5},{8,14},{9,15},{10,... | collective-permute-start | bytes 221192 | tf_op jit(solution)/shard_map/ppermute | solution.py:470
  91.8 1.9 %collective-permute-done.20.refs_5_ = bf16[72,512]{1,0:T(8,128)(2,1)S(1)} collective-permute-done((bf16[72,512]{1,0:T(8,128)(2,1)S(1)}, bf16[72,512]{1,0:T(8,128)(2,1)S(1)}, u32[]{:S(2)}, u32[]{:S(2)}) %collective-permute-start.20) | collective-permute-done | bytes 73760 | tf_op jit(solution)/shard_map/ppermute | solution.py:470
  93.7 1.5 %collective-permute-done.21.refs_6_ = bf16[72,512]{1,0:T(8,128)(2,1)S(1)} collective-permute-done((bf16[72,512]{1,0:T(8,128)(2,1)S(1)}, bf16[72,512]{1,0:T(8,128)(2,1)S(1)}, u32[]{:S(2)}, u32[]{:S(2)}) %collective-permute-start.21) | collective-permute-done | bytes 73760 | tf_op jit(solution)/shard_map/ppermute | solution.py:470
  95.7 1.9 %collective-permute-done.23.refs_5_ = bf16[520,512]{1,0:T(8,128)(2,1)S(1)} collective-permute-done((bf16[520,512]{1,0:T(8,128)(2,1)S(1)}, bf16[520,512]{1,0:T(8,128)(2,1)S(1)}, u32[]{:S(2)}, u32[]{:S(2)}) %collective-permute-start.23) | collective-permute-done | bytes 532512 | tf_op jit(solution)/shard_map/ppermute | solution.py:620
  99.0 1.8 %collective-permute-start.24 = (bf16[64,640]{1,0:T(8,128)(2,1)S(1)}, bf16[64,640]{1,0:T(8,128)(2,1)S(1)}, u32[]{:S(2)}, u32[]{:S(2)}) collective-permute-start(bf16[64,640]{1,0:T(8,128)(2,1)S(1)} %get-tuple-element.36), channel_id=1, source_target_pairs={{0,32},{16,48},{32,0},{48,16},{1,33},{17,49},{33,1},{49,17},{2,34}... | collective-permute-start | bytes 245768 | tf_op jit(solution)/shard_map/ppermute | solution.py:459
  103.2 2.4 %collective-permute-done.24.b1 = bf16[64,640]{1,0:T(8,128)(2,1)S(1)} collective-permute-done((bf16[64,640]{1,0:T(8,128)(2,1)S(1)}, bf16[64,640]{1,0:T(8,128)(2,1)S(1)}, u32[]{:S(2)}, u32[]{:S(2)}) %collective-permute-start.24) | collective-permute-done | bytes 81952 | tf_op jit(solution)/shard_map/ppermute | solution.py:459
  (94 shorter events, 28.7 us)
Async XLA Ops:
  0.0 6.7 %collective-permute-start = (bf16[64,512]{1,0:T(8,128)(2,1)}, bf16[64,512]{1,0:T(8,128)(2,1)S(1)}, u32[]{:S(2)}, u32[]{:S(2)}) collective-permute-start(bf16[64,512]{1,0:T(8,128)(2,1)} %bitcast.9), channel_id=1, source_target_pairs={{0,128},{64,192},{128,0},{192,64},{1,129},{65,193},{129,1},{193,65... | collective-permute-start | bytes 196616 | tf_op jit(solution)/shard_map/ppermute | solution.py:459
  1.4 5.3 %collective-permute-start.1 = (bf16[64,512]{1,0:T(8,128)(2,1)}, bf16[64,512]{1,0:T(8,128)(2,1)S(1)}, u32[]{:S(2)}, u32[]{:S(2)}) collective-permute-start(bf16[64,512]{1,0:T(8,128)(2,1)} %bitcast.10), channel_id=1, source_target_pairs={{0,64},{64,0},{128,192},{192,128},{1,65},{65,1},{129,193},{193,129... | collective-permute-start | bytes 196616 | tf_op jit(solution)/shard_map/ppermute | solution.py:459
  3.1 5.7 %collective-permute-start.2 = (bf16[64,512]{1,0:T(8,128)(2,1)}, bf16[64,512]{1,0:T(8,128)(2,1)S(1)}, u32[]{:S(2)}, u32[]{:S(2)}) collective-permute-start(bf16[64,512]{1,0:T(8,128)(2,1)} %bitcast.11), channel_id=1, source_target_pairs={{0,192},{64,128},{128,64},{192,0},{1,193},{65,129},{129,65},{193,1... | collective-permute-start | bytes 196616 | tf_op jit(solution)/shard_map/ppermute | solution.py:459
  9.8 12.0 %collective-permute-start.3 = (bf16[4,16,512]{2,1,0:T(8,128)(2,1)S(1)}, bf16[4,16,512]{2,1,0:T(8,128)(2,1)S(1)}, u32[]{:S(2)}, u32[]{:S(2)}) collective-permute-start(bf16[4,16,512]{2,1,0:T(8,128)(2,1)S(1)} %get-tuple-element.22), channel_id=1, source_target_pairs={{0,56},{8,16},{16,8},{24,32},{32,24},{40,48},{48,40},{56,0},{1,57}... | collective-permute-start | bytes 196616 | tf_op jit(solution)/shard_map/ppermute | solution.py:476
  9.8 11.9 %collective-permute-start.4 = (bf16[4,16,512]{2,1,0:T(8,128)(2,1)S(1)}, bf16[4,16,512]{2,1,0:T(8,128)(2,1)S(1)}, u32[]{:S(2)}, u32[]{:S(2)}) collective-permute-start(bf16[4,16,512]{2,1,0:T(8,128)(2,1)S(1)} %get-tuple-element.23), channel_id=1, source_target_pairs={{0,8},{8,0},{16,24},{24,16},{32,40},{40,32},{48,56},{56,48},{1,9},... | collective-permute-start | bytes 196616 | tf_op jit(solution)/shard_map/ppermute | solution.py:476
  9.9 21.4 %all-to-all-start = ((f32[64,1,128]{2,1,0:T(1,128)}), f32[64,1,128]{2,1,0:T(1,128)S(1)}, u32[]{:S(2)}, u32[]{:S(2)}) async-start(f32[64,1,128]{2,1,0:T(1,128)} %get-tuple-element.26), calls=%async_computation | async-start | bytes 65536 | tf_op jit(solution)/shard_map/all_to_all | solution.py:480
  21.9 9.3 %collective-permute-start.5 = (bf16[4,24,512]{2,1,0:T(8,128)(2,1)S(1)}, bf16[4,24,512]{2,1,0:T(8,128)(2,1)S(1)}, u32[]{:S(2)}, u32[]{:S(2)}) collective-permute-start(bf16[4,24,512]{2,1,0:T(8,128)(2,1)S(1)} %get-tuple-element.24), channel_id=1, source_target_pairs={{0,7},{1,2},{2,1},{3,4},{4,3},{5,6},{6,5},{7,0},{8,15},{9,10},{10,... | collective-permute-start | bytes 294920 | tf_op jit(solution)/shard_map/ppermute | solution.py:476
  24.8 6.5 %collective-permute-start.6 = (bf16[4,24,512]{2,1,0:T(8,128)(2,1)S(1)}, bf16[4,24,512]{2,1,0:T(8,128)(2,1)S(1)}, u32[]{:S(2)}, u32[]{:S(2)}) collective-permute-start(bf16[4,24,512]{2,1,0:T(8,128)(2,1)S(1)} %get-tuple-element.25), channel_id=1, source_target_pairs={{0,1},{1,0},{2,3},{3,2},{4,5},{5,4},{6,7},{7,6},{8,9},{9,8},{10,11... | collective-permute-start | bytes 294920 | tf_op jit(solution)/shard_map/ppermute | solution.py:476
  53.0 7.4 %collective-permute-start.9 = (bf16[4,104,128]{2,1,0:T(8,128)(2,1)S(1)}, bf16[4,104,128]{2,1,0:T(8,128)(2,1)S(1)}, u32[]{:S(2)}, u32[]{:S(2)}) collective-permute-start(bf16[4,104,128]{2,1,0:T(8,128)(2,1)S(1)} %shard_map.177.s0), channel_id=1, source_target_pairs={{0,128},{64,192},{128,0},{192,64},{1,129},{65,193},{129,1},{193,65... | collective-permute-start | bytes 319496 | tf_op jit(solution)/shard_map/ppermute | solution.py:459
  55.3 6.2 %collective-permute-start.7 = (bf16[4,104,128]{2,1,0:T(8,128)(2,1)S(1)}, bf16[4,104,128]{2,1,0:T(8,128)(2,1)S(1)}, u32[]{:S(2)}, u32[]{:S(2)}) collective-permute-start(bf16[4,104,128]{2,1,0:T(8,128)(2,1)S(1)} %shard_map.177.s0), channel_id=1, source_target_pairs={{0,64},{64,0},{128,192},{192,128},{1,65},{65,1},{129,193},{193,129... | collective-permute-start | bytes 319496 | tf_op jit(solution)/shard_map/ppermute | solution.py:459
  56.5 5.9 %collective-permute-start.8 = (bf16[4,104,128]{2,1,0:T(8,128)(2,1)S(1)}, bf16[4,104,128]{2,1,0:T(8,128)(2,1)S(1)}, u32[]{:S(2)}, u32[]{:S(2)}) collective-permute-start(bf16[4,104,128]{2,1,0:T(8,128)(2,1)S(1)} %shard_map.177.s0), channel_id=1, source_target_pairs={{0,192},{64,128},{128,64},{192,0},{1,193},{65,129},{129,65},{193,1... | collective-permute-start | bytes 319496 | tf_op jit(solution)/shard_map/ppermute | solution.py:459
  63.9 5.4 %collective-permute-start.10 = (bf16[72,128]{1,0:T(8,128)(2,1)S(1)}, bf16[72,128]{1,0:T(8,128)(2,1)S(1)}, u32[]{:S(2)}, u32[]{:S(2)}) collective-permute-start(bf16[72,128]{1,0:T(8,128)(2,1)S(1)} %get-tuple-element.32), channel_id=1, source_target_pairs={{0,128},{64,192},{128,0},{192,64},{1,129},{65,193},{129,1},{193,65... | collective-permute-start | bytes 55304 | tf_op jit(solution)/shard_map/ppermute | solution.py:459
  71.4 5.9 %collective-permute-start.13 = (bf16[72,512]{1,0:T(8,128)(2,1)S(1)}, bf16[72,512]{1,0:T(8,128)(2,1)S(1)}, u32[]{:S(2)}, u32[]{:S(2)}) collective-permute-start(bf16[72,512]{1,0:T(8,128)(2,1)S(1)} %shard_map.180.refs_0_.residual_ref), channel_id=1, source_target_pairs={{0,32},{16,48},{32,0},{48,16},{1,33},{17,49},{33,1},{49,17},{2,34}... | collective-permute-start | bytes 221192 | tf_op jit(solution)/shard_map/ppermute | solution.py:459
  73.4 5.6 %collective-permute-start.15 = (bf16[72,512]{1,0:T(8,128)(2,1)S(1)}, bf16[72,512]{1,0:T(8,128)(2,1)S(1)}, u32[]{:S(2)}, u32[]{:S(2)}) collective-permute-start(bf16[72,512]{1,0:T(8,128)(2,1)S(1)} %shard_map.180.refs_0_.residual_ref), channel_id=1, source_target_pairs={{0,48},{16,32},{32,16},{48,0},{1,49},{17,33},{33,17},{49,1},{2,50}... | collective-permute-start | bytes 221192 | tf_op jit(solution)/shard_map/ppermute | solution.py:459
  79.0 8.1 %collective-permute-start.16 = (bf16[72,512]{1,0:T(8,128)(2,1)S(1)}, bf16[72,512]{1,0:T(8,128)(2,1)S(1)}, u32[]{:S(2)}, u32[]{:S(2)}) collective-permute-start(bf16[72,512]{1,0:T(8,128)(2,1)S(1)} %shard_map.181.refs_0_), channel_id=1, source_target_pairs={{0,2},{1,3},{2,4},{3,5},{4,6},{5,7},{6,0},{7,1},{8,10},{9,11},{10,... | collective-permute-start | bytes 221192 | tf_op jit(solution)/shard_map/ppermute | solution.py:469
  79.7 7.9 %collective-permute-start.17 = (bf16[72,512]{1,0:T(8,128)(2,1)S(1)}, bf16[72,512]{1,0:T(8,128)(2,1)S(1)}, u32[]{:S(2)}, u32[]{:S(2)}) collective-permute-start(bf16[72,512]{1,0:T(8,128)(2,1)S(1)} %shard_map.181.refs_0_), channel_id=1, source_target_pairs={{0,1},{1,2},{2,3},{3,4},{4,5},{5,6},{6,7},{7,0},{8,9},{9,10},{10,1... | collective-permute-start | bytes 221192 | tf_op jit(solution)/shard_map/ppermute | solution.py:469
  80.3 8.2 %collective-permute-start.18 = (bf16[72,512]{1,0:T(8,128)(2,1)S(1)}, bf16[72,512]{1,0:T(8,128)(2,1)S(1)}, u32[]{:S(2)}, u32[]{:S(2)}) collective-permute-start(bf16[72,512]{1,0:T(8,128)(2,1)S(1)} %shard_map.181.refs_0_), channel_id=1, source_target_pairs={{0,7},{1,0},{2,1},{3,2},{4,3},{5,4},{6,5},{7,6},{8,15},{9,8},{10,9... | collective-permute-start | bytes 221192 | tf_op jit(solution)/shard_map/ppermute | solution.py:469
  83.0 8.8 %collective-permute-start.19 = (bf16[72,512]{1,0:T(8,128)(2,1)S(1)}, bf16[72,512]{1,0:T(8,128)(2,1)S(1)}, u32[]{:S(2)}, u32[]{:S(2)}) collective-permute-start(bf16[72,512]{1,0:T(8,128)(2,1)S(1)} %shard_map.181.refs_0_), channel_id=1, source_target_pairs={{0,6},{1,7},{2,0},{3,1},{4,2},{5,3},{6,4},{7,5},{8,14},{9,15},{10,... | collective-permute-start | bytes 221192 | tf_op jit(solution)/shard_map/ppermute | solution.py:469
  87.2 6.6 %collective-permute-start.20 = (bf16[72,512]{1,0:T(8,128)(2,1)S(1)}, bf16[72,512]{1,0:T(8,128)(2,1)S(1)}, u32[]{:S(2)}, u32[]{:S(2)}) collective-permute-start(bf16[72,512]{1,0:T(8,128)(2,1)S(1)} %collective-permute-done.16.refs_1_), channel_id=1, source_target_pairs={{0,2},{1,3},{2,4},{3,5},{4,6},{5,7},{6,0},{7,1},{8,10},{9,11},{10,... | collective-permute-start | bytes 221192 | tf_op jit(solution)/shard_map/ppermute | solution.py:470
  87.7 7.6 %collective-permute-start.21 = (bf16[72,512]{1,0:T(8,128)(2,1)S(1)}, bf16[72,512]{1,0:T(8,128)(2,1)S(1)}, u32[]{:S(2)}, u32[]{:S(2)}) collective-permute-start(bf16[72,512]{1,0:T(8,128)(2,1)S(1)} %collective-permute-done.17.refs_2_), channel_id=1, source_target_pairs={{0,2},{1,3},{2,4},{3,5},{4,6},{5,7},{6,0},{7,1},{8,10},{9,11},{10,... | collective-permute-start | bytes 221192 | tf_op jit(solution)/shard_map/ppermute | solution.py:470
  88.6 6.7 %collective-permute-start.22 = (bf16[72,512]{1,0:T(8,128)(2,1)S(1)}, bf16[72,512]{1,0:T(8,128)(2,1)S(1)}, u32[]{:S(2)}, u32[]{:S(2)}) collective-permute-start(bf16[72,512]{1,0:T(8,128)(2,1)S(1)} %collective-permute-done.18.refs_3_), channel_id=1, source_target_pairs={{0,6},{1,7},{2,0},{3,1},{4,2},{5,3},{6,4},{7,5},{8,14},{9,15},{10,... | collective-permute-start | bytes 221192 | tf_op jit(solution)/shard_map/ppermute | solution.py:470
  99.0 6.5 %collective-permute-start.24 = (bf16[64,640]{1,0:T(8,128)(2,1)S(1)}, bf16[64,640]{1,0:T(8,128)(2,1)S(1)}, u32[]{:S(2)}, u32[]{:S(2)}) collective-permute-start(bf16[64,640]{1,0:T(8,128)(2,1)S(1)} %get-tuple-element.36), channel_id=1, source_target_pairs={{0,32},{16,48},{32,0},{48,16},{1,33},{17,49},{33,1},{49,17},{2,34}... | collective-permute-start | bytes 245768 | tf_op jit(solution)/shard_map/ppermute | solution.py:459
  100.7 5.5 %collective-permute-start.25 = (bf16[64,640]{1,0:T(8,128)(2,1)S(1)}, bf16[64,640]{1,0:T(8,128)(2,1)S(1)}, u32[]{:S(2)}, u32[]{:S(2)}) collective-permute-start(bf16[64,640]{1,0:T(8,128)(2,1)S(1)} %get-tuple-element.37), channel_id=1, source_target_pairs={{0,16},{16,0},{32,48},{48,32},{1,17},{17,1},{33,49},{49,33},{2,18}... | collective-permute-start | bytes 245768 | tf_op jit(solution)/shard_map/ppermute | solution.py:459
  102.1 5.7 %collective-permute-start.26 = (bf16[64,640]{1,0:T(8,128)(2,1)S(1)}, bf16[64,640]{1,0:T(8,128)(2,1)S(1)}, u32[]{:S(2)}, u32[]{:S(2)}) collective-permute-start(bf16[64,640]{1,0:T(8,128)(2,1)S(1)} %get-tuple-element.38), channel_id=1, source_target_pairs={{0,48},{16,32},{32,16},{48,0},{1,49},{17,33},{33,17},{49,1},{2,50}... | collective-permute-start | bytes 245768 | tf_op jit(solution)/shard_map/ppermute | solution.py:459
  (22 other events, 226.0 us)

commit v8 on v7

--- a/solution.py
+++ b/solution.py
@@ -466,8 +466,8 @@
 
 def relayed(block, axis):
     count = lax.axis_size(axis)
-    after = {step: lax.ppermute(block, axis, ring(count, step)) for step in (2, 1, -1, -2)}
-    further = [lax.ppermute(after[step], axis, ring(count, move)) for step, move in ((2, 2), (1, 2), (-1, -2))]
+    after = {step: lax.ppermute(block, axis, ring(count, step)) for step in (2, -2, 1, -1)}
+    further = [lax.ppermute(after[step], axis, ring(count, move)) for step, move in ((2, 2), (2, 1), (-2, -1))]
     return [block, *after.values(), *further]
 
 

time: 111 us -> 109 us (0.982)
  waiting for transfers between devices: 32.3 us -> 30.6 us
    ppermute x4, waiting for transfers between devices: 2.39 us -> 0.61 us  [relayed(): lax.ppermute(block, axis, ring(count, step))]
    ppermute x4, starting transfers between devices: 6.24 us -> 7.45 us  [relayed(): lax.ppermute(block, axis, ring(count, step))]
  transfers between devices with their start and end apart: 28 -> 28, of which waited for: 17 -> 16; matrix products, arithmetic and copies ran while one was open for 0% -> 0% of each run, Pallas kernels for 1% -> 1%
where the time goes in v8:
time: 109 us; the launch traced here: 107 us
  starting transfers between devices  46.9 us (43%)
  waiting for transfers between devices  30.6 us (28%)
  blocking collectives  16.5 us (15%)
  Pallas kernels  10.4 us (10%)
  local copies, waits for them, and re-layouts  2.72 us (2%)
    ppermute x15, starting transfers between devices, spread_out(): lax.ppermute(block, axis, [(i, i ^ shift) for i in range(4)])  20.8 us
    ppermute x15, waiting for transfers between devices, spread_out(): lax.ppermute(block, axis, [(i, i ^ shift) for i in range(4)])  18.4 us
    all_to_all x1, blocking collectives, over_tiles(): lax.all_to_all(rows, HA + ('z',), split_axis=0, concat_axis=0, tiled=True)  16.5 us
    all_to_all x1, starting transfers between devices, over_tiles(): lax.all_to_all(rows, HA + ('z',), split_axis=0, concat_axis=0, tiled=True)  11.8 us
    pallas_call x13, Pallas kernels, call(): pl.pallas_call(kernel, out_shape=out_shape, in_specs=specs, out_specs=tup...  10.4 us
    ppermute x4, starting transfers between devices, relayed(): lax.ppermute(block, axis, ring(count, step))  7.45 us
    all_to_all x1, waiting for transfers between devices, over_tiles(): lax.all_to_all(rows, HA + ('z',), split_axis=0, concat_axis=0, tiled=True)  6.21 us
    ppermute x3, waiting for transfers between devices, relayed(): lax.ppermute(after[step], axis, ring(count, move))  3.52 us
  transfers between devices with their start and end apart: 28, of which 16 were waited for; matrix products, arithmetic and copies ran while one was open for 0% of the time, Pallas kernels for 1%

profile of v8, /device:TPU:6, one launch (start us, length us, event | category | flops | bytes accessed | tf_op | source)
XLA Modules:
  0.0 107.5 jit_solution(4509466003844496727)
XLA Ops:
  1.4 1.7 %collective-permute-start.1 = (bf16[64,512]{1,0:T(8,128)(2,1)}, bf16[64,512]{1,0:T(8,128)(2,1)S(1)}, u32[]{:S(2)}, u32[]{:S(2)}) collective-permute-start(bf16[64,512]{1,0:T(8,128)(2,1)} %bitcast.10), channel_id=1, source_target_pairs={{0,64},{64,0},{128,192},{192,128},{1,65},{65,1},{129,193},{193,129... | collective-permute-start | bytes 196616 | tf_op jit(solution)/shard_map/ppermute | solution.py:459
  6.7 2.1 %collective-permute-done.2.s3 = bf16[64,512]{1,0:T(8,128)(2,1)S(1)} collective-permute-done((bf16[64,512]{1,0:T(8,128)(2,1)}, bf16[64,512]{1,0:T(8,128)(2,1)S(1)}, u32[]{:S(2)}, u32[]{:S(2)}) %collective-permute-start.2) | collective-permute-done | bytes 65568 | tf_op jit(solution)/shard_map/ppermute | solution.py:459
  9.9 11.8 %all-to-all-start = ((f32[64,1,128]{2,1,0:T(1,128)}), f32[64,1,128]{2,1,0:T(1,128)S(1)}, u32[]{:S(2)}, u32[]{:S(2)}) async-start(f32[64,1,128]{2,1,0:T(1,128)} %get-tuple-element.26), calls=%async_computation | async-start | bytes 65536 | tf_op jit(solution)/shard_map/all_to_all | solution.py:480
  21.9 2.9 %collective-permute-start.5 = (bf16[4,24,512]{2,1,0:T(8,128)(2,1)S(1)}, bf16[4,24,512]{2,1,0:T(8,128)(2,1)S(1)}, u32[]{:S(2)}, u32[]{:S(2)}) collective-permute-start(bf16[4,24,512]{2,1,0:T(8,128)(2,1)S(1)} %get-tuple-element.24), channel_id=1, source_target_pairs={{0,7},{1,2},{2,1},{3,4},{4,3},{5,6},{6,5},{7,0},{8,15},{9,10},{10,... | collective-permute-start | bytes 294920 | tf_op jit(solution)/shard_map/ppermute | solution.py:476
  25.1 6.2 %all-to-all-done.rows_ref = f32[64,1,128]{2,1,0:T(1,128)S(1)} async-done(((f32[64,1,128]{2,1,0:T(1,128)}), f32[64,1,128]{2,1,0:T(1,128)S(1)}, u32[]{:S(2)}, u32[]{:S(2)}) %all-to-all-start) | async-done | bytes 32800 | tf_op jit(solution)/shard_map/all_to_all | solution.py:480
  33.3 2.9 %shard_map.176 = (bf16[4,104,128]{2,1,0:T(8,128)(2,1)S(1)}, f32[64,1,128]{2,1,0:T(1,128)S(1)}) custom-call(bf16[576,1536]{1,0:T(8,128)(2,1)S(1)} %get-tuple-element.27.lhs, f32[38,128]{1,0:T(8,128)S(1)} %bitcast.4, bf16[27,512,128]{2,1,0:T(8,128)(2,1)S(1)} %copy-done.3), custom_call_target="tpu_custom_call" | custom-call | flops 2000000000 | bytes 5467136 | tf_op jit(solution)/shard_map/pallas_call | solution.py:442
  36.2 16.5 %all_to_all.10.rows_ref = f32[64,1,128]{2,1,0:T(1,128)S(1)} all-to-all(f32[64,1,128]{2,1,0:T(1,128)S(1)} %get-tuple-element.29), channel_id=1, replica_groups=mesh['ta'=4,'y'=4,'core'=2,'z'=8] {'y','core','z'}, dimensions={0} | all-to-all | bytes 65536 | tf_op jit(solution)/shard_map/all_to_all | solution.py:480
  53.0 2.3 %collective-permute-start.9 = (bf16[4,104,128]{2,1,0:T(8,128)(2,1)S(1)}, bf16[4,104,128]{2,1,0:T(8,128)(2,1)S(1)}, u32[]{:S(2)}, u32[]{:S(2)}) collective-permute-start(bf16[4,104,128]{2,1,0:T(8,128)(2,1)S(1)} %shard_map.177.s0), channel_id=1, source_target_pairs={{0,128},{64,192},{128,0},{192,64},{1,129},{65,193},{129,1},{193,65... | collective-permute-start | bytes 319496 | tf_op jit(solution)/shard_map/ppermute | solution.py:459
  57.1 3.2 %collective-permute-done.9.s1 = bf16[4,104,128]{2,1,0:T(8,128)(2,1)S(1)} collective-permute-done((bf16[4,104,128]{2,1,0:T(8,128)(2,1)S(1)}, bf16[4,104,128]{2,1,0:T(8,128)(2,1)S(1)}, u32[]{:S(2)}, u32[]{:S(2)}) %collective-permute-start.9) | collective-permute-done | bytes 106528 | tf_op jit(solution)/shard_map/ppermute | solution.py:459
  62.4 1.5 %shard_map.179 = (bf16[72,128]{1,0:T(8,128)(2,1)S(1)}, bf16[72,128]{1,0:T(8,128)(2,1)S(1)}, bf16[72,128]{1,0:T(8,128)(2,1)S(1)}, bf16[72,128]{1,0:T(8,128)(2,1)S(1)}) custom-call(bf16[4,104,128]{2,1,0:T(8,128)(2,1)S(1)} %collective-permute-done.7.s2, bf16[4,104,128]{2,1,0:T(8,128)(2,1)S(1)} %collective-permute-done.8.s3, ...), custom_call_target="tpu_custom_call" | custom-call | flops 2000000000 | bytes 5975040 | tf_op jit(solution)/shard_map/pallas_call | solution.py:442
  66.4 1.7 %collective-permute-start.12 = (bf16[72,128]{1,0:T(8,128)(2,1)S(1)}, bf16[72,128]{1,0:T(8,128)(2,1)S(1)}, u32[]{:S(2)}, u32[]{:S(2)}) collective-permute-start(bf16[72,128]{1,0:T(8,128)(2,1)S(1)} %get-tuple-element.34), channel_id=1, source_target_pairs={{0,192},{64,128},{128,64},{192,0},{1,193},{65,129},{129,65},{193,1... | collective-permute-start | bytes 55304 | tf_op jit(solution)/shard_map/ppermute | solution.py:459
  69.3 2.1 %collective-permute-done.12.s3 = bf16[72,128]{1,0:T(8,128)(2,1)S(1)} collective-permute-done((bf16[72,128]{1,0:T(8,128)(2,1)S(1)}, bf16[72,128]{1,0:T(8,128)(2,1)S(1)}, u32[]{:S(2)}, u32[]{:S(2)}) %collective-permute-start.12) | collective-permute-done | bytes 18464 | tf_op jit(solution)/shard_map/ppermute | solution.py:459
  71.4 1.5 %collective-permute-start.13 = (bf16[72,512]{1,0:T(8,128)(2,1)S(1)}, bf16[72,512]{1,0:T(8,128)(2,1)S(1)}, u32[]{:S(2)}, u32[]{:S(2)}) collective-permute-start(bf16[72,512]{1,0:T(8,128)(2,1)S(1)} %shard_map.180.refs_0_.residual_ref), channel_id=1, source_target_pairs={{0,32},{16,48},{32,0},{48,16},{1,33},{17,49},{33,1},{49,17},{2,34}... | collective-permute-start | bytes 221192 | tf_op jit(solution)/shard_map/ppermute | solution.py:459
  73.4 2.2 %collective-permute-start.15 = (bf16[72,512]{1,0:T(8,128)(2,1)S(1)}, bf16[72,512]{1,0:T(8,128)(2,1)S(1)}, u32[]{:S(2)}, u32[]{:S(2)}) collective-permute-start(bf16[72,512]{1,0:T(8,128)(2,1)S(1)} %shard_map.180.refs_0_.residual_ref), channel_id=1, source_target_pairs={{0,48},{16,32},{32,16},{48,0},{1,49},{17,33},{33,17},{49,1},{2,50}... | collective-permute-start | bytes 221192 | tf_op jit(solution)/shard_map/ppermute | solution.py:459
  75.6 1.8 %collective-permute-done.13.refs_1_ = bf16[72,512]{1,0:T(8,128)(2,1)S(1)} collective-permute-done((bf16[72,512]{1,0:T(8,128)(2,1)S(1)}, bf16[72,512]{1,0:T(8,128)(2,1)S(1)}, u32[]{:S(2)}, u32[]{:S(2)}) %collective-permute-start.13) | collective-permute-done | bytes 73760 | tf_op jit(solution)/shard_map/ppermute | solution.py:459
  77.4 1.6 %collective-permute-done.15.refs_3_ = bf16[72,512]{1,0:T(8,128)(2,1)S(1)} collective-permute-done((bf16[72,512]{1,0:T(8,128)(2,1)S(1)}, bf16[72,512]{1,0:T(8,128)(2,1)S(1)}, u32[]{:S(2)}, u32[]{:S(2)}) %collective-permute-start.15) | collective-permute-done | bytes 73760 | tf_op jit(solution)/shard_map/ppermute | solution.py:459
  79.7 3.5 %collective-permute-start.17 = (bf16[72,512]{1,0:T(8,128)(2,1)S(1)}, bf16[72,512]{1,0:T(8,128)(2,1)S(1)}, u32[]{:S(2)}, u32[]{:S(2)}) collective-permute-start(bf16[72,512]{1,0:T(8,128)(2,1)S(1)} %shard_map.181.refs_0_), channel_id=1, source_target_pairs={{0,6},{1,7},{2,0},{3,1},{4,2},{5,3},{6,4},{7,5},{8,14},{9,15},{10,... | collective-permute-start | bytes 221192 | tf_op jit(solution)/shard_map/ppermute | solution.py:469
  83.8 2.6 %collective-permute-start.19 = (bf16[72,512]{1,0:T(8,128)(2,1)S(1)}, bf16[72,512]{1,0:T(8,128)(2,1)S(1)}, u32[]{:S(2)}, u32[]{:S(2)}) collective-permute-start(bf16[72,512]{1,0:T(8,128)(2,1)S(1)} %shard_map.181.refs_0_), channel_id=1, source_target_pairs={{0,7},{1,0},{2,1},{3,2},{4,3},{5,4},{6,5},{7,6},{8,15},{9,8},{10,9... | collective-permute-start | bytes 221192 | tf_op jit(solution)/shard_map/ppermute | solution.py:469
  88.0 2.4 %collective-permute-start.22 = (bf16[72,512]{1,0:T(8,128)(2,1)S(1)}, bf16[72,512]{1,0:T(8,128)(2,1)S(1)}, u32[]{:S(2)}, u32[]{:S(2)}) collective-permute-start(bf16[72,512]{1,0:T(8,128)(2,1)S(1)} %collective-permute-done.17.refs_2_), channel_id=1, source_target_pairs={{0,7},{1,0},{2,1},{3,2},{4,3},{5,4},{6,5},{7,6},{8,15},{9,8},{10,9... | collective-permute-start | bytes 221192 | tf_op jit(solution)/shard_map/ppermute | solution.py:470
  90.3 3.3 %collective-permute-done.20.refs_5_ = bf16[72,512]{1,0:T(8,128)(2,1)S(1)} collective-permute-done((bf16[72,512]{1,0:T(8,128)(2,1)S(1)}, bf16[72,512]{1,0:T(8,128)(2,1)S(1)}, u32[]{:S(2)}, u32[]{:S(2)}) %collective-permute-start.20) | collective-permute-done | bytes 73760 | tf_op jit(solution)/shard_map/ppermute | solution.py:470
  94.3 1.9 %collective-permute-done.23.refs_5_ = bf16[520,512]{1,0:T(8,128)(2,1)S(1)} collective-permute-done((bf16[520,512]{1,0:T(8,128)(2,1)S(1)}, bf16[520,512]{1,0:T(8,128)(2,1)S(1)}, u32[]{:S(2)}, u32[]{:S(2)}) %collective-permute-start.23) | collective-permute-done | bytes 532512 | tf_op jit(solution)/shard_map/ppermute | solution.py:620
  97.6 1.8 %collective-permute-start.24 = (bf16[64,640]{1,0:T(8,128)(2,1)S(1)}, bf16[64,640]{1,0:T(8,128)(2,1)S(1)}, u32[]{:S(2)}, u32[]{:S(2)}) collective-permute-start(bf16[64,640]{1,0:T(8,128)(2,1)S(1)} %get-tuple-element.36), channel_id=1, source_target_pairs={{0,32},{16,48},{32,0},{48,16},{1,33},{17,49},{33,1},{49,17},{2,34}... | collective-permute-start | bytes 245768 | tf_op jit(solution)/shard_map/ppermute | solution.py:459
  101.8 2.7 %collective-permute-done.24.b1 = bf16[64,640]{1,0:T(8,128)(2,1)S(1)} collective-permute-done((bf16[64,640]{1,0:T(8,128)(2,1)S(1)}, bf16[64,640]{1,0:T(8,128)(2,1)S(1)}, u32[]{:S(2)}, u32[]{:S(2)}) %collective-permute-start.24) | collective-permute-done | bytes 81952 | tf_op jit(solution)/shard_map/ppermute | solution.py:459
  105.0 1.4 %collective-permute-done.26.b3 = bf16[64,640]{1,0:T(8,128)(2,1)S(1)} collective-permute-done((bf16[64,640]{1,0:T(8,128)(2,1)S(1)}, bf16[64,640]{1,0:T(8,128)(2,1)S(1)}, u32[]{:S(2)}, u32[]{:S(2)}) %collective-permute-start.26) | collective-permute-done | bytes 81952 | tf_op jit(solution)/shard_map/ppermute | solution.py:459
  (94 shorter events, 25.7 us)
Async XLA Ops:
  0.0 6.7 %collective-permute-start = (bf16[64,512]{1,0:T(8,128)(2,1)}, bf16[64,512]{1,0:T(8,128)(2,1)S(1)}, u32[]{:S(2)}, u32[]{:S(2)}) collective-permute-start(bf16[64,512]{1,0:T(8,128)(2,1)} %bitcast.9), channel_id=1, source_target_pairs={{0,128},{64,192},{128,0},{192,64},{1,129},{65,193},{129,1},{193,65... | collective-permute-start | bytes 196616 | tf_op jit(solution)/shard_map/ppermute | solution.py:459
  1.4 5.3 %collective-permute-start.1 = (bf16[64,512]{1,0:T(8,128)(2,1)}, bf16[64,512]{1,0:T(8,128)(2,1)S(1)}, u32[]{:S(2)}, u32[]{:S(2)}) collective-permute-start(bf16[64,512]{1,0:T(8,128)(2,1)} %bitcast.10), channel_id=1, source_target_pairs={{0,64},{64,0},{128,192},{192,128},{1,65},{65,1},{129,193},{193,129... | collective-permute-start | bytes 196616 | tf_op jit(solution)/shard_map/ppermute | solution.py:459
  3.1 5.7 %collective-permute-start.2 = (bf16[64,512]{1,0:T(8,128)(2,1)}, bf16[64,512]{1,0:T(8,128)(2,1)S(1)}, u32[]{:S(2)}, u32[]{:S(2)}) collective-permute-start(bf16[64,512]{1,0:T(8,128)(2,1)} %bitcast.11), channel_id=1, source_target_pairs={{0,192},{64,128},{128,64},{192,0},{1,193},{65,129},{129,65},{193,1... | collective-permute-start | bytes 196616 | tf_op jit(solution)/shard_map/ppermute | solution.py:459
  9.8 12.0 %collective-permute-start.3 = (bf16[4,16,512]{2,1,0:T(8,128)(2,1)S(1)}, bf16[4,16,512]{2,1,0:T(8,128)(2,1)S(1)}, u32[]{:S(2)}, u32[]{:S(2)}) collective-permute-start(bf16[4,16,512]{2,1,0:T(8,128)(2,1)S(1)} %get-tuple-element.22), channel_id=1, source_target_pairs={{0,56},{8,16},{16,8},{24,32},{32,24},{40,48},{48,40},{56,0},{1,57}... | collective-permute-start | bytes 196616 | tf_op jit(solution)/shard_map/ppermute | solution.py:476
  9.8 11.9 %collective-permute-start.4 = (bf16[4,16,512]{2,1,0:T(8,128)(2,1)S(1)}, bf16[4,16,512]{2,1,0:T(8,128)(2,1)S(1)}, u32[]{:S(2)}, u32[]{:S(2)}) collective-permute-start(bf16[4,16,512]{2,1,0:T(8,128)(2,1)S(1)} %get-tuple-element.23), channel_id=1, source_target_pairs={{0,8},{8,0},{16,24},{24,16},{32,40},{40,32},{48,56},{56,48},{1,9},... | collective-permute-start | bytes 196616 | tf_op jit(solution)/shard_map/ppermute | solution.py:476
  9.9 21.4 %all-to-all-start = ((f32[64,1,128]{2,1,0:T(1,128)}), f32[64,1,128]{2,1,0:T(1,128)S(1)}, u32[]{:S(2)}, u32[]{:S(2)}) async-start(f32[64,1,128]{2,1,0:T(1,128)} %get-tuple-element.26), calls=%async_computation | async-start | bytes 65536 | tf_op jit(solution)/shard_map/all_to_all | solution.py:480
  21.9 9.3 %collective-permute-start.5 = (bf16[4,24,512]{2,1,0:T(8,128)(2,1)S(1)}, bf16[4,24,512]{2,1,0:T(8,128)(2,1)S(1)}, u32[]{:S(2)}, u32[]{:S(2)}) collective-permute-start(bf16[4,24,512]{2,1,0:T(8,128)(2,1)S(1)} %get-tuple-element.24), channel_id=1, source_target_pairs={{0,7},{1,2},{2,1},{3,4},{4,3},{5,6},{6,5},{7,0},{8,15},{9,10},{10,... | collective-permute-start | bytes 294920 | tf_op jit(solution)/shard_map/ppermute | solution.py:476
  24.8 6.5 %collective-permute-start.6 = (bf16[4,24,512]{2,1,0:T(8,128)(2,1)S(1)}, bf16[4,24,512]{2,1,0:T(8,128)(2,1)S(1)}, u32[]{:S(2)}, u32[]{:S(2)}) collective-permute-start(bf16[4,24,512]{2,1,0:T(8,128)(2,1)S(1)} %get-tuple-element.25), channel_id=1, source_target_pairs={{0,1},{1,0},{2,3},{3,2},{4,5},{5,4},{6,7},{7,6},{8,9},{9,8},{10,11... | collective-permute-start | bytes 294920 | tf_op jit(solution)/shard_map/ppermute | solution.py:476
  53.0 7.4 %collective-permute-start.9 = (bf16[4,104,128]{2,1,0:T(8,128)(2,1)S(1)}, bf16[4,104,128]{2,1,0:T(8,128)(2,1)S(1)}, u32[]{:S(2)}, u32[]{:S(2)}) collective-permute-start(bf16[4,104,128]{2,1,0:T(8,128)(2,1)S(1)} %shard_map.177.s0), channel_id=1, source_target_pairs={{0,128},{64,192},{128,0},{192,64},{1,129},{65,193},{129,1},{193,65... | collective-permute-start | bytes 319496 | tf_op jit(solution)/shard_map/ppermute | solution.py:459
  55.3 6.2 %collective-permute-start.7 = (bf16[4,104,128]{2,1,0:T(8,128)(2,1)S(1)}, bf16[4,104,128]{2,1,0:T(8,128)(2,1)S(1)}, u32[]{:S(2)}, u32[]{:S(2)}) collective-permute-start(bf16[4,104,128]{2,1,0:T(8,128)(2,1)S(1)} %shard_map.177.s0), channel_id=1, source_target_pairs={{0,64},{64,0},{128,192},{192,128},{1,65},{65,1},{129,193},{193,129... | collective-permute-start | bytes 319496 | tf_op jit(solution)/shard_map/ppermute | solution.py:459
  56.5 5.9 %collective-permute-start.8 = (bf16[4,104,128]{2,1,0:T(8,128)(2,1)S(1)}, bf16[4,104,128]{2,1,0:T(8,128)(2,1)S(1)}, u32[]{:S(2)}, u32[]{:S(2)}) collective-permute-start(bf16[4,104,128]{2,1,0:T(8,128)(2,1)S(1)} %shard_map.177.s0), channel_id=1, source_target_pairs={{0,192},{64,128},{128,64},{192,0},{1,193},{65,129},{129,65},{193,1... | collective-permute-start | bytes 319496 | tf_op jit(solution)/shard_map/ppermute | solution.py:459
  63.9 5.4 %collective-permute-start.10 = (bf16[72,128]{1,0:T(8,128)(2,1)S(1)}, bf16[72,128]{1,0:T(8,128)(2,1)S(1)}, u32[]{:S(2)}, u32[]{:S(2)}) collective-permute-start(bf16[72,128]{1,0:T(8,128)(2,1)S(1)} %get-tuple-element.32), channel_id=1, source_target_pairs={{0,128},{64,192},{128,0},{192,64},{1,129},{65,193},{129,1},{193,65... | collective-permute-start | bytes 55304 | tf_op jit(solution)/shard_map/ppermute | solution.py:459
  71.4 5.9 %collective-permute-start.13 = (bf16[72,512]{1,0:T(8,128)(2,1)S(1)}, bf16[72,512]{1,0:T(8,128)(2,1)S(1)}, u32[]{:S(2)}, u32[]{:S(2)}) collective-permute-start(bf16[72,512]{1,0:T(8,128)(2,1)S(1)} %shard_map.180.refs_0_.residual_ref), channel_id=1, source_target_pairs={{0,32},{16,48},{32,0},{48,16},{1,33},{17,49},{33,1},{49,17},{2,34}... | collective-permute-start | bytes 221192 | tf_op jit(solution)/shard_map/ppermute | solution.py:459
  73.4 5.6 %collective-permute-start.15 = (bf16[72,512]{1,0:T(8,128)(2,1)S(1)}, bf16[72,512]{1,0:T(8,128)(2,1)S(1)}, u32[]{:S(2)}, u32[]{:S(2)}) collective-permute-start(bf16[72,512]{1,0:T(8,128)(2,1)S(1)} %shard_map.180.refs_0_.residual_ref), channel_id=1, source_target_pairs={{0,48},{16,32},{32,16},{48,0},{1,49},{17,33},{33,17},{49,1},{2,50}... | collective-permute-start | bytes 221192 | tf_op jit(solution)/shard_map/ppermute | solution.py:459
  79.0 8.0 %collective-permute-start.16 = (bf16[72,512]{1,0:T(8,128)(2,1)S(1)}, bf16[72,512]{1,0:T(8,128)(2,1)S(1)}, u32[]{:S(2)}, u32[]{:S(2)}) collective-permute-start(bf16[72,512]{1,0:T(8,128)(2,1)S(1)} %shard_map.181.refs_0_), channel_id=1, source_target_pairs={{0,2},{1,3},{2,4},{3,5},{4,6},{5,7},{6,0},{7,1},{8,10},{9,11},{10,... | collective-permute-start | bytes 221192 | tf_op jit(solution)/shard_map/ppermute | solution.py:469
  79.7 8.2 %collective-permute-start.17 = (bf16[72,512]{1,0:T(8,128)(2,1)S(1)}, bf16[72,512]{1,0:T(8,128)(2,1)S(1)}, u32[]{:S(2)}, u32[]{:S(2)}) collective-permute-start(bf16[72,512]{1,0:T(8,128)(2,1)S(1)} %shard_map.181.refs_0_), channel_id=1, source_target_pairs={{0,6},{1,7},{2,0},{3,1},{4,2},{5,3},{6,4},{7,5},{8,14},{9,15},{10,... | collective-permute-start | bytes 221192 | tf_op jit(solution)/shard_map/ppermute | solution.py:469
  83.2 7.1 %collective-permute-start.18 = (bf16[72,512]{1,0:T(8,128)(2,1)S(1)}, bf16[72,512]{1,0:T(8,128)(2,1)S(1)}, u32[]{:S(2)}, u32[]{:S(2)}) collective-permute-start(bf16[72,512]{1,0:T(8,128)(2,1)S(1)} %shard_map.181.refs_0_), channel_id=1, source_target_pairs={{0,1},{1,2},{2,3},{3,4},{4,5},{5,6},{6,7},{7,0},{8,9},{9,10},{10,1... | collective-permute-start | bytes 221192 | tf_op jit(solution)/shard_map/ppermute | solution.py:469
  83.8 6.5 %collective-permute-start.19 = (bf16[72,512]{1,0:T(8,128)(2,1)S(1)}, bf16[72,512]{1,0:T(8,128)(2,1)S(1)}, u32[]{:S(2)}, u32[]{:S(2)}) collective-permute-start(bf16[72,512]{1,0:T(8,128)(2,1)S(1)} %shard_map.181.refs_0_), channel_id=1, source_target_pairs={{0,7},{1,0},{2,1},{3,2},{4,3},{5,4},{6,5},{7,6},{8,15},{9,8},{10,9... | collective-permute-start | bytes 221192 | tf_op jit(solution)/shard_map/ppermute | solution.py:469
  87.1 6.6 %collective-permute-start.20 = (bf16[72,512]{1,0:T(8,128)(2,1)S(1)}, bf16[72,512]{1,0:T(8,128)(2,1)S(1)}, u32[]{:S(2)}, u32[]{:S(2)}) collective-permute-start(bf16[72,512]{1,0:T(8,128)(2,1)S(1)} %collective-permute-done.16.refs_1_), channel_id=1, source_target_pairs={{0,2},{1,3},{2,4},{3,5},{4,6},{5,7},{6,0},{7,1},{8,10},{9,11},{10,... | collective-permute-start | bytes 221192 | tf_op jit(solution)/shard_map/ppermute | solution.py:470
  87.1 6.8 %collective-permute-start.21 = (bf16[72,512]{1,0:T(8,128)(2,1)S(1)}, bf16[72,512]{1,0:T(8,128)(2,1)S(1)}, u32[]{:S(2)}, u32[]{:S(2)}) collective-permute-start(bf16[72,512]{1,0:T(8,128)(2,1)S(1)} %collective-permute-done.16.refs_1_), channel_id=1, source_target_pairs={{0,1},{1,2},{2,3},{3,4},{4,5},{5,6},{6,7},{7,0},{8,9},{9,10},{10,1... | collective-permute-start | bytes 221192 | tf_op jit(solution)/shard_map/ppermute | solution.py:470
  88.0 5.9 %collective-permute-start.22 = (bf16[72,512]{1,0:T(8,128)(2,1)S(1)}, bf16[72,512]{1,0:T(8,128)(2,1)S(1)}, u32[]{:S(2)}, u32[]{:S(2)}) collective-permute-start(bf16[72,512]{1,0:T(8,128)(2,1)S(1)} %collective-permute-done.17.refs_2_), channel_id=1, source_target_pairs={{0,7},{1,0},{2,1},{3,2},{4,3},{5,4},{6,5},{7,6},{8,15},{9,8},{10,9... | collective-permute-start | bytes 221192 | tf_op jit(solution)/shard_map/ppermute | solution.py:470
  97.6 6.9 %collective-permute-start.24 = (bf16[64,640]{1,0:T(8,128)(2,1)S(1)}, bf16[64,640]{1,0:T(8,128)(2,1)S(1)}, u32[]{:S(2)}, u32[]{:S(2)}) collective-permute-start(bf16[64,640]{1,0:T(8,128)(2,1)S(1)} %get-tuple-element.36), channel_id=1, source_target_pairs={{0,32},{16,48},{32,0},{48,16},{1,33},{17,49},{33,1},{49,17},{2,34}... | collective-permute-start | bytes 245768 | tf_op jit(solution)/shard_map/ppermute | solution.py:459
  99.4 5.5 %collective-permute-start.25 = (bf16[64,640]{1,0:T(8,128)(2,1)S(1)}, bf16[64,640]{1,0:T(8,128)(2,1)S(1)}, u32[]{:S(2)}, u32[]{:S(2)}) collective-permute-start(bf16[64,640]{1,0:T(8,128)(2,1)S(1)} %get-tuple-element.37), channel_id=1, source_target_pairs={{0,16},{16,0},{32,48},{48,32},{1,17},{17,1},{33,49},{49,33},{2,18}... | collective-permute-start | bytes 245768 | tf_op jit(solution)/shard_map/ppermute | solution.py:459
  100.7 5.7 %collective-permute-start.26 = (bf16[64,640]{1,0:T(8,128)(2,1)S(1)}, bf16[64,640]{1,0:T(8,128)(2,1)S(1)}, u32[]{:S(2)}, u32[]{:S(2)}) collective-permute-start(bf16[64,640]{1,0:T(8,128)(2,1)S(1)} %get-tuple-element.38), channel_id=1, source_target_pairs={{0,48},{16,32},{32,16},{48,0},{1,49},{17,33},{33,17},{49,1},{2,50}... | collective-permute-start | bytes 245768 | tf_op jit(solution)/shard_map/ppermute | solution.py:459
  (22 other events, 220.6 us)

commit v9 on v8

--- a/solution.py
+++ b/solution.py
@@ -14,7 +14,7 @@
 F32 = jnp.float32
 LANES = 128
 LIMIT = 32 * 1024 * 1024
-SHIFTS = (0, 2, 1, 3)
+SHIFTS = (0, 2, 3, 1)
 PAIRS = ((0, 1), (2, 3), (4, 5), (6, 7), (8,))
 VMEM = pl.BlockSpec(memory_space=pltpu.VMEM)
 

time: 109 us -> 107 us (0.982)
    ppermute x15, starting transfers between devices: 20.8 us -> 17.8 us  [spread_out(): lax.ppermute(block, axis, [(i, i ^ shift) for i in range(4)])]
where the time goes in v9:
time: 107 us; the launch traced here: 106 us
  starting transfers between devices  46.1 us (43%)
  waiting for transfers between devices  29.7 us (28%)
  blocking collectives  16.5 us (15%)
  Pallas kernels  10.4 us (10%)
  local copies, waits for them, and re-layouts  2.75 us (3%)
    ppermute x15, starting transfers between devices, spread_out(): lax.ppermute(block, axis, [(i, i ^ shift) for i in range(4)])  17.8 us
    ppermute x15, waiting for transfers between devices, spread_out(): lax.ppermute(block, axis, [(i, i ^ shift) for i in range(4)])  17.7 us
    all_to_all x1, blocking collectives, over_tiles(): lax.all_to_all(rows, HA + ('z',), split_axis=0, concat_axis=0, tiled=True)  16.5 us
    all_to_all x1, starting transfers between devices, over_tiles(): lax.all_to_all(rows, HA + ('z',), split_axis=0, concat_axis=0, tiled=True)  11.8 us
    pallas_call x13, Pallas kernels, call(): pl.pallas_call(kernel, out_shape=out_shape, in_specs=specs, out_specs=tup...  10.4 us
    ppermute x4, starting transfers between devices, relayed(): lax.ppermute(block, axis, ring(count, step))  7.45 us
    all_to_all x1, waiting for transfers between devices, over_tiles(): lax.all_to_all(rows, HA + ('z',), split_axis=0, concat_axis=0, tiled=True)  6.21 us
    ppermute x3, starting transfers between devices, relayed(): lax.ppermute(after[step], axis, ring(count, move))  3.92 us
  transfers between devices with their start and end apart: 28, of which 16 were waited for; matrix products, arithmetic and copies ran while one was open for 0% of the time, Pallas kernels for 1%

profile of v9, /device:TPU:6, one launch (start us, length us, event | category | flops | bytes accessed | tf_op | source)
XLA Modules:
  0.0 105.9 jit_solution(7052005725493258171)
XLA Ops:
  0.0 1.4 %collective-permute-start = (bf16[64,512]{1,0:T(8,128)(2,1)}, bf16[64,512]{1,0:T(8,128)(2,1)S(1)}, u32[]{:S(2)}, u32[]{:S(2)}) collective-permute-start(bf16[64,512]{1,0:T(8,128)(2,1)} %bitcast.9), channel_id=1, source_target_pairs={{0,128},{64,192},{128,0},{192,64},{1,129},{65,193},{129,1},{193,65... | collective-permute-start | bytes 196616 | tf_op jit(solution)/shard_map/ppermute | solution.py:459
  1.4 2.1 %collective-permute-start.1 = (bf16[64,512]{1,0:T(8,128)(2,1)}, bf16[64,512]{1,0:T(8,128)(2,1)S(1)}, u32[]{:S(2)}, u32[]{:S(2)}) collective-permute-start(bf16[64,512]{1,0:T(8,128)(2,1)} %bitcast.10), channel_id=1, source_target_pairs={{0,192},{64,128},{128,64},{192,0},{1,193},{65,129},{129,65},{193,1... | collective-permute-start | bytes 196616 | tf_op jit(solution)/shard_map/ppermute | solution.py:459
  10.7 11.8 %all-to-all-start = ((f32[64,1,128]{2,1,0:T(1,128)}), f32[64,1,128]{2,1,0:T(1,128)S(1)}, u32[]{:S(2)}, u32[]{:S(2)}) async-start(f32[64,1,128]{2,1,0:T(1,128)} %get-tuple-element.26), calls=%async_computation | async-start | bytes 65536 | tf_op jit(solution)/shard_map/all_to_all | solution.py:480
  22.7 2.9 %collective-permute-start.5 = (bf16[4,24,512]{2,1,0:T(8,128)(2,1)S(1)}, bf16[4,24,512]{2,1,0:T(8,128)(2,1)S(1)}, u32[]{:S(2)}, u32[]{:S(2)}) collective-permute-start(bf16[4,24,512]{2,1,0:T(8,128)(2,1)S(1)} %get-tuple-element.24), channel_id=1, source_target_pairs={{0,7},{1,2},{2,1},{3,4},{4,3},{5,6},{6,5},{7,0},{8,15},{9,10},{10,... | collective-permute-start | bytes 294920 | tf_op jit(solution)/shard_map/ppermute | solution.py:476
  25.8 6.2 %all-to-all-done.rows_ref = f32[64,1,128]{2,1,0:T(1,128)S(1)} async-done(((f32[64,1,128]{2,1,0:T(1,128)}), f32[64,1,128]{2,1,0:T(1,128)S(1)}, u32[]{:S(2)}, u32[]{:S(2)}) %all-to-all-start) | async-done | bytes 32800 | tf_op jit(solution)/shard_map/all_to_all | solution.py:480
  34.0 2.9 %shard_map.176 = (bf16[4,104,128]{2,1,0:T(8,128)(2,1)S(1)}, f32[64,1,128]{2,1,0:T(1,128)S(1)}) custom-call(bf16[576,1536]{1,0:T(8,128)(2,1)S(1)} %get-tuple-element.27.lhs, f32[38,128]{1,0:T(8,128)S(1)} %bitcast.4, bf16[27,512,128]{2,1,0:T(8,128)(2,1)S(1)} %copy-done.3), custom_call_target="tpu_custom_call" | custom-call | flops 2000000000 | bytes 5467136 | tf_op jit(solution)/shard_map/pallas_call | solution.py:442
  36.9 16.5 %all_to_all.10.rows_ref = f32[64,1,128]{2,1,0:T(1,128)S(1)} all-to-all(f32[64,1,128]{2,1,0:T(1,128)S(1)} %get-tuple-element.29), channel_id=1, replica_groups=mesh['ta'=4,'y'=4,'core'=2,'z'=8] {'y','core','z'}, dimensions={0} | all-to-all | bytes 65536 | tf_op jit(solution)/shard_map/all_to_all | solution.py:480
  54.4 2.1 %collective-permute-start.7 = (bf16[4,104,128]{2,1,0:T(8,128)(2,1)S(1)}, bf16[4,104,128]{2,1,0:T(8,128)(2,1)S(1)}, u32[]{:S(2)}, u32[]{:S(2)}) collective-permute-start(bf16[4,104,128]{2,1,0:T(8,128)(2,1)S(1)} %shard_map.177.s0), channel_id=1, source_target_pairs={{0,192},{64,128},{128,64},{192,0},{1,193},{65,129},{129,65},{193,1... | collective-permute-start | bytes 319496 | tf_op jit(solution)/shard_map/ppermute | solution.py:459
  57.3 3.8 %collective-permute-done.9.s1 = bf16[4,104,128]{2,1,0:T(8,128)(2,1)S(1)} collective-permute-done((bf16[4,104,128]{2,1,0:T(8,128)(2,1)S(1)}, bf16[4,104,128]{2,1,0:T(8,128)(2,1)S(1)}, u32[]{:S(2)}, u32[]{:S(2)}) %collective-permute-start.9) | collective-permute-done | bytes 106528 | tf_op jit(solution)/shard_map/ppermute | solution.py:459
  62.2 1.5 %shard_map.179 = (bf16[72,128]{1,0:T(8,128)(2,1)S(1)}, bf16[72,128]{1,0:T(8,128)(2,1)S(1)}, bf16[72,128]{1,0:T(8,128)(2,1)S(1)}, bf16[72,128]{1,0:T(8,128)(2,1)S(1)}) custom-call(bf16[4,104,128]{2,1,0:T(8,128)(2,1)S(1)} %collective-permute-done.7.s2, bf16[4,104,128]{2,1,0:T(8,128)(2,1)S(1)} %collective-permute-done.8.s3, ...), custom_call_target="tpu_custom_call" | custom-call | flops 2000000000 | bytes 5975040 | tf_op jit(solution)/shard_map/pallas_call | solution.py:442
  64.5 1.9 %collective-permute-start.11 = (bf16[72,128]{1,0:T(8,128)(2,1)S(1)}, bf16[72,128]{1,0:T(8,128)(2,1)S(1)}, u32[]{:S(2)}, u32[]{:S(2)}) collective-permute-start(bf16[72,128]{1,0:T(8,128)(2,1)S(1)} %get-tuple-element.33), channel_id=1, source_target_pairs={{0,192},{64,128},{128,64},{192,0},{1,193},{65,129},{129,65},{193,1... | collective-permute-start | bytes 55304 | tf_op jit(solution)/shard_map/ppermute | solution.py:459
  67.3 1.8 %collective-permute-done.10.s1 = bf16[72,128]{1,0:T(8,128)(2,1)S(1)} collective-permute-done((bf16[72,128]{1,0:T(8,128)(2,1)S(1)}, bf16[72,128]{1,0:T(8,128)(2,1)S(1)}, u32[]{:S(2)}, u32[]{:S(2)}) %collective-permute-start.10) | collective-permute-done | bytes 18464 | tf_op jit(solution)/shard_map/ppermute | solution.py:459
  70.2 1.5 %collective-permute-start.13 = (bf16[72,512]{1,0:T(8,128)(2,1)S(1)}, bf16[72,512]{1,0:T(8,128)(2,1)S(1)}, u32[]{:S(2)}, u32[]{:S(2)}) collective-permute-start(bf16[72,512]{1,0:T(8,128)(2,1)S(1)} %shard_map.180.refs_0_.residual_ref), channel_id=1, source_target_pairs={{0,32},{16,48},{32,0},{48,16},{1,33},{17,49},{33,1},{49,17},{2,34}... | collective-permute-start | bytes 221192 | tf_op jit(solution)/shard_map/ppermute | solution.py:459
  71.7 1.9 %collective-permute-start.14 = (bf16[72,512]{1,0:T(8,128)(2,1)S(1)}, bf16[72,512]{1,0:T(8,128)(2,1)S(1)}, u32[]{:S(2)}, u32[]{:S(2)}) collective-permute-start(bf16[72,512]{1,0:T(8,128)(2,1)S(1)} %shard_map.180.refs_0_.residual_ref), channel_id=1, source_target_pairs={{0,48},{16,32},{32,16},{48,0},{1,49},{17,33},{33,17},{49,1},{2,50}... | collective-permute-start | bytes 221192 | tf_op jit(solution)/shard_map/ppermute | solution.py:459
  73.8 2.4 %collective-permute-done.13.refs_1_ = bf16[72,512]{1,0:T(8,128)(2,1)S(1)} collective-permute-done((bf16[72,512]{1,0:T(8,128)(2,1)S(1)}, bf16[72,512]{1,0:T(8,128)(2,1)S(1)}, u32[]{:S(2)}, u32[]{:S(2)}) %collective-permute-start.13) | collective-permute-done | bytes 73760 | tf_op jit(solution)/shard_map/ppermute | solution.py:459
  78.8 3.5 %collective-permute-start.17 = (bf16[72,512]{1,0:T(8,128)(2,1)S(1)}, bf16[72,512]{1,0:T(8,128)(2,1)S(1)}, u32[]{:S(2)}, u32[]{:S(2)}) collective-permute-start(bf16[72,512]{1,0:T(8,128)(2,1)S(1)} %shard_map.181.refs_0_), channel_id=1, source_target_pairs={{0,6},{1,7},{2,0},{3,1},{4,2},{5,3},{6,4},{7,5},{8,14},{9,15},{10,... | collective-permute-start | bytes 221192 | tf_op jit(solution)/shard_map/ppermute | solution.py:469
  82.9 2.6 %collective-permute-start.19 = (bf16[72,512]{1,0:T(8,128)(2,1)S(1)}, bf16[72,512]{1,0:T(8,128)(2,1)S(1)}, u32[]{:S(2)}, u32[]{:S(2)}) collective-permute-start(bf16[72,512]{1,0:T(8,128)(2,1)S(1)} %shard_map.181.refs_0_), channel_id=1, source_target_pairs={{0,7},{1,0},{2,1},{3,2},{4,3},{5,4},{6,5},{7,6},{8,15},{9,8},{10,9... | collective-permute-start | bytes 221192 | tf_op jit(solution)/shard_map/ppermute | solution.py:469
  86.8 2.7 %collective-permute-start.22 = (bf16[72,512]{1,0:T(8,128)(2,1)S(1)}, bf16[72,512]{1,0:T(8,128)(2,1)S(1)}, u32[]{:S(2)}, u32[]{:S(2)}) collective-permute-start(bf16[72,512]{1,0:T(8,128)(2,1)S(1)} %collective-permute-done.17.refs_2_), channel_id=1, source_target_pairs={{0,7},{1,0},{2,1},{3,2},{4,3},{5,4},{6,5},{7,6},{8,15},{9,8},{10,9... | collective-permute-start | bytes 221192 | tf_op jit(solution)/shard_map/ppermute | solution.py:470
  89.5 2.6 %collective-permute-done.20.refs_5_ = bf16[72,512]{1,0:T(8,128)(2,1)S(1)} collective-permute-done((bf16[72,512]{1,0:T(8,128)(2,1)S(1)}, bf16[72,512]{1,0:T(8,128)(2,1)S(1)}, u32[]{:S(2)}, u32[]{:S(2)}) %collective-permute-start.20) | collective-permute-done | bytes 73760 | tf_op jit(solution)/shard_map/ppermute | solution.py:470
  93.8 1.9 %collective-permute-done.23.refs_5_ = bf16[520,512]{1,0:T(8,128)(2,1)S(1)} collective-permute-done((bf16[520,512]{1,0:T(8,128)(2,1)S(1)}, bf16[520,512]{1,0:T(8,128)(2,1)S(1)}, u32[]{:S(2)}, u32[]{:S(2)}) %collective-permute-start.23) | collective-permute-done | bytes 532512 | tf_op jit(solution)/shard_map/ppermute | solution.py:620
  95.7 1.4 %shard_map.183 = (bf16[64,640]{1,0:T(8,128)(2,1)S(1)}, bf16[64,640]{1,0:T(8,128)(2,1)S(1)}, bf16[64,640]{1,0:T(8,128)(2,1)S(1)}, bf16[64,640]{1,0:T(8,128)(2,1)S(1)}) custom-call(bf16[72,512]{1,0:T(8,128)(2,1)S(1)} %shard_map.180.refs_0_.residual_ref, bf16[72,512]{1,0:T(8,128)(2,1)S(1)} %collective-permute-done.13.refs_1_, ...), custom_call_target="tpu_custom_call" | custom-call | flops 1000000000 | bytes 2755584 | tf_op jit(solution)/shard_map/pallas_call | solution.py:442
  97.2 1.5 %collective-permute-start.25 = (bf16[64,640]{1,0:T(8,128)(2,1)S(1)}, bf16[64,640]{1,0:T(8,128)(2,1)S(1)}, u32[]{:S(2)}, u32[]{:S(2)}) collective-permute-start(bf16[64,640]{1,0:T(8,128)(2,1)S(1)} %get-tuple-element.37), channel_id=1, source_target_pairs={{0,48},{16,32},{32,16},{48,0},{1,49},{17,33},{33,17},{49,1},{2,50}... | collective-permute-start | bytes 245768 | tf_op jit(solution)/shard_map/ppermute | solution.py:459
  98.7 2.0 %collective-permute-start.26 = (bf16[64,640]{1,0:T(8,128)(2,1)S(1)}, bf16[64,640]{1,0:T(8,128)(2,1)S(1)}, u32[]{:S(2)}, u32[]{:S(2)}) collective-permute-start(bf16[64,640]{1,0:T(8,128)(2,1)S(1)} %get-tuple-element.38), channel_id=1, source_target_pairs={{0,16},{16,0},{32,48},{48,32},{1,17},{17,1},{33,49},{49,33},{2,18}... | collective-permute-start | bytes 245768 | tf_op jit(solution)/shard_map/ppermute | solution.py:459
  100.7 3.3 %collective-permute-done.24.b1 = bf16[64,640]{1,0:T(8,128)(2,1)S(1)} collective-permute-done((bf16[64,640]{1,0:T(8,128)(2,1)S(1)}, bf16[64,640]{1,0:T(8,128)(2,1)S(1)}, u32[]{:S(2)}, u32[]{:S(2)}) %collective-permute-start.24) | collective-permute-done | bytes 81952 | tf_op jit(solution)/shard_map/ppermute | solution.py:459
  (94 shorter events, 23.2 us)
Async XLA Ops:
  0.0 6.1 %collective-permute-start = (bf16[64,512]{1,0:T(8,128)(2,1)}, bf16[64,512]{1,0:T(8,128)(2,1)S(1)}, u32[]{:S(2)}, u32[]{:S(2)}) collective-permute-start(bf16[64,512]{1,0:T(8,128)(2,1)} %bitcast.9), channel_id=1, source_target_pairs={{0,128},{64,192},{128,0},{192,64},{1,129},{65,193},{129,1},{193,65... | collective-permute-start | bytes 196616 | tf_op jit(solution)/shard_map/ppermute | solution.py:459
  1.4 5.7 %collective-permute-start.1 = (bf16[64,512]{1,0:T(8,128)(2,1)}, bf16[64,512]{1,0:T(8,128)(2,1)S(1)}, u32[]{:S(2)}, u32[]{:S(2)}) collective-permute-start(bf16[64,512]{1,0:T(8,128)(2,1)} %bitcast.10), channel_id=1, source_target_pairs={{0,192},{64,128},{128,64},{192,0},{1,193},{65,129},{129,65},{193,1... | collective-permute-start | bytes 196616 | tf_op jit(solution)/shard_map/ppermute | solution.py:459
  9.0 13.5 %collective-permute-start.3 = (bf16[4,16,512]{2,1,0:T(8,128)(2,1)S(1)}, bf16[4,16,512]{2,1,0:T(8,128)(2,1)S(1)}, u32[]{:S(2)}, u32[]{:S(2)}) collective-permute-start(bf16[4,16,512]{2,1,0:T(8,128)(2,1)S(1)} %get-tuple-element.22), channel_id=1, source_target_pairs={{0,56},{8,16},{16,8},{24,32},{32,24},{40,48},{48,40},{56,0},{1,57}... | collective-permute-start | bytes 196616 | tf_op jit(solution)/shard_map/ppermute | solution.py:476
  9.8 12.7 %collective-permute-start.4 = (bf16[4,16,512]{2,1,0:T(8,128)(2,1)S(1)}, bf16[4,16,512]{2,1,0:T(8,128)(2,1)S(1)}, u32[]{:S(2)}, u32[]{:S(2)}) collective-permute-start(bf16[4,16,512]{2,1,0:T(8,128)(2,1)S(1)} %get-tuple-element.23), channel_id=1, source_target_pairs={{0,8},{8,0},{16,24},{24,16},{32,40},{40,32},{48,56},{56,48},{1,9},... | collective-permute-start | bytes 196616 | tf_op jit(solution)/shard_map/ppermute | solution.py:476
  10.7 21.4 %all-to-all-start = ((f32[64,1,128]{2,1,0:T(1,128)}), f32[64,1,128]{2,1,0:T(1,128)S(1)}, u32[]{:S(2)}, u32[]{:S(2)}) async-start(f32[64,1,128]{2,1,0:T(1,128)} %get-tuple-element.26), calls=%async_computation | async-start | bytes 65536 | tf_op jit(solution)/shard_map/all_to_all | solution.py:480
  22.7 9.3 %collective-permute-start.5 = (bf16[4,24,512]{2,1,0:T(8,128)(2,1)S(1)}, bf16[4,24,512]{2,1,0:T(8,128)(2,1)S(1)}, u32[]{:S(2)}, u32[]{:S(2)}) collective-permute-start(bf16[4,24,512]{2,1,0:T(8,128)(2,1)S(1)} %get-tuple-element.24), channel_id=1, source_target_pairs={{0,7},{1,2},{2,1},{3,4},{4,3},{5,6},{6,5},{7,0},{8,15},{9,10},{10,... | collective-permute-start | bytes 294920 | tf_op jit(solution)/shard_map/ppermute | solution.py:476
  25.6 6.5 %collective-permute-start.6 = (bf16[4,24,512]{2,1,0:T(8,128)(2,1)S(1)}, bf16[4,24,512]{2,1,0:T(8,128)(2,1)S(1)}, u32[]{:S(2)}, u32[]{:S(2)}) collective-permute-start(bf16[4,24,512]{2,1,0:T(8,128)(2,1)S(1)} %get-tuple-element.25), channel_id=1, source_target_pairs={{0,1},{1,0},{2,3},{3,2},{4,5},{5,4},{6,7},{7,6},{8,9},{9,8},{10,11... | collective-permute-start | bytes 294920 | tf_op jit(solution)/shard_map/ppermute | solution.py:476
  53.7 7.4 %collective-permute-start.9 = (bf16[4,104,128]{2,1,0:T(8,128)(2,1)S(1)}, bf16[4,104,128]{2,1,0:T(8,128)(2,1)S(1)}, u32[]{:S(2)}, u32[]{:S(2)}) collective-permute-start(bf16[4,104,128]{2,1,0:T(8,128)(2,1)S(1)} %shard_map.177.s0), channel_id=1, source_target_pairs={{0,128},{64,192},{128,0},{192,64},{1,129},{65,193},{129,1},{193,65... | collective-permute-start | bytes 319496 | tf_op jit(solution)/shard_map/ppermute | solution.py:459
  54.4 7.8 %collective-permute-start.7 = (bf16[4,104,128]{2,1,0:T(8,128)(2,1)S(1)}, bf16[4,104,128]{2,1,0:T(8,128)(2,1)S(1)}, u32[]{:S(2)}, u32[]{:S(2)}) collective-permute-start(bf16[4,104,128]{2,1,0:T(8,128)(2,1)S(1)} %shard_map.177.s0), channel_id=1, source_target_pairs={{0,192},{64,128},{128,64},{192,0},{1,193},{65,129},{129,65},{193,1... | collective-permute-start | bytes 319496 | tf_op jit(solution)/shard_map/ppermute | solution.py:459
  56.5 5.7 %collective-permute-start.8 = (bf16[4,104,128]{2,1,0:T(8,128)(2,1)S(1)}, bf16[4,104,128]{2,1,0:T(8,128)(2,1)S(1)}, u32[]{:S(2)}, u32[]{:S(2)}) collective-permute-start(bf16[4,104,128]{2,1,0:T(8,128)(2,1)S(1)} %shard_map.177.s0), channel_id=1, source_target_pairs={{0,64},{64,0},{128,192},{192,128},{1,65},{65,1},{129,193},{193,129... | collective-permute-start | bytes 319496 | tf_op jit(solution)/shard_map/ppermute | solution.py:459
  63.7 5.4 %collective-permute-start.10 = (bf16[72,128]{1,0:T(8,128)(2,1)S(1)}, bf16[72,128]{1,0:T(8,128)(2,1)S(1)}, u32[]{:S(2)}, u32[]{:S(2)}) collective-permute-start(bf16[72,128]{1,0:T(8,128)(2,1)S(1)} %get-tuple-element.32), channel_id=1, source_target_pairs={{0,128},{64,192},{128,0},{192,64},{1,129},{65,193},{129,1},{193,65... | collective-permute-start | bytes 55304 | tf_op jit(solution)/shard_map/ppermute | solution.py:459
  64.5 5.0 %collective-permute-start.11 = (bf16[72,128]{1,0:T(8,128)(2,1)S(1)}, bf16[72,128]{1,0:T(8,128)(2,1)S(1)}, u32[]{:S(2)}, u32[]{:S(2)}) collective-permute-start(bf16[72,128]{1,0:T(8,128)(2,1)S(1)} %get-tuple-element.33), channel_id=1, source_target_pairs={{0,192},{64,128},{128,64},{192,0},{1,193},{65,129},{129,65},{193,1... | collective-permute-start | bytes 55304 | tf_op jit(solution)/shard_map/ppermute | solution.py:459
  70.2 6.0 %collective-permute-start.13 = (bf16[72,512]{1,0:T(8,128)(2,1)S(1)}, bf16[72,512]{1,0:T(8,128)(2,1)S(1)}, u32[]{:S(2)}, u32[]{:S(2)}) collective-permute-start(bf16[72,512]{1,0:T(8,128)(2,1)S(1)} %shard_map.180.refs_0_.residual_ref), channel_id=1, source_target_pairs={{0,32},{16,48},{32,0},{48,16},{1,33},{17,49},{33,1},{49,17},{2,34}... | collective-permute-start | bytes 221192 | tf_op jit(solution)/shard_map/ppermute | solution.py:459
  71.7 5.6 %collective-permute-start.14 = (bf16[72,512]{1,0:T(8,128)(2,1)S(1)}, bf16[72,512]{1,0:T(8,128)(2,1)S(1)}, u32[]{:S(2)}, u32[]{:S(2)}) collective-permute-start(bf16[72,512]{1,0:T(8,128)(2,1)S(1)} %shard_map.180.refs_0_.residual_ref), channel_id=1, source_target_pairs={{0,48},{16,32},{32,16},{48,0},{1,49},{17,33},{33,17},{49,1},{2,50}... | collective-permute-start | bytes 221192 | tf_op jit(solution)/shard_map/ppermute | solution.py:459
  78.1 7.5 %collective-permute-start.16 = (bf16[72,512]{1,0:T(8,128)(2,1)S(1)}, bf16[72,512]{1,0:T(8,128)(2,1)S(1)}, u32[]{:S(2)}, u32[]{:S(2)}) collective-permute-start(bf16[72,512]{1,0:T(8,128)(2,1)S(1)} %shard_map.181.refs_0_), channel_id=1, source_target_pairs={{0,2},{1,3},{2,4},{3,5},{4,6},{5,7},{6,0},{7,1},{8,10},{9,11},{10,... | collective-permute-start | bytes 221192 | tf_op jit(solution)/shard_map/ppermute | solution.py:469
  78.8 8.0 %collective-permute-start.17 = (bf16[72,512]{1,0:T(8,128)(2,1)S(1)}, bf16[72,512]{1,0:T(8,128)(2,1)S(1)}, u32[]{:S(2)}, u32[]{:S(2)}) collective-permute-start(bf16[72,512]{1,0:T(8,128)(2,1)S(1)} %shard_map.181.refs_0_), channel_id=1, source_target_pairs={{0,6},{1,7},{2,0},{3,1},{4,2},{5,3},{6,4},{7,5},{8,14},{9,15},{10,... | collective-permute-start | bytes 221192 | tf_op jit(solution)/shard_map/ppermute | solution.py:469
  82.3 7.2 %collective-permute-start.18 = (bf16[72,512]{1,0:T(8,128)(2,1)S(1)}, bf16[72,512]{1,0:T(8,128)(2,1)S(1)}, u32[]{:S(2)}, u32[]{:S(2)}) collective-permute-start(bf16[72,512]{1,0:T(8,128)(2,1)S(1)} %shard_map.181.refs_0_), channel_id=1, source_target_pairs={{0,1},{1,2},{2,3},{3,4},{4,5},{5,6},{6,7},{7,0},{8,9},{9,10},{10,1... | collective-permute-start | bytes 221192 | tf_op jit(solution)/shard_map/ppermute | solution.py:469
  82.9 6.6 %collective-permute-start.19 = (bf16[72,512]{1,0:T(8,128)(2,1)S(1)}, bf16[72,512]{1,0:T(8,128)(2,1)S(1)}, u32[]{:S(2)}, u32[]{:S(2)}) collective-permute-start(bf16[72,512]{1,0:T(8,128)(2,1)S(1)} %shard_map.181.refs_0_), channel_id=1, source_target_pairs={{0,7},{1,0},{2,1},{3,2},{4,3},{5,4},{6,5},{7,6},{8,15},{9,8},{10,9... | collective-permute-start | bytes 221192 | tf_op jit(solution)/shard_map/ppermute | solution.py:469
  85.5 6.6 %collective-permute-start.20 = (bf16[72,512]{1,0:T(8,128)(2,1)S(1)}, bf16[72,512]{1,0:T(8,128)(2,1)S(1)}, u32[]{:S(2)}, u32[]{:S(2)}) collective-permute-start(bf16[72,512]{1,0:T(8,128)(2,1)S(1)} %collective-permute-done.16.refs_1_), channel_id=1, source_target_pairs={{0,2},{1,3},{2,4},{3,5},{4,6},{5,7},{6,0},{7,1},{8,10},{9,11},{10,... | collective-permute-start | bytes 221192 | tf_op jit(solution)/shard_map/ppermute | solution.py:470
  85.5 7.8 %collective-permute-start.21 = (bf16[72,512]{1,0:T(8,128)(2,1)S(1)}, bf16[72,512]{1,0:T(8,128)(2,1)S(1)}, u32[]{:S(2)}, u32[]{:S(2)}) collective-permute-start(bf16[72,512]{1,0:T(8,128)(2,1)S(1)} %collective-permute-done.16.refs_1_), channel_id=1, source_target_pairs={{0,1},{1,2},{2,3},{3,4},{4,5},{5,6},{6,7},{7,0},{8,9},{9,10},{10,1... | collective-permute-start | bytes 221192 | tf_op jit(solution)/shard_map/ppermute | solution.py:470
  86.8 6.6 %collective-permute-start.22 = (bf16[72,512]{1,0:T(8,128)(2,1)S(1)}, bf16[72,512]{1,0:T(8,128)(2,1)S(1)}, u32[]{:S(2)}, u32[]{:S(2)}) collective-permute-start(bf16[72,512]{1,0:T(8,128)(2,1)S(1)} %collective-permute-done.17.refs_2_), channel_id=1, source_target_pairs={{0,7},{1,0},{2,1},{3,2},{4,3},{5,4},{6,5},{7,6},{8,15},{9,8},{10,9... | collective-permute-start | bytes 221192 | tf_op jit(solution)/shard_map/ppermute | solution.py:470
  97.1 6.9 %collective-permute-start.24 = (bf16[64,640]{1,0:T(8,128)(2,1)S(1)}, bf16[64,640]{1,0:T(8,128)(2,1)S(1)}, u32[]{:S(2)}, u32[]{:S(2)}) collective-permute-start(bf16[64,640]{1,0:T(8,128)(2,1)S(1)} %get-tuple-element.36), channel_id=1, source_target_pairs={{0,32},{16,48},{32,0},{48,16},{1,33},{17,49},{33,1},{49,17},{2,34}... | collective-permute-start | bytes 245768 | tf_op jit(solution)/shard_map/ppermute | solution.py:459
  97.2 7.5 %collective-permute-start.25 = (bf16[64,640]{1,0:T(8,128)(2,1)S(1)}, bf16[64,640]{1,0:T(8,128)(2,1)S(1)}, u32[]{:S(2)}, u32[]{:S(2)}) collective-permute-start(bf16[64,640]{1,0:T(8,128)(2,1)S(1)} %get-tuple-element.37), channel_id=1, source_target_pairs={{0,48},{16,32},{32,16},{48,0},{1,49},{17,33},{33,17},{49,1},{2,50}... | collective-permute-start | bytes 245768 | tf_op jit(solution)/shard_map/ppermute | solution.py:459
  98.7 6.1 %collective-permute-start.26 = (bf16[64,640]{1,0:T(8,128)(2,1)S(1)}, bf16[64,640]{1,0:T(8,128)(2,1)S(1)}, u32[]{:S(2)}, u32[]{:S(2)}) collective-permute-start(bf16[64,640]{1,0:T(8,128)(2,1)S(1)} %get-tuple-element.38), channel_id=1, source_target_pairs={{0,16},{16,0},{32,48},{48,32},{1,17},{17,1},{33,49},{49,33},{2,18}... | collective-permute-start | bytes 245768 | tf_op jit(solution)/shard_map/ppermute | solution.py:459
  (22 other events, 217.6 us)
